TPU v7x, 32 devices: a whole 2x2x4 slice. The times are simulated.
32 devices in a mesh: feat: 4 (over z), tok: 8 (over y, x, core).
Axes of the slice: x: 2, y: 2, z: 4, core: 2. Of those that a mesh axis runs over, the one named last changes fastest.
Arguments:
- master: float32 [422144], P(('feat', 'tok')), may hold values from -2 to 2
- first_moment: float32 [422144], P(('feat', 'tok')), may hold values from -1 to 1
- second_moment: float32 [422144], P(('feat', 'tok')), may hold values from 0 to 1
- observations: bfloat16 [61440, 512], P('tok', 'feat'), may hold values from -6 to 6
- camera_counts: int32 [2048, 10], P('tok'), may hold values from 1 to 3, as said below
- code_targets: int32 [61440, 2], P('tok'), may hold values from 0 to 15
- action_targets: float32 [35, 61440], P(None, 'tok'), may hold values from -6 to 6
- action_valid: int32 [35, 61440], P(None, 'tok'), may hold values from 0 to 1
Outputs:
- master_new: float32 [422144], P(('feat', 'tok'))
- first_new: float32 [422144], P(('feat', 'tok'))
- second_new: float32 [422144], P(('feat', 'tok'))
- loss_parts: float32 [4], replicated
Inputs may be any that keep to these rules, and one draw needn't show every extreme that they name: `camera_counts`: every timestep has at least one live camera token.
All inputs are finite; a program needn't handle non-finite values.
Results may differ from a plain program's by a relative error of at most 0.002.
The roundings to bfloat16 on the way count: a program that leaves them out, or rounds other values in their place, can miss the bound.
Values may be sent and summed in bfloat16 or wider, within the bound.
A program may use at most 192 MiB of HBM per device.

v0:
```python
import math

import jax
import jax.numpy as jnp
from jax import lax
from jax.sharding import PartitionSpec as P

D = 120
H = 6
HD = 20
FF = 480
OBS = 512
LAYERS = 2
CAMS = 3
BOOKS = 2
CODES = 16
SPAN = 5
ACT = 7
STEP_NO = 10
WIN = 30


NORM_EPS = 1e-05
BETA_ONE = 0.9
BETA_TWO = 0.999
ADAM_EPS = 1e-08
DECAY_RATE = 0.1
LEARN_RATE = 0.05


def layout_table():
    table_rows = [("obs_w", (OBS, D)), ("obs_b", (D,)), ("pos_table", (WIN, D))]
    for depth_index in range(LAYERS):
        table_rows += [
            ("gain_one", (D,)),
            ("bias_one", (D,)),
            ("qkv_w", (D, 3 * D)),
            ("qv_b", (2 * D,)),
            ("out_w", (D, D)),
            ("out_b", (D,)),
            ("gain_two", (D,)),
            ("bias_two", (D,)),
            ("fc_w", (D, FF)),
            ("fc_b", (FF,)),
            ("proj_w", (FF, D)),
            ("proj_b", (D,)),
        ]
    table_rows += [
        ("gain_final", (D,)),
        ("bias_final", (D,)),
        ("code_w", (D, BOOKS * CODES)),
        ("code_b", (BOOKS * CODES,)),
        ("off_w", (D, SPAN * ACT)),
        ("off_b", (SPAN * ACT,)),
    ]
    return table_rows


def unpack_flat(flat):
    pieces = []
    offset = 0
    for entry in layout_table():
        length_now = math.prod(entry[1])
        pieces.append(flat[offset : offset + length_now].reshape(entry[1]))
        offset += length_now
    return pieces


def slot_masks(counts):
    slot_ids = jnp.arange(WIN, dtype=jnp.int32)
    step_of = slot_ids // CAMS
    live_slots = (slot_ids % CAMS)[None, :] < jnp.repeat(counts, CAMS, axis=1)
    allowed = (step_of[:, None] >= step_of[None, :])[None, :, :] & live_slots[:, None, :]
    return (live_slots, allowed)


def layer_norm(values, gain, shift):
    center = values - jnp.mean(values, axis=-1, keepdims=True)
    spread = jnp.mean(center * center, axis=-1, keepdims=True)
    return center * lax.rsqrt(spread + NORM_EPS) * gain + shift


def attend_windows(mixed, allowed):
    windows = mixed.shape[0]
    queries = mixed[:, :, :D].reshape(windows, WIN, H, HD)
    keys_all = mixed[:, :, D : 2 * D].reshape(windows, WIN, H, HD)
    values_all = mixed[:, :, 2 * D :].reshape(windows, WIN, H, HD)
    scores = jnp.einsum(
        "wqhe,wkhe->whqk", queries, keys_all, precision=lax.Precision.HIGHEST
    ) * HD ** (-0.5)
    scores = jnp.where(allowed[:, None, :, :], scores, -1e30)
    highest = jnp.max(scores, axis=-1, keepdims=True)
    probs = jnp.exp(scores - highest)
    probs = probs / jnp.sum(probs, axis=-1, keepdims=True)
    output = jnp.einsum("whqk,wkhe->wqhe", probs, values_all, precision=lax.Precision.HIGHEST)
    return output.reshape(windows, WIN, D)


def head_sums(logits, offsets, live_rows, codes, actions, valid_rows):
    grouped = logits.reshape(-1, BOOKS, CODES)
    highest = jnp.max(grouped, axis=-1, keepdims=True)
    total_exp = jnp.log(jnp.sum(jnp.exp(grouped - highest), axis=-1)) + highest[..., 0]
    picked = jnp.sum(
        jnp.where(codes[..., None] == jnp.arange(CODES, dtype=jnp.int32), grouped, 0.0), axis=-1
    )
    code_sum = jnp.sum((total_exp - picked) * live_rows[:, None])
    action_sum = jnp.sum(valid_rows * jnp.sqrt((offsets - actions) ** 2 + 1.0))
    return (code_sum, action_sum)


def outer_sum(left, right):
    return lax.dot_general(
        left, right, (((0,), (0,)), ((), ())), preferred_element_type=jnp.float32
    )


def back_input(grad_low, weight):
    return lax.dot_general(
        grad_low, weight, (((1,), (1,)), ((), ())), preferred_element_type=jnp.float32
    )


def activate(values):
    return jax.nn.gelu(values, approximate=True)


def layer_forward(hidden, weights, allowed):
    (
        gain_one,
        bias_one,
        qkv_w,
        qv_b,
        out_w,
        out_b,
        gain_two,
        bias_two,
        fc_w,
        fc_b,
        proj_w,
        proj_b,
    ) = weights
    windows = allowed.shape[0]
    rows = hidden.shape[0]
    normed, norm_one_back = jax.vjp(layer_norm, hidden, gain_one, bias_one)
    normed_low = normed.astype(jnp.bfloat16)
    qkv_bias = jnp.concatenate([qv_b[:D], jnp.zeros((D,), jnp.float32), qv_b[D:]])
    mixed = jnp.dot(normed_low, qkv_w, preferred_element_type=jnp.float32) + qkv_bias

    def attend_rows(values):
        return attend_windows(values.reshape(windows, WIN, 3 * D), allowed).reshape(rows, D)

    attended, attend_back = jax.vjp(attend_rows, mixed)
    attended_low = attended.astype(jnp.bfloat16)
    hidden_mid = hidden + jnp.dot(attended_low, out_w, preferred_element_type=jnp.float32) + out_b
    normed_two, norm_two_back = jax.vjp(layer_norm, hidden_mid, gain_two, bias_two)
    normed_two_low = normed_two.astype(jnp.bfloat16)
    inner, gelu_back = jax.vjp(
        activate, jnp.dot(normed_two_low, fc_w, preferred_element_type=jnp.float32) + fc_b
    )
    inner_low = inner.astype(jnp.bfloat16)
    hidden_out = (
        hidden_mid + jnp.dot(inner_low, proj_w, preferred_element_type=jnp.float32) + proj_b
    )
    record = (
        normed_low,
        attended_low,
        normed_two_low,
        inner_low,
        norm_one_back,
        attend_back,
        norm_two_back,
        gelu_back,
    )
    return (hidden_out, record)


def layer_backward(grad_out, weights, record):
    (
        gain_one,
        bias_one,
        qkv_w,
        qv_b,
        out_w,
        out_b,
        gain_two,
        bias_two,
        fc_w,
        fc_b,
        proj_w,
        proj_b,
    ) = weights
    (
        normed_low,
        attended_low,
        normed_two_low,
        inner_low,
        norm_one_back,
        attend_back,
        norm_two_back,
        gelu_back,
    ) = record
    out_low = grad_out.astype(jnp.bfloat16)
    d_proj_w = outer_sum(inner_low, out_low)
    d_proj_b = jnp.sum(grad_out, axis=0)
    d_pre = gelu_back(back_input(out_low, proj_w))[0]
    d_fc_b = jnp.sum(d_pre, axis=0)
    pre_low = d_pre.astype(jnp.bfloat16)
    d_fc_w = outer_sum(normed_two_low, pre_low)
    d_mid, d_gain_two, d_bias_two = norm_two_back(back_input(pre_low, fc_w))
    d_mid = d_mid + grad_out
    mid_low = d_mid.astype(jnp.bfloat16)
    d_out_w = outer_sum(attended_low, mid_low)
    d_out_b = jnp.sum(d_mid, axis=0)
    d_mixed = attend_back(back_input(mid_low, out_w))[0]
    d_qv_b = jnp.concatenate(
        [jnp.sum(d_mixed[:, :D], axis=0), jnp.sum(d_mixed[:, 2 * D :], axis=0)]
    )
    mixed_low = d_mixed.astype(jnp.bfloat16)
    d_qkv_w = outer_sum(normed_low, mixed_low)
    d_input, d_gain_one, d_bias_one = norm_one_back(back_input(mixed_low, qkv_w))
    grads = [
        d_gain_one,
        d_bias_one,
        d_qkv_w,
        d_qv_b,
        d_out_w,
        d_out_b,
        d_gain_two,
        d_bias_two,
        d_fc_w,
        d_fc_b,
        d_proj_w,
        d_proj_b,
    ]
    return (d_input + d_mid, grads)


def shards(
    master,
    first_moment,
    second_moment,
    observations,
    camera_counts,
    code_targets,
    action_targets,
    action_valid,
):
    gathered = lax.all_gather(master.astype(jnp.bfloat16), ("feat", "tok"), axis=0, tiled=True)
    pieces = unpack_flat(gathered)
    params = [
        piece if piece.ndim == 2 and position != 2 else piece.astype(jnp.float32)
        for position, piece in enumerate(pieces)
    ]
    feat_index = lax.axis_index("feat")
    feat_count = lax.axis_size("feat")
    own_windows = camera_counts.shape[0] // feat_count
    own_rows = own_windows * WIN
    counts_own = lax.dynamic_slice_in_dim(camera_counts, feat_index * own_windows, own_windows, 0)
    codes_own = lax.dynamic_slice_in_dim(code_targets, feat_index * own_rows, own_rows, 0)
    actions_own = jnp.transpose(
        lax.dynamic_slice_in_dim(action_targets, feat_index * own_rows, own_rows, 1)
    )
    valid_own = jnp.transpose(
        lax.dynamic_slice_in_dim(action_valid, feat_index * own_rows, own_rows, 1)
    )
    live_slots, allowed = slot_masks(counts_own)
    live_ints = live_slots.reshape(-1).astype(jnp.int32)
    valid_ints = valid_own * live_ints[:, None]
    totals = lax.psum((jnp.sum(live_ints), jnp.sum(valid_ints)), ("feat", "tok"))
    live_total = totals[0].astype(jnp.float32)
    valid_total = totals[1].astype(jnp.float32)
    obs_w = params[0]
    column_count = observations.shape[1]
    weight_rows = lax.dynamic_slice_in_dim(obs_w, feat_index * column_count, column_count, 0)
    hidden = lax.psum_scatter(
        jnp.dot(observations, weight_rows, preferred_element_type=jnp.float32),
        "feat",
        scatter_dimension=0,
        tiled=True,
    )
    hidden = hidden + params[1] + jnp.tile(params[2], (own_windows, 1))
    records = []
    for depth_index in range(LAYERS):
        first_slot = 3 + 12 * depth_index
        hidden, record = layer_forward(hidden, params[first_slot : first_slot + 12], allowed)
        records.append(record)
    head_start = 3 + 12 * LAYERS
    code_w = params[head_start + 2]
    off_w = params[head_start + 4]
    final, final_back = jax.vjp(layer_norm, hidden, params[head_start], params[head_start + 1])
    final_low = final.astype(jnp.bfloat16)
    logits = jnp.dot(final_low, code_w, preferred_element_type=jnp.float32) + params[head_start + 3]
    offsets = jnp.dot(final_low, off_w, preferred_element_type=jnp.float32) + params[head_start + 5]
    live_rows = live_ints.astype(jnp.float32)
    valid_rows = valid_ints.astype(jnp.float32)

    def local_loss(logit_values, offset_values):
        code_sum, action_sum = head_sums(
            logit_values, offset_values, live_rows, codes_own, actions_own, valid_rows
        )
        return (code_sum / live_total + action_sum / valid_total, (code_sum, action_sum))

    loss_value, loss_back, local_sums = jax.vjp(local_loss, logits, offsets, has_aux=True)
    d_logits, d_offsets = loss_back(jnp.ones((), jnp.float32))
    logit_low = d_logits.astype(jnp.bfloat16)
    offset_low = d_offsets.astype(jnp.bfloat16)
    tail_grads = [
        outer_sum(final_low, logit_low),
        jnp.sum(d_logits, axis=0),
        outer_sum(final_low, offset_low),
        jnp.sum(d_offsets, axis=0),
    ]
    d_final = back_input(logit_low, code_w) + back_input(offset_low, off_w)
    grad_hidden, d_gain_final, d_bias_final = final_back(d_final)
    layer_grads = []
    for depth_index in reversed(range(LAYERS)):
        first_slot = 3 + 12 * depth_index
        grad_hidden, grads_now = layer_backward(
            grad_hidden, params[first_slot : first_slot + 12], records[depth_index]
        )
        layer_grads = grads_now + layer_grads
    hidden_low = grad_hidden.astype(jnp.bfloat16)
    group_grad = lax.all_gather(hidden_low, "feat", axis=0, tiled=True)
    rows_part = outer_sum(observations, group_grad)
    d_obs_w = lax.dynamic_update_slice(
        jnp.zeros((OBS, D), jnp.float32),
        rows_part,
        (feat_index * column_count, jnp.zeros((), jnp.int32)),
    )
    head_grads = [
        d_obs_w,
        jnp.sum(grad_hidden, axis=0),
        jnp.sum(grad_hidden.reshape(own_windows, WIN, D), axis=0),
    ]
    all_grads = head_grads + layer_grads + [d_gain_final, d_bias_final] + tail_grads
    used_length = sum((math.prod(entry[1]) for entry in layout_table()))
    flat_grad = jnp.concatenate(
        [piece.reshape(-1).astype(jnp.float32) for piece in all_grads]
        + [jnp.zeros((gathered.shape[0] - used_length,), jnp.float32)]
    )
    reduced = lax.psum_scatter(flat_grad, ("feat", "tok"), scatter_dimension=0, tiled=True)
    first_new = BETA_ONE * first_moment + (1.0 - BETA_ONE) * reduced
    second_new = BETA_TWO * second_moment + (1.0 - BETA_TWO) * reduced * reduced
    first_hat = first_new / (1.0 - BETA_ONE**STEP_NO)
    second_hat = second_new / (1.0 - BETA_TWO**STEP_NO)
    master_new = master - LEARN_RATE * (
        first_hat / (jnp.sqrt(second_hat) + ADAM_EPS) + DECAY_RATE * master
    )
    losses = lax.psum((local_sums[0], local_sums[1]), ("feat", "tok"))
    loss_parts = jnp.stack([losses[0], live_total, losses[1], valid_total])
    return (master_new, first_new, second_new, loss_parts)


def solution(mesh):
    in_specs = (
        P(("feat", "tok")),
        P(("feat", "tok")),
        P(("feat", "tok")),
        P("tok", "feat"),
        P("tok", None),
        P("tok", None),
        P(None, "tok"),
        P(None, "tok"),
    )
    out_specs = (P(("feat", "tok")), P(("feat", "tok")), P(("feat", "tok")), P())
    return jax.shard_map(shards, mesh=mesh, in_specs=in_specs, out_specs=out_specs, check_vma=False)
```

profile of v0, /device:TPU:0, one launch (start us, length us, event | category | flops | bytes accessed | tf_op | source)
XLA Modules:
  0.0 924.9 jit_solution(6591480454594963005)
XLA Ops:
  9.8 134.5 %all-reduce.13.cloned.1.call-done = bf16[422144]{0:T(1024)(128)(2,1)} async-done(((bf16[422144]{0:T(1024)(128)(2,1)}), bf16[422144]{0:T(1024)(128)(2,1)}) %all-reduce.13.cloned.1.call-update) | async-done | bytes 844304
  152.5 44.5 %all-reduce.8 = (s32[]{:T(128)}, s32[]{:T(128)}) all-reduce(s32[]{:T(128)} %convert_reduce_fusion.3, s32[]{:T(128)} %fusion.74), channel_id=1, replica_groups=mesh['feat'=4,'tok'=8] {'feat','tok'}, use_global_device_ids=true, to_apply=%region_1.2 | all-reduce | flops 2 | bytes 16 | tf_op jit(solution)/shard_map/psum | solution.py:269
  239.7 4.9 fusion.140
  256.5 5.1 copy.99
  261.6 5.1 copy.97
  266.7 5.1 copy.98
  271.8 14.4 %fusion.1 = (f32[64,6,30]{2,1,0:T(8,128)S(1)}, f32[64,6,30,30]{2,3,1,0:T(8,128)S(1)}) fusion(pred[64,30,30]{1,2,0:T(8,128)(4,1)S(1)} %broadcast_and_fusion, f32[64,30,6,20]{1,3,2,0:T(8,128)} %copy.97, f32[64,30,6,20]{1,3,2,0:T(8,128)} %copy.98), kind=kOutput, calls=%fused_computation.20 | convolution fusion | flops 83969280 | bytes 3329280 | tf_op jit(solution)/shard_map/jvp(wqhe,wkhe->whqk)/dot_general | solution.py:88
  289.8 11.4 %convert_bitcast_fusion.1 = bf16[64,30,6,20]{1,3,2,0:T(8,128)(2,1)S(1)} fusion(f32[64,30,6,20]{1,3,2,0:T(8,128)} %copy.99, f32[64,6,30]{2,1,0:T(8,128)S(1)} %fusion.114, f32[64,6,30,30]{2,3,1,0:T(8,128)S(1)} %get-tuple-element.113, f32[64,6,30]{2,1,0:T(8,128)S(1)} %get-tuple-element.112, pred[64,30,30]{1,2,0:T(8,128)(4,1)S(1)} %broadcast_and_fusion), kind=kOutput, calls=%fused_computation.75 | convolution fusion | flops 84556800 | bytes 2914560 | tf_op jit(solution)/shard_map/jvp(whqk,wkhe->wqhe)/dot_general | solution.py:95
  303.1 4.2 convert_element_type.218
  308.9 4.3 multiply_convert_fusion.1
  320.3 4.3 reshape.504
  324.6 4.9 fusion.139
  341.4 5.1 copy.108
  346.6 5.1 copy.106
  351.6 5.1 copy.107
  356.7 14.4 %fusion.3 = (f32[64,6,30]{2,1,0:T(8,128)S(1)}, f32[64,6,30,30]{2,3,1,0:T(8,128)S(1)}) fusion(pred[64,30,30]{1,2,0:T(8,128)(4,1)S(1)} %broadcast_and_fusion, f32[64,30,6,20]{1,3,2,0:T(8,128)} %copy.106, f32[64,30,6,20]{1,3,2,0:T(8,128)} %copy.107), kind=kOutput, calls=%fused_computation.22 | convolution fusion | flops 83969280 | bytes 3329280 | tf_op jit(solution)/shard_map/jvp(wqhe,wkhe->whqk)/dot_general | solution.py:88
  374.7 11.0 %convert_bitcast_fusion = bf16[64,30,6,20]{1,3,2,0:T(8,128)(2,1)S(1)} fusion(f32[64,30,6,20]{1,3,2,0:T(8,128)} %copy.108, f32[64,6,30]{2,1,0:T(8,128)S(1)} %fusion.115, f32[64,6,30,30]{2,3,1,0:T(8,128)S(1)} %get-tuple-element.121, f32[64,6,30]{2,1,0:T(8,128)S(1)} %get-tuple-element.120, pred[64,30,30]{1,2,0:T(8,128)(4,1)S(1)} %broadcast_and_fusion), kind=kOutput, calls=%fused_computation.74 | convolution fusion | flops 84556800 | bytes 2914560 | tf_op jit(solution)/shard_map/jvp(whqk,wkhe->wqhe)/dot_general | solution.py:95
  387.7 4.6 convert_element_type.232
  421.0 5.4 copy.113
  426.4 15.9 %fusion.49 = f32[64,30,6,20]{1,3,2,0:T(8,128)} fusion(f32[64,6,20,30]{3,2,1,0:T(8,128)} %copy.113, f32[64,6,30]{2,1,0:T(8,128)} %copy-done.32, f32[64,6,30,30]{2,3,1,0:T(8,128)} %copy-done.5, f32[64,6,30]{2,1,0:T(8,128)} %copy-done.28, pred[64,30,30]{1,2,0:T(8,128)(4,1)S(1)} %broadcast_and_fusion), kind=kOutput, calls=%fused_computation.82 | convolution fusion | flops 84326400 | bytes 3375360 | tf_op jit(solution)/shard_map/transpose(jvp(whqk,wkhe->wqhe))/dot_general | solution.py:95
  442.3 18.3 %convert_reduce_fusion.1 = (f32[64,6,30]{2,1,0:T(8,128)}, pred[64,6,30,30]{2,3,1,0:T(8,128)(4,1)S(1)}, f32[64,6,30]{2,1,0:T(8,128)S(1)}, f32[64,6,30,30]{2,3,1,0:T(8,128)S(1)}) fusion(f32[64,6,30]{2,1,0:T(8,128)S(1)} %copy-done.29, f32[64,6,30,30]{2,3,1,0:T(8,128)} %copy-done.5, pred[64,30,30]{1,2,0:T(8,128)(4,1)S(1)} %broadcast_and_fusion, ...), kind=kOutput, calls=%fused_computation.6 | convolution fusion | flops 86031360 | bytes 5195520 | tf_op jit(solution)/shard_map/transpose(jvp(whqk,wkhe->wqhe))/dot_general | solution.py:95
  460.7 5.6 fusion.134
  466.4 11.4 %fusion.48 = f32[64,30,6,20]{1,3,2,0:T(8,128)} fusion(f32[64,30,6,20]{1,3,2,0:T(8,128)S(1)} %bitcast.176, f32[64,6,30,30]{2,3,1,0:T(8,128)S(1)} %get-tuple-element.56, pred[64,6,30,30]{2,3,1,0:T(8,128)(4,1)S(1)} %get-tuple-element.58, f32[64,6,30]{2,1,0:T(8,128)S(1)} %negate_divide_fusion.1, pred[64,30,30]{1,2,0:T(8,128)(4,1)S(1)} %broadcast_and_fusion), kind=kOutput, calls=%fused_computation.81 | convolution fusion | flops 84326400 | bytes 3674880 | tf_op jit(solution)/shard_map/transpose(jvp(wqhe,wkhe->whqk))/dot_general | solution.py:88
  477.8 12.9 %fusion.47 = f32[64,30,6,20]{1,3,2,0:T(8,128)} fusion(f32[64,30,6,20]{1,3,2,0:T(8,128)S(1)} %bitcast.174, f32[64,6,30,30]{2,3,1,0:T(8,128)S(1)} %get-tuple-element.56, pred[64,6,30,30]{2,3,1,0:T(8,128)(4,1)S(1)} %get-tuple-element.58, f32[64,6,30]{2,1,0:T(8,128)S(1)} %negate_divide_fusion.1, pred[64,30,30]{1,2,0:T(8,128)(4,1)S(1)} %broadcast_and_fusion), kind=kOutput, calls=%fused_computation.80 | convolution fusion | flops 84326400 | bytes 3674880 | tf_op jit(solution)/shard_map/transpose(jvp(wqhe,wkhe->whqk))/dot_general | solution.py:88
  490.6 5.2 copy.115
  495.9 5.2 copy.120
  501.1 15.8 %copy.123 = f32[64,30,6,20]{0,1,3,2:T(8,128)} copy(f32[64,30,6,20]{1,3,2,0:T(8,128)} %fusion.48) | data formatting | bytes 1843200 | tf_op jit(solution)/shard_map/transpose(jvp(wqhe,wkhe->whqk))/transpose | solution.py:88
  516.9 5.7 pad_add_fusion.1
  522.5 6.9 copy.124
  539.4 4.1 fusion.150
  554.0 5.5 copy.127
  559.5 15.7 %fusion.50 = f32[64,30,6,20]{1,3,2,0:T(8,128)} fusion(f32[64,6,20,30]{3,2,1,0:T(8,128)} %copy.127, f32[64,6,30]{2,1,0:T(8,128)S(1)} %copy-done.31, f32[64,6,30,30]{2,3,1,0:T(8,128)} %copy-done.4, f32[64,6,30]{2,1,0:T(8,128)S(1)} %get-tuple-element.112, pred[64,30,30]{1,2,0:T(8,128)(4,1)S(1)} %broadcast_and_fusion), kind=kOutput, calls=%fused_computation.83 | convolution fusion | flops 84326400 | bytes 3375360 | tf_op jit(solution)/shard_map/transpose(jvp(whqk,wkhe->wqhe))/dot_general | solution.py:95
  575.2 17.5 %convert_reduce_fusion = (f32[64,6,30]{2,1,0:T(8,128)}, pred[64,6,30,30]{2,3,1,0:T(8,128)(4,1)S(1)}, f32[64,6,30]{2,1,0:T(8,128)S(1)}, f32[64,6,30,30]{2,3,1,0:T(8,128)S(1)}) fusion(f32[64,6,30]{2,1,0:T(8,128)S(1)} %get-tuple-element.112, f32[64,6,30,30]{2,3,1,0:T(8,128)} %copy-done.4, pred[64,30,30]{1,2,0:T(8,128)(4,1)S(1)} %broadcast_and_fusion, ...), kind=kOutput, calls=%fused_computation.2 | convolution fusion | flops 86031360 | bytes 5195520 | tf_op jit(solution)/shard_map/transpose(jvp(whqk,wkhe->wqhe))/dot_general | solution.py:95
  592.8 5.8 fusion.132
  598.7 11.3 %fusion.46 = f32[64,30,6,20]{1,3,2,0:T(8,128)} fusion(f32[64,30,6,20]{1,3,2,0:T(8,128)S(1)} %bitcast.172, f32[64,6,30,30]{2,3,1,0:T(8,128)S(1)} %get-tuple-element.52, pred[64,6,30,30]{2,3,1,0:T(8,128)(4,1)S(1)} %get-tuple-element.54, f32[64,6,30]{2,1,0:T(8,128)S(1)} %negate_divide_fusion, pred[64,30,30]{1,2,0:T(8,128)(4,1)S(1)} %broadcast_and_fusion), kind=kOutput, calls=%fused_computation.79 | convolution fusion | flops 84326400 | bytes 3674880 | tf_op jit(solution)/shard_map/transpose(jvp(wqhe,wkhe->whqk))/dot_general | solution.py:88
  610.0 12.8 %fusion.45 = f32[64,30,6,20]{1,3,2,0:T(8,128)} fusion(f32[64,30,6,20]{1,3,2,0:T(8,128)S(1)} %bitcast.170, f32[64,6,30,30]{2,3,1,0:T(8,128)S(1)} %get-tuple-element.52, pred[64,6,30,30]{2,3,1,0:T(8,128)(4,1)S(1)} %get-tuple-element.54, f32[64,6,30]{2,1,0:T(8,128)S(1)} %negate_divide_fusion, pred[64,30,30]{1,2,0:T(8,128)(4,1)S(1)} %broadcast_and_fusion), kind=kOutput, calls=%fused_computation.78 | convolution fusion | flops 84326400 | bytes 3674880 | tf_op jit(solution)/shard_map/transpose(jvp(wqhe,wkhe->whqk))/dot_general | solution.py:88
  622.9 5.2 copy.129
  628.1 5.2 copy.134
  633.3 5.4 copy.137
  638.7 5.7 pad_add_fusion
  644.4 6.9 copy.138
  680.9 7.4 copy.142
  688.2 4.2 reshape.528
  708.1 7.1 copy.141
  715.3 4.2 reshape.523
  733.0 50.5 %concatenate.11 = f32[422144]{0:T(1024)} concatenate(f32[61440]{0:T(1024)S(1)} %reshape.520, f32[120]{0:T(128)} %get-tuple-element.49, f32[3600]{0:T(1024)} %reshape.522, f32[120]{0:T(128)} %get-tuple-element.14, f32[120]{0:T(128)} %get-tuple-element.25, f32[43200]{0:T(1024)} %reshape.524, f32[120]{0:T(128)} %get-tuple-element.7, f32[120]{0:T(128)} %get-tuple-element.6, ...), dimensions={0} | concatenate | bytes 3377152 | tf_op jit(solution)/shard_map/concatenate | solution.py:337
  784.2 40.1 %all-reduce.9 = (f32[1]{0:T(128)}, f32[1]{0:T(128)}) all-reduce(f32[1]{0:T(128)} %bitcast.35, f32[1]{0:T(128)} %bitcast.33), channel_id=1, replica_groups=mesh['feat'=4,'tok'=8] {'feat','tok'}, use_global_device_ids=true, to_apply=%region_68.69 | all-reduce | flops 2 | bytes 16 | tf_op jit(solution)/shard_map/psum | solution.py:349
  826.2 90.3 %all-reduce.15.cloned.1.call-done = f32[422144]{0:T(1024)} async-done(((f32[422144]{0:T(1024)}), f32[422144]{0:T(1024)}) %all-reduce.15.cloned.1.call-update) | async-done | bytes 1688592
  (442 shorter events, 206.3 us)
Async XLA Ops:
  7.2 138.3 %copy-start = (bf16[7680,128]{1,0:T(8,128)(2,1)S(1)}, bf16[7680,128]{1,0:T(8,128)(2,1)}, u32[]{:S(2)}) copy-start(bf16[7680,128]{1,0:T(8,128)(2,1)} %param.11) | copy-start | bytes 5898244
  7.2 137.1 %all-reduce.13.cloned.1.call-start = ((), (), s32[]{:S(2)}) async-start(), calls=%async_computation.3 | async-start | bytes 1691648
  9.7 218.4 %reduce-scatter.2.cloned.1.call-start = ((), (), s32[]{:S(2)}) async-start(), calls=%async_computation.1 | async-start | bytes 4608000 | tf_op jit(solution)/shard_map/reduce_scatter | solution.py:275
  148.7 581.5 %all-gather.2.cloned.1.call-start = ((), (), s32[]{:S(2)}) async-start(), calls=%async_computation.2 | async-start | bytes 2304000 | tf_op jit(solution)/shard_map/all_gather | solution.py:323
  150.1 51.2 %copy-start.81 = (s32[1920]{0:T(1024)}, s32[1920]{0:T(1024)S(1)}, u32[]{:S(2)}) copy-start(s32[1920]{0:T(1024)S(1)} %get-tuple-element.35) | copy-start | bytes 23044
  210.1 104.5 %copy-start.38 = (bf16[120,360]{1,0:T(8,128)(2,1)}, bf16[120,360]{1,0:T(8,128)(2,1)S(1)}, u32[]{:S(2)}) copy-start(bf16[120,360]{1,0:T(8,128)(2,1)S(1)} %reshape.503) | copy-start | bytes 259204
  212.7 17.2 %copy-start.37 = (bf16[120,360]{1,0:T(8,128)(2,1)}, bf16[120,360]{1,0:T(8,128)(2,1)S(1)}, u32[]{:S(2)}) copy-start(bf16[120,360]{1,0:T(8,128)(2,1)S(1)} %reshape.494) | copy-start | bytes 259204
  228.0 80.8 %copy-start.92 = (f32[120]{0:T(128)}, f32[120]{0:T(128)S(1)}, u32[]{:S(2)}) copy-start(f32[120]{0:T(128)S(1)} %get-tuple-element.89) | copy-start | bytes 1444
  228.0 310.4 %copy-start.91 = (f32[120]{0:T(128)}, f32[120]{0:T(128)S(1)}, u32[]{:S(2)}) copy-start(f32[120]{0:T(128)S(1)} %get-tuple-element.86) | copy-start | bytes 1444
  229.7 77.6 %copy-start.1 = (f32[1920,120]{0,1:T(8,128)}, f32[1920,120]{0,1:T(8,128)S(1)}, u32[]{:S(2)}) copy-start(f32[1920,120]{0,1:T(8,128)S(1)} %get-tuple-element.64) | copy-start | bytes 2764804
  286.2 15.1 %copy-start.4 = (f32[64,6,30,30]{2,3,1,0:T(8,128)}, f32[64,6,30,30]{2,3,1,0:T(8,128)S(1)}, u32[]{:S(2)}) copy-start(f32[64,6,30,30]{2,3,1,0:T(8,128)S(1)} %get-tuple-element.113) | copy-start | bytes 4147204
  308.7 237.2 %copy-start.49 = (f32[1920]{0:T(1024)}, f32[1920]{0:T(1024)S(1)}, u32[]{:S(2)}) copy-start(f32[1920]{0:T(1024)S(1)} %broadcast_multiply_fusion.3) | copy-start | bytes 23044
  314.5 224.0 %copy-start.3 = (f32[1920,120]{0,1:T(8,128)}, f32[1920,120]{0,1:T(8,128)S(1)}, u32[]{:S(2)}) copy-start(f32[1920,120]{0,1:T(8,128)S(1)} %get-tuple-element.119) | copy-start | bytes 2764804
  371.1 14.6 %copy-start.5 = (f32[64,6,30,30]{2,3,1,0:T(8,128)}, f32[64,6,30,30]{2,3,1,0:T(8,128)S(1)}, u32[]{:S(2)}) copy-start(f32[64,6,30,30]{2,3,1,0:T(8,128)S(1)} %get-tuple-element.121) | copy-start | bytes 4147204
  371.2 14.6 %copy-start.28 = (f32[64,6,30]{2,1,0:T(8,128)}, f32[64,6,30]{2,1,0:T(8,128)S(1)}, u32[]{:S(2)}) copy-start(f32[64,6,30]{2,1,0:T(8,128)S(1)} %get-tuple-element.120) | copy-start | bytes 138244
  393.6 17.4 %copy-start.8 = (f32[1920,120]{0,1:T(8,128)}, f32[1920,120]{0,1:T(8,128)S(1)}, u32[]{:S(2)}) copy-start(f32[1920,120]{0,1:T(8,128)S(1)} %get-tuple-element.123) | copy-start | bytes 2764804
  393.7 17.4 %copy-start.50 = (f32[1920]{0:T(1024)}, f32[1920]{0:T(1024)S(1)}, u32[]{:S(2)}) copy-start(f32[1920]{0:T(1024)S(1)} %broadcast_multiply_fusion.1) | copy-start | bytes 23044
  393.8 17.2 %copy-start.71 = (f32[1920]{0:T(1024)}, f32[1920]{0:T(1024)S(1)}, u32[]{:S(2)}) copy-start(f32[1920]{0:T(1024)S(1)} %fusion.95) | copy-start | bytes 23044
  426.4 15.9 %copy-start.22 = (f32[64,6,20,30]{3,2,1,0:T(8,128)S(1)}, f32[64,6,20,30]{3,2,1,0:T(8,128)}, u32[]{:S(2)}) copy-start(f32[64,6,20,30]{3,2,1,0:T(8,128)} %copy.113) | copy-start | bytes 2764804
  426.4 15.9 %copy-start.29 = (f32[64,6,30]{2,1,0:T(8,128)S(1)}, f32[64,6,30]{2,1,0:T(8,128)}, u32[]{:S(2)}) copy-start(f32[64,6,30]{2,1,0:T(8,128)} %copy-done.28) | copy-start | bytes 138244
  426.4 15.9 %copy-start.56 = (f32[64,6,30]{2,1,0:T(8,128)S(1)}, f32[64,6,30]{2,1,0:T(8,128)}, u32[]{:S(2)}) copy-start(f32[64,6,30]{2,1,0:T(8,128)} %multiply_divide_fusion.1) | copy-start | bytes 138244
  426.4 40.0 %slice-start.6 = ((s8[4718592]{0:T(1024)(128)(4,1)}), s8[4194304]{0:T(1024)(128)(4,1)S(1)}, s32[]{:S(2)}) async-start(s8[4718592]{0:T(1024)(128)(4,1)} %bitcast.175), calls=%async_computation.11 | async-start | bytes 8388608
  442.3 24.1 %slice-start.7 = ((s8[4718592]{0:T(1024)(128)(4,1)}), s8[524288]{0:T(1024)(128)(4,1)S(1)}, s32[]{:S(2)}) async-start(s8[4718592]{0:T(1024)(128)(4,1)} %bitcast.175), calls=%async_computation.12 | async-start | bytes 1048576
  442.3 35.4 %slice-start.4 = ((s8[4718592]{0:T(1024)(128)(4,1)}), s8[4194304]{0:T(1024)(128)(4,1)S(1)}, s32[]{:S(2)}) async-start(s8[4718592]{0:T(1024)(128)(4,1)} %bitcast.173), calls=%async_computation.9 | async-start | bytes 8388608
  460.7 17.1 %slice-start.5 = ((s8[4718592]{0:T(1024)(128)(4,1)}), s8[524288]{0:T(1024)(128)(4,1)S(1)}, s32[]{:S(2)}) async-start(s8[4718592]{0:T(1024)(128)(4,1)} %bitcast.173), calls=%async_computation.10 | async-start | bytes 1048576
  554.0 21.2 %slice-start.8 = ((s8[4718592]{0:T(1024)(128)(4,1)}), s8[524288]{0:T(1024)(128)(4,1)S(1)}, s32[]{:S(2)}) async-start(s8[4718592]{0:T(1024)(128)(4,1)} %bitcast.189), calls=%async_computation.13 | async-start | bytes 1048576
  559.5 15.7 %slice-start.9 = ((s8[4718592]{0:T(1024)(128)(4,1)}), s8[4194304]{0:T(1024)(128)(4,1)S(1)}, s32[]{:S(2)}) async-start(s8[4718592]{0:T(1024)(128)(4,1)} %bitcast.189), calls=%async_computation.14 | async-start | bytes 8388608
  559.5 15.7 %copy-start.23 = (f32[64,6,20,30]{3,2,1,0:T(8,128)S(1)}, f32[64,6,20,30]{3,2,1,0:T(8,128)}, u32[]{:S(2)}) copy-start(f32[64,6,20,30]{3,2,1,0:T(8,128)} %copy.127) | copy-start | bytes 2764804
  559.5 15.7 %copy-start.55 = (f32[64,6,30]{2,1,0:T(8,128)S(1)}, f32[64,6,30]{2,1,0:T(8,128)}, u32[]{:S(2)}) copy-start(f32[64,6,30]{2,1,0:T(8,128)} %multiply_divide_fusion) | copy-start | bytes 138244
  559.5 39.2 %slice-start.2 = ((s8[4718592]{0:T(1024)(128)(4,1)}), s8[4194304]{0:T(1024)(128)(4,1)S(1)}, s32[]{:S(2)}) async-start(s8[4718592]{0:T(1024)(128)(4,1)} %bitcast.171), calls=%async_computation.7 | async-start | bytes 8388608
  575.2 23.4 %slice-start.3 = ((s8[4718592]{0:T(1024)(128)(4,1)}), s8[524288]{0:T(1024)(128)(4,1)S(1)}, s32[]{:S(2)}) async-start(s8[4718592]{0:T(1024)(128)(4,1)} %bitcast.171), calls=%async_computation.8 | async-start | bytes 1048576
  575.2 34.8 %slice-start = ((s8[4718592]{0:T(1024)(128)(4,1)}), s8[4194304]{0:T(1024)(128)(4,1)S(1)}, s32[]{:S(2)}) async-start(s8[4718592]{0:T(1024)(128)(4,1)} %bitcast.169), calls=%async_computation.5 | async-start | bytes 8388608
  592.8 17.2 %slice-start.1 = ((s8[4718592]{0:T(1024)(128)(4,1)}), s8[524288]{0:T(1024)(128)(4,1)S(1)}, s32[]{:S(2)}) async-start(s8[4718592]{0:T(1024)(128)(4,1)} %bitcast.169), calls=%async_computation.6 | async-start | bytes 1048576
  644.4 13.4 %copy-start.61 = (f32[1920]{0:T(1024)S(1)}, f32[1920]{0:T(1024)}, u32[]{:S(2)}) copy-start(f32[1920]{0:T(1024)} %copy-done.60) | copy-start | bytes 23044
  660.1 13.6 %copy-start.51 = (f32[1920]{0:T(1024)S(1)}, f32[1920]{0:T(1024)}, u32[]{:S(2)}) copy-start(f32[1920]{0:T(1024)} %copy-done.50) | copy-start | bytes 23044
  660.1 13.6 %copy-start.72 = (f32[1920]{0:T(1024)S(1)}, f32[1920]{0:T(1024)}, u32[]{:S(2)}) copy-start(f32[1920]{0:T(1024)} %copy-done.71) | copy-start | bytes 23044
  660.1 13.6 %copy-start.95 = (f32[120]{0:T(128)S(1)}, f32[120]{0:T(128)}, u32[]{:S(2)}) copy-start(f32[120]{0:T(128)} %get-tuple-element.83) | copy-start | bytes 1444
  660.1 13.6 %copy-start.109 = (f32[120]{0:T(128)S(1)}, f32[120]{0:T(128)}, u32[]{:S(2)}) copy-start(f32[120]{0:T(128)} %get-tuple-element.82) | copy-start | bytes 1444
  661.9 254.6 %all-reduce.15.cloned.1.call-start = ((), (), s32[]{:S(2)}) async-start(), calls=%async_computation.4 | async-start | bytes 3383296
  662.8 16.0 %copy-start.25 = (bf16[1920,120]{0,1:T(8,128)(2,1)S(1)}, bf16[1920,120]{0,1:T(8,128)(2,1)}, u32[]{:S(2)}) copy-start(bf16[1920,120]{0,1:T(8,128)(2,1)} %convert_element_type.232) | copy-start | bytes 1382404
  692.4 13.7 %copy-start.24 = (bf16[1920,120]{0,1:T(8,128)(2,1)S(1)}, bf16[1920,120]{0,1:T(8,128)(2,1)}, u32[]{:S(2)}) copy-start(bf16[1920,120]{0,1:T(8,128)(2,1)} %convert_element_type.218) | copy-start | bytes 1382404
  730.2 53.3 %copy-start.48 = (f32[1920,2]{0,1:T(2,128)S(1)}, f32[1920,2]{0,1:T(2,128)}, u32[]{:S(2)}) copy-start(f32[1920,2]{0,1:T(2,128)} %copy-done.47) | copy-start | bytes 46084
  730.2 53.3 %copy-start.88 = (f32[1920]{0:T(1024)S(1)}, f32[1920]{0:T(1024)}, u32[]{:S(2)}) copy-start(f32[1920]{0:T(1024)} %get-tuple-element.34) | copy-start | bytes 23044
  732.9 50.7 %copy-start.67 = (f32[1920,2]{0,1:T(2,128)S(1)}, f32[1920,2]{0,1:T(2,128)}, u32[]{:S(2)}) copy-start(f32[1920,2]{0,1:T(2,128)} %copy-done.66) | copy-start | bytes 46084
  732.9 50.7 %copy-start.84 = (f32[1920,2]{0,1:T(2,128)S(1)}, f32[1920,2]{0,1:T(2,128)}, u32[]{:S(2)}) copy-start(f32[1920,2]{0,1:T(2,128)} %get-tuple-element.29) | copy-start | bytes 46084
  732.9 183.6 %copy-start.59 = (f32[13192]{0:T(1024)S(1)}, f32[13192]{0:T(1024)}, u32[]{:S(2)}) copy-start(f32[13192]{0:T(1024)} %param.8) | copy-start | bytes 158308
  732.9 183.6 %copy-start.85 = (f32[13192]{0:T(1024)S(1)}, f32[13192]{0:T(1024)}, u32[]{:S(2)}) copy-start(f32[13192]{0:T(1024)} %param.9) | copy-start | bytes 158308
  732.9 183.6 %copy-start.86 = (f32[13192]{0:T(1024)S(1)}, f32[13192]{0:T(1024)}, u32[]{:S(2)}) copy-start(f32[13192]{0:T(1024)} %param.10) | copy-start | bytes 158308
  (80 other events, 427.3 us)
Sparse Core Ops, SparseCore 0:
  13.2 130.9 all-reduce.12
  148.8 70.0 reduce-scatter.1
  662.0 41.5 all-gather.1
  783.6 132.8 all-reduce.14
where the time goes:
time: 927 us; the launch traced here: 925 us
  local copies, waits for them, and re-layouts  293 us (32%)
  matrix products  236 us (25%)
  waiting for transfers between devices  225 us (24%)
  blocking collectives  84.7 us (9%)
  other arithmetic  68.6 us (7%)
  between operations  17.2 us (2%)
    unnamed x6, waiting for transfers between devices  225 us
    dot_general x6, matrix products, attend_windows(): jnp.einsum('whqk,wkhe->wqhe', probs, values_all, precision=lax.Precision....  89.9 us
    dot_general x6, matrix products, attend_windows(): jnp.einsum('wqhe,wkhe->whqk', queries, keys_all, precision=lax.Precision....  77.3 us
    concatenate x1, local copies, waits for them, and re-layouts, shards(): jnp.concatenate([piece.reshape(-1).astype(jnp.float32) for piece in all_g...  50.5 us
    psum x1, blocking collectives, shards(): lax.psum((jnp.sum(live_ints), jnp.sum(valid_ints)), ('feat', 'tok'))  44.5 us
    psum x1, blocking collectives, shards(): losses = lax.psum((local_sums[0], local_sums[1]), ('feat', 'tok'))  40.1 us
    transpose x4, local copies, waits for them, and re-layouts, attend_windows(): jnp.einsum('wqhe,wkhe->whqk', queries, keys_all, precision=lax.Precision....  31.6 us
    dot_general x11, matrix products, outer_sum(): lax.dot_general(left, right, (((0,), (0,)), ((), ())), preferred_element_...  24.5 us
  transfers between devices with their start and end apart: 4, of which 2 were waited for; matrix products, arithmetic and copies ran while one was open for 11% of the time, Pallas kernels for 0%

commit v1 on v0

v1 whole, which is shorter than its diff:
```python
import functools
import math

import jax
import jax.numpy as jnp
from jax import lax
from jax.experimental import pallas as pl
from jax.experimental.pallas import tpu as pltpu
from jax.sharding import PartitionSpec as PSpec

D = 120
H = 6
HD = 20
FF = 480
OBS = 512
LAYERS = 2
CAMS = 3
BOOKS = 2
CODES = 16
SPAN = 5
ACT = 7
WIN = 30
OFFS = SPAN * ACT
NORM_EPS = 1e-05
STEP_NO = 10
BETA_ONE = 0.9
BETA_TWO = 0.999
ADAM_EPS = 1e-08
DECAY_RATE = 0.1
LEARN_RATE = 0.05
GW = 4
GT = GW * WIN
CG = 4
L = CG * 128
CT = CG * GT
F32 = jnp.float32
BF = jnp.bfloat16
SCALE = HD ** (-0.5)
LROW = 2 * 1 + 3 * D + 2 + D + 1 + 2 + 4 * D + 4 + 4 * D + 1
BASE = OBS + 1 + WIN
HEAD = BASE + LAYERS * LROW
NV = 13
VROWS = [0, 1, 362, 363, 484, 485, 486, 967, 968, 969, 970, 1451]
(G1, B1, QB, VB, OB, G2, B2, FB0, FB1, FB2, FB3, PB) = range(12)


def nn(a, b):
    return lax.dot_general(a, b, (((1,), (0,)), ((), ())), preferred_element_type=F32)


def nt(a, b, precision=None):
    return lax.dot_general(a, b, (((1,), (1,)), ((), ())), preferred_element_type=F32, precision=precision)


def low(v):
    return v.astype(BF)


def pad8(v):
    return jnp.concatenate([v, jnp.zeros((8, v.shape[1]), v.dtype)], axis=0)


def tile4(v):
    return jnp.concatenate([v] * CG, axis=1)


def fold4(v):
    out = v[:, 0:128]
    for g in range(1, CG):
        out = out + v[:, 128 * g:128 * (g + 1)]
    return out


def iota(shape, axis):
    return lax.broadcasted_iota(jnp.int32, shape, axis)


def slab_at(h):
    return 20 * h - (4 if h % 2 else 0)


def head_stack(v):
    rows = iota((8, 128), 0)
    cols = []
    for h in range(H):
        a = slab_at(h)
        if h % 2 == 0:
            parts = [v[a:a + 16], jnp.where(rows < 4, v[a + 16:a + 24], 0.0)]
        else:
            parts = [jnp.where(rows >= 4, v[a:a + 8], 0.0), v[a + 8:a + 24]]
        if a > 0:
            parts = [jnp.zeros((a, 128), F32)] + parts
        if a + 24 < 128:
            parts = parts + [jnp.zeros((128 - a - 24, 128), F32)]
        cols.append(jnp.concatenate(parts, axis=0))
    return jnp.concatenate(cols, axis=1)


def join_slabs(slabs):
    rows = iota((8, 128), 0)
    parts = []
    for p in range(3):
        a, b = slabs[2 * p], slabs[2 * p + 1]
        parts += [a[0:16], jnp.where(rows < 4, a[16:24], b[0:8]), b[8:24]]
    return jnp.concatenate(parts, axis=0)


def slabs_of(v):
    return [v[slab_at(h):slab_at(h) + 24] for h in range(H)]


def hi_lo(v):
    hi = low(v)
    return hi, low(v - hi.astype(F32))


def normed(x):
    mean = jnp.sum(x, axis=0, keepdims=True) * (1.0 / D)
    c = x - mean
    var = jnp.sum(c * c, axis=0, keepdims=True) * (1.0 / D)
    r = lax.rsqrt(var + NORM_EPS)
    return c * r, r


def normed_back(d, xh, r):
    m0 = jnp.sum(d, axis=0, keepdims=True) * (1.0 / D)
    m1 = jnp.sum(d * xh, axis=0, keepdims=True) * (1.0 / D)
    return r * (d - m0 - xh * m1)


GA = math.sqrt(2.0 / math.pi)
GB = 0.044715


def gelu(x):
    t = jnp.tanh(GA * (x + GB * x * x * x))
    return 0.5 * x * (1.0 + t)


def gelu_back(x):
    x2 = x * x
    t = jnp.tanh(GA * x * (1.0 + GB * x2))
    return 0.5 * (1.0 + t) + (0.5 * GA) * x * (1.0 - t * t) * (1.0 + 3.0 * GB * x2)


PRECISE = True


class Refs:
    pass


def scratch_list(chunks):
    groups = chunks * CG
    return dict(
        w_obs=pltpu.VMEM((OBS, 128), BF),
        posb=pltpu.VMEM((GT, 128), F32),
        qkv_t=pltpu.VMEM((LAYERS, 384, 128), BF),
        qkv=pltpu.VMEM((LAYERS, 128, 384), BF),
        out_t=pltpu.VMEM((LAYERS, 128, 128), BF),
        out=pltpu.VMEM((LAYERS, 128, 128), BF),
        fc_t=pltpu.VMEM((LAYERS, 512, 128), BF),
        fc=pltpu.VMEM((LAYERS, 128, 512), BF),
        proj_t=pltpu.VMEM((LAYERS, 128, 512), BF),
        proj=pltpu.VMEM((LAYERS, 512, 128), BF),
        head_t=pltpu.VMEM((72, 128), BF),
        head=pltpu.VMEM((128, 128), BF),
        vec=pltpu.VMEM((32, 128), F32),
        bc=pltpu.VMEM((LAYERS, 12, GT, 128), F32),
        bcf=pltpu.VMEM((2, GT, 128), F32),
        bch=pltpu.VMEM((72, 128), F32),
        hc=pltpu.VMEM((128, 128), F32),
        ho=pltpu.VMEM((128, 128), F32),
        cnt=pltpu.VMEM((16, 256), F32),
        bias=pltpu.VMEM((groups, GT, 128), F32),
        live=pltpu.VMEM((chunks, 1, L), F32),
        act=pltpu.VMEM((chunks, 40, L), F32),
        val=pltpu.VMEM((chunks, 40, L), F32),
        code=pltpu.VMEM((chunks, 2, L), F32),
        x=pltpu.VMEM((chunks, D, L), F32),
        xh1=pltpu.VMEM((LAYERS, chunks, D, L), F32),
        r1=pltpu.VMEM((LAYERS, chunks, 1, L), F32),
        xh2=pltpu.VMEM((LAYERS, chunks, D, L), F32),
        r2=pltpu.VMEM((LAYERS, chunks, 1, L), F32),
        n1=pltpu.VMEM((LAYERS, chunks, 128, L), BF),
        n2=pltpu.VMEM((LAYERS, chunks, 128, L), BF),
        att=pltpu.VMEM((LAYERS, chunks, 128, L), BF),
        mix=pltpu.VMEM((LAYERS, chunks, 360, L), F32),
        prob=pltpu.VMEM((LAYERS, groups, GT, H * 128), F32),
        pre=pltpu.VMEM((LAYERS, chunks, FF, L), F32),
        inner=pltpu.VMEM((LAYERS, chunks, 512, L), BF),
        a_qkv=pltpu.VMEM((LAYERS, 128, 384), F32),
        a_out=pltpu.VMEM((LAYERS, 128, 128), F32),
        a_fc=pltpu.VMEM((LAYERS, 128, 512), F32),
        a_proj=pltpu.VMEM((LAYERS, 512, 128), F32),
        a_bias=pltpu.VMEM((LAYERS, 12, 128, 128), F32),
        a_obs=pltpu.VMEM((128, 512), F32),
        a_x=pltpu.VMEM((128, 128), F32),
        a_fin=pltpu.VMEM((2, 128, 128), F32),
        a_head=pltpu.VMEM((128, 128), F32),
        a_hb=pltpu.VMEM((128, 128), F32),
        loss=pltpu.VMEM((2, 8, 128), F32),
    )


def code_phases():
    for p in range(15):
        yield p, (32 * p) // D, (32 * p) % D


def off_phases():
    for p in range(24):
        yield p, (35 * p + 32) // D, (35 * p + 32) % D


def shifted(v, by):
    by %= 128
    return v if by == 0 else pltpu.roll(v, by, 1)


def take_phase(load, a, s, width, rows):
    lanes = iota((rows, 128), 1)
    first = shifted(load(a), -s)
    if s + width > D:
        second = shifted(load(a + 1), D - s)
        first = jnp.where(lanes < D - s, first, second)
    return jnp.where(lanes < width, first, 0.0)


def prep_weights(rg, R):
    R.w_obs[...] = low(rg[0:OBS, :])
    for w in range(GW):
        R.posb[pl.ds(WIN * w, WIN), :] = rg[OBS + 1:OBS + 1 + WIN, :] + rg[OBS:OBS + 1, :]
    R.vec[...] = jnp.zeros((32, 128), F32)
    for l in range(LAYERS):
        b = BASE + LROW * l
        for j in range(3):
            w = pad8(rg[pl.ds(b + 2 + j, D, stride=3), :])
            R.qkv[l, :, 128 * j:128 * (j + 1)] = low(w)
            R.qkv_t[l, 128 * j:128 * (j + 1), :] = low(w.T)
        w = pad8(rg[pl.ds(b + 364, D), :])
        R.out[l] = low(w)
        R.out_t[l] = low(w.T)
        for j in range(4):
            w = pad8(rg[pl.ds(b + 487 + j, D, stride=4), :])
            R.fc[l, :, 128 * j:128 * (j + 1)] = low(w)
            R.fc_t[l, 128 * j:128 * (j + 1), :] = low(w.T)
            w = pad8(rg[pl.ds(b + 971 + D * j, D), :])
            R.proj[l, 128 * j:128 * (j + 1), :] = low(w)
            R.proj_t[l, :, 128 * j:128 * (j + 1)] = low(w.T)
        for i, r in enumerate(VROWS):
            R.vec[pl.ds(12 * l + i, 1), :] = rg[pl.ds(b + r, 1), :]
    R.vec[24:26, :] = rg[pl.ds(HEAD, 2), :]
    R.hc[...] = jnp.zeros((128, 128), F32)
    R.ho[...] = jnp.zeros((128, 128), F32)
    c0 = HEAD + 2
    for p, a, s in code_phases():
        R.hc[pl.ds(p, 8, stride=15), :] = take_phase(
            lambda i: rg[pl.ds(c0 + i, 8, stride=4), :], a, s, 32, 8)
    o0 = c0 + 32
    for p, a, s in off_phases():
        R.ho[pl.ds(p, 5, stride=24), :] = take_phase(
            lambda i: rg[pl.ds(o0 + i, 5, stride=7), :], a, s, OFFS, 5)
    hw = R.hc[...] + shifted(R.ho[...], 32)
    R.head[...] = low(hw)
    R.head_t[...] = low(hw.T[0:72])
    lanes = iota((1, 128), 1)
    hb = jnp.where(lanes < 32, rg[pl.ds(o0, 1), :], 0.0)
    a, s = (D * OFFS + 32) // D, (D * OFFS + 32) % D
    ob = take_phase(lambda i: rg[pl.ds(o0 + i, 1), :], a, s, OFFS, 1)
    R.vec[26:27, :] = hb + shifted(ob, 32)
    columns = jnp.concatenate([R.vec[...], jnp.zeros((96, 128), F32)], axis=0).T
    for l in range(LAYERS):
        for i in range(12):
            R.bc[l, i] = jnp.broadcast_to(columns[0:D, 12 * l + i:12 * l + i + 1], (D, 128))
    for i in range(2):
        R.bcf[i] = jnp.broadcast_to(columns[0:D, 24 + i:25 + i], (D, 128))
    R.bch[...] = jnp.broadcast_to(columns[0:72, 26:27], (72, 128))


def spread_groups(v, groups, width):
    rows = v.shape[0]
    lanes = iota((rows, 128), 1)
    out = []
    for g in range(groups):
        t, o = (GT * g) // 128, (GT * g) % 128
        a = shifted(v[:, 128 * t:128 * (t + 1)], -o)
        if o + GT > 128:
            b = shifted(v[:, 128 * (t + 1):128 * (t + 2)], -o)
            a = jnp.where(lanes < 128 - o, a, b)
        out.append(jnp.where(lanes < GT, a, 0))
    return out


def prep_tokens(R, counts, codes, actions, valid, feat, chunks):
    groups = chunks * CG
    wins = counts.shape[1]
    R.cnt[...] = jnp.zeros(R.cnt.shape, F32)
    R.cnt[0:WIN // CAMS, :] = counts[...].astype(F32)
    k = iota((GT, 16), 0)
    step = (k % WIN) // CAMS
    sel = jnp.where(step == iota((GT, 16), 1), 1.0, 0.0)
    x = nn(low(sel), low(R.cnt[...]))
    y = jnp.where(iota((GT, wins), 1) % GW == iota((GT, wins), 0) // WIN, x, 0.0)
    pick = jnp.where(iota((wins, 128), 0) // GW == iota((wins, 128), 1) + groups * feat, 1.0, 0.0)
    z = nn(low(y), low(pick))
    kk = iota((GT, 128), 0)
    alive = jnp.where((kk % CAMS).astype(F32) < z, 1.0, 0.0)
    q = iota((GT, 128), 1)
    same = (kk // WIN == q // WIN) & ((kk % WIN) // CAMS <= (q % WIN) // CAMS) & (q < GT)
    base = jnp.where(same, 0.0, -1e30)
    for g in range(groups):
        R.bias[g] = jnp.where(jnp.broadcast_to(alive[:, g:g + 1], (GT, 128)) > 0.5, base, -1e30)
    rows = pad8(alive).T
    live_count = 0.0
    for g in range(groups):
        R.live[g // CG, :, 128 * (g % CG):128 * (g % CG + 1)] = rows[g:g + 1, :]
    for name, src in (("code", codes), ("act", actions), ("val", valid)):
        parts = spread_groups(src[...].astype(F32), groups, GT)
        dst = getattr(R, name)
        for g in range(groups):
            c, lo = g // CG, 128 * (g % CG)
            part = parts[g]
            if name == "val":
                part = part * rows[g:g + 1, :]
            if name != "code":
                dst[c, 32:40, lo:lo + 128] = jnp.zeros((8, 128), F32)
            dst[c, 0:part.shape[0], lo:lo + 128] = part
    lanes = iota((GT, 128), 1)
    live_total = jnp.sum(jnp.where(lanes < groups, alive, 0.0), keepdims=True)
    v = jnp.zeros((40, L), F32)
    for c in range(chunks):
        v = v + R.val[c]
    valid_total = jnp.sum(v, keepdims=True)
    return live_total, valid_total


def attend(q, k, v, bias):
    krow = pad8(k).T[0:GT]
    if PRECISE:
        kh, kl = hi_lo(krow)
        qh, ql = hi_lo(head_stack(q))
        s = nn(jnp.concatenate([kh, kl, kh], axis=1), jnp.concatenate([qh, qh, ql], axis=0))
    else:
        s = nn(low(krow), low(head_stack(q)))
    s = s + jnp.concatenate([bias] * H, axis=1)
    e = jnp.exp(s - jnp.max(s, axis=0, keepdims=True))
    p = e * (1.0 / jnp.sum(e, axis=0, keepdims=True))
    slabs = []
    vs = slabs_of(v)
    for h in range(H):
        ph = pad8(p[:, 128 * h:128 * (h + 1)])
        if PRECISE:
            pa, pb = hi_lo(ph)
            va, vb = hi_lo(vs[h])
            slabs.append(nn(jnp.concatenate([va, vb, va], axis=1), jnp.concatenate([pa, pa, pb], axis=0)))
        else:
            slabs.append(nn(low(vs[h]), low(ph)))
    return join_slabs(slabs), p


def attend_back(do, p, q, k, v):
    vrow = pad8(v).T[0:GT]
    dp = nn(low(vrow), low(head_stack(do)))
    t = p * dp
    ds = t - p * jnp.sum(t, axis=0, keepdims=True)
    dq, dk, dv = [], [], []
    qs, ks, os = slabs_of(q), slabs_of(k), slabs_of(do)
    for h in range(H):
        dsh = low(pad8(ds[:, 128 * h:128 * (h + 1)]))
        ph = low(pad8(p[:, 128 * h:128 * (h + 1)]))
        dq.append(nn(low(ks[h]), dsh))
        dk.append(nt(low(qs[h]), dsh))
        dv.append(nt(low(os[h]), ph))
    return join_slabs(dq) * SCALE, join_slabs(dk), join_slabs(dv)


def embed(R, obs, c):
    rows = nn(jnp.concatenate(obs, axis=1), R.w_obs[...])
    parts = []
    for g in range(CG):
        r = rows[GT * g:GT * (g + 1)] + R.posb[...]
        parts.append(pad8(r).T[0:D])
    return jnp.concatenate(parts, axis=1)


def layer_fwd(R, l, c, x):
    def vec(i):
        return tile4(R.bc[l, i])

    xh, r = normed(x)
    R.xh1[l, c] = xh
    R.r1[l, c] = r
    n1 = low(pad8(xh * vec(G1) + vec(B1)))
    R.n1[l, c] = n1
    mix = nn(R.qkv_t[l], n1)
    q = (mix[0:D] + vec(QB)) * SCALE
    k = mix[128:128 + D]
    v = mix[256:256 + D] + vec(VB)
    R.mix[l, c, 0:D] = q
    R.mix[l, c, D:2 * D] = k
    R.mix[l, c, 2 * D:3 * D] = v
    parts = []
    for g in range(CG):
        at = slice(128 * g, 128 * (g + 1))
        o, p = attend(q[:, at], k[:, at], v[:, at], R.bias[c * CG + g])
        R.prob[l, c * CG + g] = p
        parts.append(o)
    att = low(pad8(jnp.concatenate(parts, axis=1)))
    R.att[l, c] = att
    x1 = x + nn(R.out_t[l], att)[0:D] + vec(OB)
    xh, r = normed(x1)
    R.xh2[l, c] = xh
    R.r2[l, c] = r
    n2 = low(pad8(xh * vec(G2) + vec(B2)))
    R.n2[l, c] = n2
    pre = nn(R.fc_t[l], n2)
    parts = []
    for j in range(4):
        pj = pre[128 * j:128 * j + D] + vec(FB0 + j)
        R.pre[l, c, D * j:D * (j + 1)] = pj
        parts.append(low(pad8(gelu(pj))))
    inner = jnp.concatenate(parts, axis=0)
    R.inner[l, c] = inner
    return x1 + nn(R.proj_t[l], inner)[0:D] + vec(PB)


def head_step(R, c, x, live_total, valid_total):
    xh, r = normed(x)
    fin = low(pad8(xh * tile4(R.bcf[0]) + tile4(R.bcf[1])))
    hd = nn(R.head_t[...], fin) + tile4(R.bch[...])
    live = R.live[c]
    lw = live * (1.0 / live_total)
    rows = iota((CODES, L), 0).astype(F32)
    grads = []
    csum = jnp.zeros((1, L), F32)
    for b in range(BOOKS):
        lg = hd[CODES * b:CODES * (b + 1)]
        m = jnp.max(lg, axis=0, keepdims=True)
        e = jnp.exp(lg - m)
        s = jnp.sum(e, axis=0, keepdims=True)
        hot = rows == R.code[c, b:b + 1, :]
        picked = jnp.sum(jnp.where(hot, lg, 0.0), axis=0, keepdims=True)
        csum = csum + (jnp.log(s) + m - picked) * live
        grads.append((e * (1.0 / s) - jnp.where(hot, 1.0, 0.0)) * lw)
    diff = hd[32:72] - R.act[c]
    val = R.val[c]
    sq = diff * diff + 1.0
    ri = lax.rsqrt(sq)
    asum = val * (sq * ri)
    grads.append((val * (1.0 / valid_total)) * (diff * ri))
    R.loss[0, 0:1] += fold4(csum)
    af = fold4(asum)
    R.loss[1] += af[0:8] + af[8:16] + af[16:24] + af[24:32] + af[32:40]
    dh = jnp.concatenate(grads, axis=0)
    R.a_hb[0:72] += fold4(dh)
    dhl = low(jnp.concatenate([dh, jnp.zeros((56, L), F32)], axis=0))
    R.a_head[...] += nt(fin, dhl)
    df = nn(R.head[...], dhl)[0:D]
    R.a_fin[0, 0:D] += fold4(df * xh)
    R.a_fin[1, 0:D] += fold4(df)
    return normed_back(df * tile4(R.bcf[0]), xh, r)


def layer_bwd(R, l, c, dout):
    def vec(i):
        return tile4(R.bc[l, i])

    def add_bias(i, v):
        R.a_bias[l, i, 0:D] += fold4(v)

    outl = low(pad8(dout))
    R.a_proj[l] += nt(R.inner[l, c], outl)
    add_bias(PB, dout)
    di = nn(R.proj[l], outl)
    parts = []
    for j in range(4):
        pj = di[128 * j:128 * j + D] * gelu_back(R.pre[l, c, D * j:D * (j + 1)])
        plow = low(pad8(pj))
        add_bias(FB0 + j, plow.astype(F32)[0:D])
        parts.append(plow)
    prel = jnp.concatenate(parts, axis=0)
    R.a_fc[l] += nt(R.n2[l, c], prel)
    dn = nn(R.fc[l], prel)[0:D]
    xh = R.xh2[l, c]
    add_bias(G2, dn * xh)
    add_bias(B2, dn)
    dmid = normed_back(dn * vec(G2), xh, R.r2[l, c]) + dout
    midl = low(pad8(dmid))
    R.a_out[l] += nt(R.att[l, c], midl)
    add_bias(OB, dmid)
    da = nn(R.out[l], midl)[0:D]
    dq, dk, dv = [], [], []
    for g in range(CG):
        at = slice(128 * g, 128 * (g + 1))
        res = attend_back(da[:, at], R.prob[l, c * CG + g], R.mix[l, c, 0:D, at],
                          R.mix[l, c, D:2 * D, at], R.mix[l, c, 2 * D:3 * D, at])
        for lst, val in zip((dq, dk, dv), res):
            lst.append(val)
    dq, dk, dv = (jnp.concatenate(v, axis=1) for v in (dq, dk, dv))
    add_bias(QB, dq)
    add_bias(VB, dv)
    mixl = jnp.concatenate([low(pad8(dq)), low(pad8(dk)), low(pad8(dv))], axis=0)
    R.a_qkv[l] += nt(R.n1[l, c], mixl)
    dn = nn(R.qkv[l], mixl)[0:D]
    xh = R.xh1[l, c]
    add_bias(G1, dn * xh)
    add_bias(B1, dn)
    return normed_back(dn * vec(G1), xh, R.r1[l, c]) + dmid


def embed_bwd(R, obs, c, dx):
    R.a_x[0:D] += fold4(dx)
    lanes = iota((D, 128), 1)
    tiles = []
    gs = [dx[:, 128 * g:128 * (g + 1)] for g in range(CG)]
    for t in range(CG):
        a = shifted(gs[t], -8 * t)
        b = shifted(gs[t + 1], 120 - 8 * t) if t + 1 < CG else jnp.zeros((D, 128), F32)
        tiles.append(jnp.where(lanes < GT - 8 * t, a, b))
    gl = low(pad8(jnp.concatenate(tiles, axis=1)))
    R.a_obs[...] += nn(gl, jnp.concatenate(obs, axis=1))


def zero_grads(R):
    for name in ("a_qkv", "a_out", "a_fc", "a_proj", "a_bias", "a_obs", "a_x", "a_fin", "a_head", "a_hb", "loss"):
        ref = getattr(R, name)
        ref[...] = jnp.zeros(ref.shape, F32)


HIGH = lax.Precision.HIGHEST


def pack_layer(R, rg, l):
    b = BASE + LROW * l
    for j in range(3):
        rg[pl.ds(b + 2 + j, D, stride=3), :] = R.a_qkv[l, 0:D, 128 * j:128 * (j + 1)]
    rg[pl.ds(b + 364, D), :] = R.a_out[l, 0:D]
    for j in range(4):
        rg[pl.ds(b + 487 + j, D, stride=4), :] = R.a_fc[l, 0:D, 128 * j:128 * (j + 1)]
        rg[pl.ds(b + 971 + D * j, D), :] = R.a_proj[l, 128 * j:128 * j + D, :]
    rows = nt(jnp.ones((8, 128), F32), R.a_bias[l].reshape(12 * 128, 128), HIGH)
    for i, r in enumerate(VROWS):
        rg[pl.ds(b + r, 1), :] = rows[0:1, 128 * i:128 * (i + 1)]


def pack_embed(R, rg):
    for f in range(OBS // 128):
        rg[128 * f:128 * (f + 1), :] = R.a_obs[:, 128 * f:128 * (f + 1)].T
    slot, lane = iota((32, 128), 0), iota((32, 128), 1)
    sel = jnp.where((slot == 0) | (lane % WIN == slot - 1), 1.0, 0.0)
    sel = jnp.where(lane < GT, sel, 0.0)
    rows = nt(sel, R.a_x[...], HIGH)
    rg[pl.ds(OBS, 1 + WIN), :] = rows[0:1 + WIN]


def pack_head(R, rg):
    rows = nt(jnp.ones((8, 128), F32), R.a_fin[...].reshape(256, 128), HIGH)
    for i in range(2):
        rg[pl.ds(HEAD + i, 1), :] = rows[0:1, 128 * i:128 * (i + 1)]
    lanes8 = iota((8, 128), 1)
    grad = R.a_head[...]
    R.hc[...] = jnp.where(iota((128, 128), 1) < 32, grad, 0.0)
    R.ho[...] = jnp.where(iota((128, 128), 1) < OFFS, shifted(grad, -32), 0.0)
    c0 = HEAD + 2
    o0 = c0 + 32

    def put(phases, src, rows_n, stride, width, count):
        acc = [jnp.zeros((rows_n, 128), F32) for _ in range(count + 1)]
        lanes = iota((rows_n, 128), 1)
        for p, a, s in phases:
            v = src[pl.ds(p, rows_n, stride=stride), :]
            first = shifted(v, s)
            if s + width > D:
                acc[a] = acc[a] + jnp.where((lanes >= s) & (lanes < D), first, 0.0)
                acc[a + 1] = acc[a + 1] + jnp.where(lanes < s + width - D, shifted(v, s - D), 0.0)
            else:
                acc[a] = acc[a] + first
        return acc

    acc = put(code_phases(), R.hc, 8, 15, 32, 4)
    for a in range(4):
        rg[pl.ds(c0 + a, 8, stride=4), :] = acc[a]
    hb = nt(jnp.ones((8, 128), F32), R.a_hb[...], HIGH)[0:1]
    lane1 = iota((1, 128), 1)
    rg[pl.ds(o0, 48), :] = jnp.zeros((48, 128), F32)
    acc = put(off_phases(), R.ho, 5, 24, OFFS, 7)
    for a in range(7):
        rg[pl.ds(o0 + a, 5, stride=7), :] = acc[a]
    rg[pl.ds(o0 + 7, 5, stride=7), :] = rg[pl.ds(o0 + 7, 5, stride=7), :] + acc[7]
    rg[pl.ds(o0, 1), :] = rg[pl.ds(o0, 1), :] + jnp.where(lane1 < 32, hb, 0.0)
    a, s = (D * OFFS + 32) // D, (D * OFFS + 32) % D
    ob = jnp.where(lane1 < OFFS, shifted(hb, -32), 0.0)
    rg[pl.ds(o0 + a, 1), :] = rg[pl.ds(o0 + a, 1), :] + shifted(ob, s)


MESH = pl.DeviceIdType.MESH


def round_up(n, m):
    return -(-n // m) * m


class Plan:
    def __init__(self, feats, toks, shard, tok_rows):
        self.feats, self.toks, self.chips = feats, toks, toks // 2
        self.shard = shard
        self.block = round_up(-(-(shard + 112) // D), 16)
        self.flat_rows = self.block // 16 * 15
        self.local = round_up(-(-shard // 128), 8)
        self.work = round_up(max(self.flat_rows, self.local + 1), 8)
        self.own_rows = tok_rows // feats
        self.chunks = self.own_rows // CT
        self.grid = round_up(-(-(shard * feats * toks) // D) + self.block, 8)


def comm_scratch(P):
    dma = pltpu.SemaphoreType.DMA
    B, C, Fn = P.block, P.chips, P.feats
    return dict(
        rg=pltpu.VMEM((P.grid, 128), F32),
        ob=pltpu.VMEM((P.chunks, Fn, L, 128), BF),
        pg=pltpu.VMEM((2, C, Fn, B, 128), BF),
        loc=pltpu.VMEM((P.work, 128), F32),
        rblk=pltpu.VMEM((B, 128), F32),
        codes_in=pltpu.VMEM((BOOKS, P.own_rows), jnp.int32),
        act_in=pltpu.VMEM((OFFS, P.own_rows), F32),
        val_in=pltpu.VMEM((OFFS, P.own_rows), jnp.int32),
        tz=pltpu.VMEM((2, Fn, 8, 128), F32),
        tc=pltpu.VMEM((2, C, 8, 128), F32),
        ts=pltpu.VMEM((2, 2, 8, 128), F32),
        sb1=pltpu.VMEM((C, Fn, B, 128), F32),
        rb1=pltpu.VMEM((C, Fn, B, 128), F32),
        sb2=pltpu.VMEM((C, Fn, B, 128), F32),
        rb2=pltpu.VMEM((C, Fn, B, 128), F32),
        sb3=pltpu.VMEM((Fn, B, 128), F32),
        rb3=pltpu.VMEM((Fn, B, 128), F32),
        s_p1=dma((2, Fn)), s_p2=dma((2, C)), s_p3=dma((2, C)),
        s_tz=dma((2, 2, Fn)), s_tc=dma((2, 2, C)), s_ts=dma((2, 2)),
        s_ob=dma((2, P.chunks, Fn)),
        s_in=dma((3,)),
        s_r1=dma((2, C)), s_r2=dma((2, C)), s_r3=dma((2, Fn)),
    )


def to_rows(loc, rblk, delta, P):
    v = loc[...]
    lanes = iota(v.shape, 1)
    moved = pltpu.roll(v, delta, 1)
    loc[...] = jnp.where(lanes >= delta, moved, pltpu.roll(moved, 1, 0))
    n = P.block // 16
    lane = iota((n, 128), 1)
    for j in range(16):
        if j < 15:
            a = shifted(loc[pl.ds(j, n, stride=15), :], 8 * j)
        if j > 0:
            b = shifted(loc[pl.ds(j - 1, n, stride=15), :], 8 * j)
            a = jnp.where(lane < 8 * j, b, a) if j < 15 else b
        rblk[pl.ds(j, n, stride=16), :] = jnp.where(lane < D, a, 0.0)


def from_rows(rblk, loc, delta, P):
    n = P.block // 16
    lane = iota((n, 128), 1)
    loc[...] = jnp.zeros(loc.shape, F32)
    for i in range(15):
        a = shifted(rblk[pl.ds(i, n, stride=16), :], -8 * i)
        b = shifted(rblk[pl.ds(i + 1, n, stride=16), :], D - 8 * i)
        loc[pl.ds(i, n, stride=15), :] = jnp.where(lane < D - 8 * i, a, b)
    v = loc[...]
    lanes = iota(v.shape, 1)
    moved = pltpu.roll(v, lax.rem(128 - delta, 128), 1)
    v = jnp.where(lanes < 128 - delta, moved, pltpu.roll(moved, P.work - 1, 0))
    return v[0:P.local]


def step_kernel(P, names, master, first, second, obs, counts, codes, actions, valid,
                new_master, new_first, new_second, sums, *scratch):
    R = Refs()
    for name, ref in zip(names, scratch):
        setattr(R, name, ref)
    Fn, C, B = P.feats, P.chips, P.block
    feat = lax.axis_index("feat")
    tok = lax.axis_index("tok")
    chip = tok // 2
    core = tok % 2
    me = feat * P.toks + tok
    delta = lax.rem(me * P.shard, D)

    def z_peer(i):
        return lax.rem(feat + i, Fn)

    def z_from(i):
        return lax.rem(feat + Fn - i, Fn)

    def c_peer(i):
        return lax.rem(chip + i, C)

    def c_from(i):
        return lax.rem(chip + C - i, C)

    def to_z(i):
        return (z_peer(i), tok)

    def to_c(i):
        return (feat, 2 * c_peer(i) + core)

    sibling = (feat, 2 * chip + 1 - core)

    def send(src, dst, sems, at, dev):
        return pltpu.make_async_remote_copy(
            src_ref=src, dst_ref=dst, send_sem=sems.at[(0,) + at], recv_sem=sems.at[(1,) + at],
            device_id=dev, device_id_type=MESH)

    n = P.own_rows
    ins = []
    for i, (src, dst) in enumerate(((codes, R.codes_in), (actions, R.act_in), (valid, R.val_in))):
        ins.append(pltpu.make_async_copy(src.at[:, pl.ds(pl.multiple_of(feat * n, 128), n)], dst, R.s_in.at[i]))
        ins[-1].start()

    barrier = pltpu.get_barrier_semaphore()
    peers = [to_z(i) for i in range(1, Fn)] + [to_c(i) for i in range(1, C)] + [sibling]
    for dev in peers:
        pl.semaphore_signal(barrier, inc=1, device_id=dev, device_id_type=MESH)

    R.loc[...] = jnp.zeros(R.loc.shape, F32)
    R.loc[0:P.local, :] = master[...]
    to_rows(R.loc, R.rblk, delta, P)
    R.pg[core, chip, feat] = low(R.rblk[...])
    pl.semaphore_wait(barrier, len(peers))

    p1 = []
    for i in range(1, Fn):
        blk = R.pg.at[core, chip, feat]
        p1.append(send(blk, blk, R.s_p1, (i,), to_z(i)))
        p1[-1].start()

    own = []
    others = []

    def start_obs(c):
        for i in range(1, Fn):
            src = obs.at[pl.ds(pl.multiple_of(z_peer(i) * n + CT * c, 16), CT), :]
            cp = send(src, R.ob.at[c, feat, pl.ds(0, CT), :], R.s_ob, (c, i), to_z(i))
            cp.start()
            others.append(cp)
        src = obs.at[pl.ds(pl.multiple_of(feat * n + CT * c, 16), CT), :]
        cp = pltpu.make_async_copy(src, R.ob.at[c, feat, pl.ds(0, CT), :], R.s_ob.at[0, c, 0])
        cp.start()
        own.append(cp)

    start_obs(0)
    for cp in ins:
        cp.wait()
    zero_grads(R)
    for c in range(P.chunks):
        for f in range(Fn):
            R.ob[c, f, CT:L, :] = jnp.zeros((L - CT, 128), BF)
    live_n, valid_n = prep_tokens(R, counts, R.codes_in, R.act_in, R.val_in, feat, P.chunks)

    def two_rows(a, b):
        return jnp.concatenate([jnp.broadcast_to(a, (1, 128)), jnp.broadcast_to(b, (1, 128)),
                                jnp.zeros((6, 128), F32)], axis=0)

    def hop_z(w, value):
        R.tz[w, feat] = value
        cps = []
        for i in range(1, Fn):
            cps.append(send(R.tz.at[w, feat], R.tz.at[w, feat], R.s_tz.at[w], (i,), to_z(i)))
            cps[-1].start()
        return cps

    def hop_c(w, value):
        R.tc[w, chip] = value
        cps = []
        for i in range(1, C):
            cps.append(send(R.tc.at[w, chip], R.tc.at[w, chip], R.s_tc.at[w], (i,), to_c(i)))
            cps[-1].start()
        return cps

    def hop_s(w, value):
        R.ts[w, core] = value
        cp = send(R.ts.at[w, core], R.ts.at[w, core], R.s_ts.at[w], (), sibling)
        cp.start()
        return [cp]

    def total(ref, w, count):
        v = ref[w, 0]
        for i in range(1, count):
            v = v + ref[w, i]
        return v

    def wait_all(cps):
        for cp in cps:
            cp.wait()

    tz = hop_z(0, two_rows(live_n, valid_n))
    wait_all(p1)
    p2 = []
    for i in range(1, C):
        blk = R.pg.at[core, chip]
        p2.append(send(blk, blk, R.s_p2, (i,), to_c(i)))
        p2[-1].start()
    p3 = [send(R.pg.at[core, chip], R.pg.at[core, chip], R.s_p3, (0,), sibling)]
    p3[0].start()
    wait_all(tz)
    tc = hop_c(0, total(R.tz, 0, Fn))
    for i in range(1, C):
        p2[i - 1].wait_recv()
        blk = R.pg.at[core, c_from(i)]
        p3.append(send(blk, blk, R.s_p3, (i,), sibling))
        p3[-1].start()
    for c in range(1, P.chunks):
        start_obs(c)
    wait_all(tc)
    ts = hop_s(0, total(R.tc, 0, C))
    for cp in p2:
        cp.wait_send()
    wait_all(p3)
    wait_all(ts)
    counted = total(R.ts, 0, 2)
    live_total = counted[0:1, 0:1]
    valid_total = counted[1:2, 0:1]

    R.rg[0:8, :] = jnp.zeros((8, 128), F32)

    def place(d, _):
        r0 = (P.shard * d) // D
        f, t = d // P.toks, d % P.toks
        blk = R.pg[t % 2, t // 2, f].astype(F32)
        before = R.rg[pl.ds(r0, 1), :]
        R.rg[pl.ds(r0, B), :] = blk
        R.rg[pl.ds(r0, 1), :] = blk[0:1] + before
        return 0

    lax.fori_loop(0, Fn * P.toks, place, 0)
    prep_weights(R.rg, R)

    def fwd(c, _):
        for i in range(1, Fn):
            send(R.ob.at[c, feat, pl.ds(0, CT), :], R.ob.at[c, feat, pl.ds(0, CT), :],
                 R.s_ob, (c, i), to_z(i)).wait_recv()
        pltpu.make_async_copy(obs.at[pl.ds(0, CT), :], R.ob.at[c, feat, pl.ds(0, CT), :],
                              R.s_ob.at[0, c, 0]).wait()
        R.x[c] = embed(R, [R.ob[c, f, 0:CT, :] for f in range(Fn)], c)

        def lay(l, _):
            R.x[c] = layer_fwd(R, l, c, R.x[c])
            return 0

        lax.fori_loop(0, LAYERS, lay, 0)
        return 0

    lax.fori_loop(0, P.chunks, fwd, 0)

    def heads(c, _):
        R.x[c] = head_step(R, c, R.x[c], live_total, valid_total)
        return 0

    lax.fori_loop(0, P.chunks, heads, 0)
    lz = hop_z(1, two_rows(jnp.sum(R.loss[0], keepdims=True), jnp.sum(R.loss[1], keepdims=True)))

    def back(i, _):
        def chunk(c, _):
            R.x[c] = layer_bwd(R, LAYERS - 1 - i, c, R.x[c])
            return 0

        lax.fori_loop(0, P.chunks, chunk, 0)
        return 0

    lax.fori_loop(0, LAYERS, back, 0)

    def last(c, _):
        embed_bwd(R, [R.ob[c, f] for f in range(Fn)], c, R.x[c])
        return 0

    lax.fori_loop(0, P.chunks, last, 0)
    wait_all(lz)
    lc = hop_c(1, total(R.tz, 1, Fn))
    R.rg[pl.ds(HEAD + 32, P.grid - HEAD - 32), :] = jnp.zeros((P.grid - HEAD - 32, 128), F32)
    for l in range(LAYERS):
        pack_layer(R, R.rg, l)
    pack_embed(R, R.rg)
    pack_head(R, R.rg)

    def rows_of(f, ch, co):
        return (P.shard * (f * P.toks + 2 * ch + co)) // D

    r1 = []
    for i in range(1, C + 1):
        ch = c_peer(i)
        for f in range(Fn):
            R.sb1[i - 1, f] = R.rg[pl.ds(rows_of(f, ch, 1 - core), B), :]
        r1.append(send(R.sb1.at[i - 1], R.rb1.at[i - 1], R.s_r1, (i - 1,), sibling))
        r1[-1].start()
    wait_all(lc)
    ls = hop_s(1, total(R.tc, 1, C))
    r2 = []
    for i in range(1, C):
        ch = c_peer(i)
        r1[i - 1].wait_recv()
        for f in range(Fn):
            R.sb2[i, f] = R.rg[pl.ds(rows_of(f, ch, core), B), :] + R.rb1[i - 1, f]
        r2.append(send(R.sb2.at[i], R.rb2.at[i], R.s_r2, (i,), to_c(i)))
        r2[-1].start()
    r1[C - 1].wait_recv()
    for f in range(Fn):
        R.sb2[0, f] = R.rg[pl.ds(rows_of(f, chip, core), B), :] + R.rb1[C - 1, f]
    for cp in r2:
        cp.wait_recv()
    r3 = []
    for i in range(1, Fn):
        f = z_peer(i)
        v = R.sb2[0, f]
        for j in range(1, C):
            v = v + R.rb2[j, f]
        R.sb3[i] = v
        r3.append(send(R.sb3.at[i], R.rb3.at[i], R.s_r3, (i,), to_z(i)))
        r3[-1].start()
    v = R.sb2[0, feat]
    for j in range(1, C):
        v = v + R.rb2[j, feat]
    for i in range(1, Fn):
        r3[i - 1].wait_recv()
        v = v + R.rb3[i]
    R.rblk[...] = v
    grad = from_rows(R.rblk, R.loc, delta, P)
    f_new = BETA_ONE * first[...] + (1.0 - BETA_ONE) * grad
    s_new = BETA_TWO * second[...] + (1.0 - BETA_TWO) * grad * grad
    f_hat = f_new / (1.0 - BETA_ONE ** STEP_NO)
    s_hat = s_new / (1.0 - BETA_TWO ** STEP_NO)
    old = master[...]
    new_first[...] = f_new
    new_second[...] = s_new
    new_master[...] = old - LEARN_RATE * (f_hat / (jnp.sqrt(s_hat) + ADAM_EPS) + DECAY_RATE * old)
    wait_all(ls)
    lost = total(R.ts, 1, 2)
    sums[...] = jnp.concatenate([lost[0:1], counted[0:1], lost[1:2], counted[1:2], jnp.zeros((4, 128), F32)], axis=0)
    for cps in (others, r1, r2, r3):
        for cp in cps:
            cp.wait_send()


def solution(mesh):
    feats, toks = mesh.shape["feat"], mesh.shape["tok"]

    def shards(master, first, second, obs, counts, codes, actions, valid):
        P_ = Plan(feats, toks, master.shape[0], obs.shape[0])
        scratch = dict(scratch_list(P_.chunks))
        scratch.update(comm_scratch(P_))
        pad = P_.local * 128 - P_.shard
        flat = [jnp.pad(v, (0, pad)).reshape(P_.local, 128) for v in (master, first, second)]
        vmem = pl.BlockSpec(memory_space=pltpu.VMEM)
        hbm = pl.BlockSpec(memory_space=pl.ANY)
        out = jax.ShapeDtypeStruct((P_.local, 128), F32)
        outs = pl.pallas_call(
            functools.partial(step_kernel, P_, list(scratch)),
            out_shape=(out, out, out, jax.ShapeDtypeStruct((8, 128), F32)),
            in_specs=[vmem, vmem, vmem, hbm, vmem, hbm, hbm, hbm],
            out_specs=(vmem,) * 4,
            scratch_shapes=list(scratch.values()),
            compiler_params=pltpu.CompilerParams(
                collective_id=0, has_side_effects=True, vmem_limit_bytes=60 * 2 ** 20),
        )(*flat, obs, counts.T, codes.T, actions, valid)
        cut = [v.reshape(-1)[:P_.shard] for v in outs[:3]]
        return (*cut, outs[3][0:4, 0])

    weights = PSpec(("feat", "tok"))
    return jax.shard_map(
        shards, mesh=mesh,
        in_specs=(weights, weights, weights, PSpec("tok", "feat"), PSpec("tok", None), PSpec("tok", None),
                  PSpec(None, "tok"), PSpec(None, "tok")),
        out_specs=(weights, weights, weights, PSpec()), check_vma=False)
```

time: 927 us -> 125 us (0.13)
  local copies, waits for them, and re-layouts: 293 us -> 8.51 us
  matrix products: 236 us -> 0 us
  waiting for transfers between devices: 225 us -> 0 us
  Pallas kernels: 0 us -> 115 us
  blocking collectives: 84.7 us -> 0 us
  other arithmetic: 68.6 us -> 0 us
  between operations: 17.2 us -> 0.64 us
    dot_general x44 -> x0, matrix products: 236 us -> none  [the longest x6 89.9 us: attend_windows(): jnp.einsum('whqk,wkhe->wqhe', probs, values_all, precision=lax.Precision....]
    unnamed x6 -> x0, waiting for transfers between devices: 225 us -> none
    pallas_call x0 -> x1, Pallas kernels: none -> 115 us  [shards(): pl.pallas_call(functools.partial(step_kernel, P_, list(scratch)), out_sha...]
    psum x2 -> x0, blocking collectives: 84.7 us -> none  [the longest x1 44.5 us: shards(): lax.psum((jnp.sum(live_ints), jnp.sum(valid_ints)), ('feat', 'tok'))]
    reshape x36 -> x2, local copies, waits for them, and re-layouts: 70.2 us -> 2.91 us  [shards(): jnp.pad(v, (0, pad)).reshape(P_.local, 128)]
    transpose x8 -> x0, local copies, waits for them, and re-layouts: 52.9 us -> none  [the longest x4 31.6 us: attend_windows(): jnp.einsum('wqhe,wkhe->whqk', queries, keys_all, precision=lax.Precision....]
    concatenate x1 -> x0, local copies, waits for them, and re-layouts: 50.5 us -> none  [shards(): jnp.concatenate([piece.reshape(-1).astype(jnp.float32) for piece in all_g...]
    reduce_sum x28 -> x0, other arithmetic: 39.1 us -> none  [the longest x2 11.4 us: attend_windows(): probs = jnp.exp(scores - highest)]
  transfers between devices with their start and end apart: 4 -> 0, of which waited for: 2 -> 0; matrix products, arithmetic and copies ran while one was open for 11% -> 0% of each run, Pallas kernels for 0% -> 0%
where the time goes in v1:
time: 125 us; the launch traced here: 124 us
  Pallas kernels  115 us (92%)
  local copies, waits for them, and re-layouts  8.51 us (7%)
    pallas_call x1, Pallas kernels, shards(): pl.pallas_call(functools.partial(step_kernel, P_, list(scratch)), out_sha...  115 us
    unnamed x3, local copies, waits for them, and re-layouts  4.3 us
    reshape x2, local copies, waits for them, and re-layouts, shards(): jnp.pad(v, (0, pad)).reshape(P_.local, 128)  2.91 us

profile of v1, /device:TPU:0, one launch (start us, length us, event | category | flops | bytes accessed | tf_op | source)
XLA Modules:
  0.0 124.4 jit_solution(2276210133457451188)
XLA Ops:
  0.6 1.4 %pad_bitcast_fusion.2.master = f32[104,128]{1,0:T(8,128)} fusion(f32[13192]{0:T(1024)} %param.8), kind=kLoop, calls=%fused_computation.2 | loop fusion | bytes 106016 | tf_op jit(solution)/shard_map/reshape | solution.py:952
  2.1 1.5 %pad_bitcast_fusion = (f32[104,128]{1,0:T(8,128)}, f32[104,128]{1,0:T(8,128)}) fusion(f32[13192]{0:T(1024)} %param.10, f32[13192]{0:T(1024)} %param.9), kind=kLoop, calls=%fused_computation | loop fusion | bytes 212032 | tf_op jit(solution)/shard_map/reshape | solution.py:952
  3.5 115.2 %shard_map.111 = (f32[104,128]{1,0:T(8,128)}, f32[104,128]{1,0:T(8,128)}, f32[104,128]{1,0:T(8,128)}, f32[8,128]{1,0:T(8,128)}) custom-call(f32[104,128]{1,0:T(8,128)} %pad_bitcast_fusion.2.master, f32[104,128]{1,0:T(8,128)} %get-tuple-element.13.first, f32[104,128]{1,0:T(8,128)} %get-tuple-element.12.second, bf16[7680,128]{1,0:T(8,128)(2,1)} %obs.1, ...), custom_call_target="tpu_custom_call" | custom-call | tf_op jit(solution)/shard_map/pallas_call | solution.py:956
  118.8 1.3 %slice_reduce_fusion = f32[4]{0:T(128)} fusion(f32[8,128]{1,0:T(8,128)} %get-tuple-element.11), kind=kLoop, calls=%fused_computation.3 | loop fusion | bytes 32 | tf_op jit(solution)/shard_map/slice | solution.py:966
  120.1 1.4 %copy.15 = f32[13192]{0:T(1024)} copy(f32[13192]{0:T(1024)} %bitcast.17) | data formatting | bytes 105536
  121.5 1.4 %copy.16 = f32[13192]{0:T(1024)} copy(f32[13192]{0:T(1024)} %bitcast.16) | data formatting | bytes 105536
  123.0 1.4 %copy.17 = f32[13192]{0:T(1024)} copy(f32[13192]{0:T(1024)} %bitcast.15) | data formatting | bytes 105536

commit v2 on v1

--- a/solution.py
+++ b/solution.py
@@ -132,18 +132,16 @@
 GB = 0.044715
 
 
-def gelu(x):
-    t = jnp.tanh(GA * (x + GB * x * x * x))
-    return 0.5 * x * (1.0 + t)
-
-
-def gelu_back(x):
-    x2 = x * x
-    t = jnp.tanh(GA * x * (1.0 + GB * x2))
-    return 0.5 * (1.0 + t) + (0.5 * GA) * x * (1.0 - t * t) * (1.0 + 3.0 * GB * x2)
-
-
-PRECISE = True
+def gelu_half(x):
+    return 0.5 + 0.5 * jnp.tanh(x * (GA + (GA * GB) * (x * x)))
+
+
+def gelu_slope(x, s):
+    return s + (x * s) * (1.0 - s) * (2.0 * GA + (6.0 * GA * GB) * (x * x))
+
+
+LOG2E = math.log2(math.e)
+BIG = 1e30
 
 
 class Refs:
@@ -172,27 +170,34 @@
         hc=pltpu.VMEM((128, 128), F32),
         ho=pltpu.VMEM((128, 128), F32),
         cnt=pltpu.VMEM((16, 256), F32),
-        bias=pltpu.VMEM((groups, GT, 128), F32),
         live=pltpu.VMEM((chunks, 1, L), F32),
         act=pltpu.VMEM((chunks, 40, L), F32),
         val=pltpu.VMEM((chunks, 40, L), F32),
         code=pltpu.VMEM((chunks, 2, L), F32),
-        x=pltpu.VMEM((chunks, D, L), F32),
-        xh1=pltpu.VMEM((LAYERS, chunks, D, L), F32),
-        r1=pltpu.VMEM((LAYERS, chunks, 1, L), F32),
-        xh2=pltpu.VMEM((LAYERS, chunks, D, L), F32),
-        r2=pltpu.VMEM((LAYERS, chunks, 1, L), F32),
-        n1=pltpu.VMEM((LAYERS, chunks, 128, L), BF),
-        n2=pltpu.VMEM((LAYERS, chunks, 128, L), BF),
-        att=pltpu.VMEM((LAYERS, chunks, 128, L), BF),
-        mix=pltpu.VMEM((LAYERS, chunks, 360, L), F32),
-        prob=pltpu.VMEM((LAYERS, groups, GT, H * 128), F32),
-        pre=pltpu.VMEM((LAYERS, chunks, FF, L), F32),
-        inner=pltpu.VMEM((LAYERS, chunks, 512, L), BF),
+        x=pltpu.VMEM((D, L), F32),
+        xh1=pltpu.VMEM((LAYERS, D, L), F32),
+        r1=pltpu.VMEM((LAYERS, 1, L), F32),
+        xh2=pltpu.VMEM((LAYERS, D, L), F32),
+        r2=pltpu.VMEM((LAYERS, 1, L), F32),
+        n1=pltpu.VMEM((LAYERS, 128, L), BF),
+        n2=pltpu.VMEM((LAYERS, 128, L), BF),
+        att=pltpu.VMEM((LAYERS, 128, L), BF),
+        q_low=pltpu.VMEM((LAYERS, H, 24, L), BF),
+        k_low=pltpu.VMEM((LAYERS, H, 24, L), BF),
+        v_low=pltpu.VMEM((LAYERS, 128, L), BF),
+        rsum=pltpu.VMEM((LAYERS, H, 1, L), F32),
+        prob=pltpu.VMEM((LAYERS, CG, GT, H * 128), F32),
+        prob_low=pltpu.VMEM((LAYERS, CG, 128, H * 128), BF),
+        k_mask=pltpu.VMEM((48, 128), BF),
+        q_mask=pltpu.VMEM((48, 128), BF),
+        dead=pltpu.VMEM((groups, 8, 128), F32),
+        pre=pltpu.VMEM((LAYERS, FF, L), F32),
+        half=pltpu.VMEM((LAYERS, FF, L), F32),
+        inner=pltpu.VMEM((LAYERS, 512, L), BF),
         a_qkv=pltpu.VMEM((LAYERS, 128, 384), F32),
         a_out=pltpu.VMEM((LAYERS, 128, 128), F32),
         a_fc=pltpu.VMEM((LAYERS, 128, 512), F32),
-        a_proj=pltpu.VMEM((LAYERS, 512, 128), F32),
+        a_proj=pltpu.VMEM((LAYERS, 128, 512), F32),
         a_bias=pltpu.VMEM((LAYERS, 12, 128, 128), F32),
         a_obs=pltpu.VMEM((128, 512), F32),
         a_x=pltpu.VMEM((128, 128), F32),
@@ -225,6 +230,16 @@
         second = shifted(load(a + 1), D - s)
         first = jnp.where(lanes < D - s, first, second)
     return jnp.where(lanes < width, first, 0.0)
+
+
+def with_bias(w, bias):
+    if bias is not None:
+        w = jnp.where(iota((128, 128), 0) == D, bias, w)
+    return low(w.T)
+
+
+def ones8(v):
+    return jnp.concatenate([v, jnp.where(iota((8, v.shape[1]), 0) == 0, 1.0, 0.0)], axis=0)
 
 
 def prep_weights(rg, R):
@@ -237,17 +252,17 @@
         for j in range(3):
             w = pad8(rg[pl.ds(b + 2 + j, D, stride=3), :])
             R.qkv[l, :, 128 * j:128 * (j + 1)] = low(w)
-            R.qkv_t[l, 128 * j:128 * (j + 1), :] = low(w.T)
+            R.qkv_t[l, 128 * j:128 * (j + 1), :] = with_bias(w, None if j == 1 else rg[pl.ds(b + 362 + j // 2, 1), :])
         w = pad8(rg[pl.ds(b + 364, D), :])
         R.out[l] = low(w)
-        R.out_t[l] = low(w.T)
+        R.out_t[l] = with_bias(w, rg[pl.ds(b + 484, 1), :])
         for j in range(4):
             w = pad8(rg[pl.ds(b + 487 + j, D, stride=4), :])
             R.fc[l, :, 128 * j:128 * (j + 1)] = low(w)
-            R.fc_t[l, 128 * j:128 * (j + 1), :] = low(w.T)
+            R.fc_t[l, 128 * j:128 * (j + 1), :] = with_bias(w, rg[pl.ds(b + 967 + j, 1), :])
             w = pad8(rg[pl.ds(b + 971 + D * j, D), :])
             R.proj[l, 128 * j:128 * (j + 1), :] = low(w)
-            R.proj_t[l, :, 128 * j:128 * (j + 1)] = low(w.T)
+            R.proj_t[l, :, 128 * j:128 * (j + 1)] = with_bias(w, None if j else rg[pl.ds(b + 1451, 1), :])
         for i, r in enumerate(VROWS):
             R.vec[pl.ds(12 * l + i, 1), :] = rg[pl.ds(b + r, 1), :]
     R.vec[24:26, :] = rg[pl.ds(HEAD, 2), :]
@@ -306,15 +321,16 @@
     z = nn(low(y), low(pick))
     kk = iota((GT, 128), 0)
     alive = jnp.where((kk % CAMS).astype(F32) < z, 1.0, 0.0)
-    q = iota((GT, 128), 1)
-    same = (kk // WIN == q // WIN) & ((kk % WIN) // CAMS <= (q % WIN) // CAMS) & (q < GT)
-    base = jnp.where(same, 0.0, -1e30)
-    for g in range(groups):
-        R.bias[g] = jnp.where(jnp.broadcast_to(alive[:, g:g + 1], (GT, 128)) > 0.5, base, -1e30)
+    steps = WIN // CAMS
+    j, at = iota((48, 128), 0), iota((48, 128), 1)
+    own = (at // WIN == j // steps) & ((at % WIN) // CAMS == j % steps) & (at < GT)
+    R.k_mask[...] = low(jnp.where(own, 1.0, 0.0))
+    may = (at // WIN == j // steps) & ((at % WIN) // CAMS >= j % steps)
+    R.q_mask[...] = low(jnp.where(may | (j >= GW * steps), 0.0, -BIG))
     rows = pad8(alive).T
-    live_count = 0.0
     for g in range(groups):
         R.live[g // CG, :, 128 * (g % CG):128 * (g % CG + 1)] = rows[g:g + 1, :]
+        R.dead[g] = jnp.where(iota((8, 128), 0) == 0, 1.0 - rows[g:g + 1, :], 0.0)
     for name, src in (("code", codes), ("act", actions), ("val", valid)):
         parts = spread_groups(src[...].astype(F32), groups, GT)
         dst = getattr(R, name)
@@ -335,44 +351,137 @@
     return live_total, valid_total
 
 
-def attend(q, k, v, bias):
-    krow = pad8(k).T[0:GT]
-    if PRECISE:
-        kh, kl = hi_lo(krow)
-        qh, ql = hi_lo(head_stack(q))
-        s = nn(jnp.concatenate([kh, kl, kh], axis=1), jnp.concatenate([qh, qh, ql], axis=0))
-    else:
-        s = nn(low(krow), low(head_stack(q)))
-    s = s + jnp.concatenate([bias] * H, axis=1)
-    e = jnp.exp(s - jnp.max(s, axis=0, keepdims=True))
-    p = e * (1.0 / jnp.sum(e, axis=0, keepdims=True))
-    slabs = []
-    vs = slabs_of(v)
-    for h in range(H):
-        ph = pad8(p[:, 128 * h:128 * (h + 1)])
-        if PRECISE:
-            pa, pb = hi_lo(ph)
-            va, vb = hi_lo(vs[h])
-            slabs.append(nn(jnp.concatenate([va, vb, va], axis=1), jnp.concatenate([pa, pa, pb], axis=0)))
-        else:
-            slabs.append(nn(low(vs[h]), low(ph)))
-    return join_slabs(slabs), p
-
-
-def attend_back(do, p, q, k, v):
-    vrow = pad8(v).T[0:GT]
-    dp = nn(low(vrow), low(head_stack(do)))
-    t = p * dp
-    ds = t - p * jnp.sum(t, axis=0, keepdims=True)
-    dq, dk, dv = [], [], []
-    qs, ks, os = slabs_of(q), slabs_of(k), slabs_of(do)
-    for h in range(H):
-        dsh = low(pad8(ds[:, 128 * h:128 * (h + 1)]))
-        ph = low(pad8(p[:, 128 * h:128 * (h + 1)]))
-        dq.append(nn(low(ks[h]), dsh))
-        dk.append(nt(low(qs[h]), dsh))
-        dv.append(nt(low(os[h]), ph))
-    return join_slabs(dq) * SCALE, join_slabs(dk), join_slabs(dv)
+def own_rows(slab, h):
+    rows = iota((8, 128), 0)
+    if h % 2 == 0:
+        return jnp.concatenate([slab[0:16], jnp.where(rows < 4, slab[16:24], 0.0)], axis=0)
+    return jnp.concatenate([jnp.where(rows >= 4, slab[0:8], 0.0), slab[8:24]], axis=0)
+
+
+def split(v):
+    hi = low(v).astype(F32)
+    return hi, v - hi
+
+
+def attend(R, l, c, q, k, v):
+    qh, ql = split(q)
+    kh, kl = split(k)
+    vh, vl = split(v)
+    minus = jnp.where(iota((8, 128), 0) == 0, -BIG, 0.0)
+
+    none = jnp.zeros((128, 128), BF)
+
+    def scores(g, p):
+        at = slice(128 * g, 128 * (g + 1))
+        qs, ks = [], []
+        for h in (2 * p, 2 * p + 1):
+            sl = slice(slab_at(h), slab_at(h) + 24)
+            hi = own_rows(qh[sl, at], h)
+            qd = low(jnp.concatenate([hi, hi, own_rows(ql[sl, at], h), minus], axis=0))
+            kd = low(jnp.concatenate([kh[sl, at], kl[sl, at], kh[sl, at], R.dead[c * CG + g]], axis=0))
+            qs.append(jnp.concatenate([qd, R.q_mask[...]], axis=0))
+            ks.append(jnp.concatenate([kd, R.k_mask[...]], axis=0).T)
+        if PAIR:
+            both = jnp.concatenate([jnp.concatenate([qs[0], none], axis=1),
+                                    jnp.concatenate([none, qs[1]], axis=1)], axis=0)
+            return nn(jnp.concatenate(ks, axis=1), both)[0:GT]
+        return jnp.concatenate([nn(ks[0], qs[0])[0:GT], nn(ks[1], qs[1])[0:GT]], axis=1)
+
+    def soft(g, p, s):
+        at = slice(128 * g, 128 * (g + 1))
+        e = jnp.exp2(s - jnp.max(s, axis=0, keepdims=True))
+        r = 1.0 / jnp.sum(e, axis=0, keepdims=True)
+        e8 = pad8(e)
+        eh = low(e8)
+        el = low(e8 - eh.astype(F32))
+        cols = slice(256 * p, 256 * (p + 1))
+        R.prob[l, g, :, cols] = e
+        R.prob_low[l, g, :, cols] = eh
+        R.rsum[l, 2 * p, :, at] = r[:, 0:128]
+        R.rsum[l, 2 * p + 1, :, at] = r[:, 128:256]
+        return r, eh, el
+
+    def values(g, p, r, eh, el):
+        at = slice(128 * g, 128 * (g + 1))
+        out = []
+        for i in range(2):
+            sl = slice(slab_at(2 * p + i), slab_at(2 * p + i) + 24)
+            cols = slice(128 * i, 128 * (i + 1))
+            vs = low(jnp.concatenate([vh[sl, at], vl[sl, at]], axis=0))
+            o = nn(jnp.concatenate([vs, vs], axis=1), jnp.concatenate([eh[:, cols], el[:, cols]], axis=0))
+            out.append((o[0:24] + o[24:48]) * r[:, cols])
+        return out
+
+    items = [(g, p) for g in range(CG) for p in range(H // 2)]
+    slabs = pipeline(items, scores, soft, values, FAHEAD)
+    slabs = [t for pair in slabs for t in pair]
+    return jnp.concatenate([join_slabs(slabs[H * g:H * (g + 1)]) for g in range(CG)], axis=1)
+
+
+PAIR = True
+FAHEAD = 2
+BAHEAD = 2
+
+
+def pipeline(items, first, second, third, ahead, between=()):
+    n = len(items)
+    a, b, out = {}, {}, []
+    between = list(between)
+    done = 0
+    for t in range(n + ahead):
+        if t < n:
+            a[t] = first(*items[t])
+        m = t - ahead + 1
+        if 0 <= m < n:
+            b[m] = second(*items[m], *(a.pop(m) if isinstance(a[m], tuple) else (a.pop(m),)))
+        m = t - ahead
+        if 0 <= m < n:
+            out.append(third(*items[m], *b.pop(m)))
+        while done < len(between) * (t + 1) // (n + ahead):
+            between[done]()
+            done += 1
+    return out
+
+
+def attend_back(R, l, do, between=()):
+    vrows = [R.v_low[l, :, 128 * g:128 * (g + 1)].T for g in range(CG)]
+
+    def probs(g, p):
+        at = slice(128 * g, 128 * (g + 1))
+        ds, stack = [], []
+        for h in (2 * p, 2 * p + 1):
+            a = slab_at(h)
+            d = own_rows(do[a:a + 24, at], h) * R.rsum[l, h, :, at]
+            parts = ([jnp.zeros((a, 128), F32)] if a else []) + [d] + ([jnp.zeros((104 - a, 128), F32)])
+            ds.append(low(d))
+            stack.append(low(jnp.concatenate(parts, axis=0)))
+        return ds, nn(vrows[g], jnp.concatenate(stack, axis=1))[0:GT]
+
+    def inner(g, p, d, dp):
+        at = slice(128 * g, 128 * (g + 1))
+        e = R.prob[l, g, :, 256 * p:256 * (p + 1)]
+        r = jnp.concatenate([R.rsum[l, 2 * p, :, at], R.rsum[l, 2 * p + 1, :, at]], axis=1)
+        total = jnp.sum(e * dp, axis=0, keepdims=True) * r
+        return d, low(pad8(e * (dp - total)))
+
+    def outer(g, p, d, ds):
+        at = slice(128 * g, 128 * (g + 1))
+        out = []
+        for i in range(2):
+            h = 2 * p + i
+            dsh = ds[:, 128 * i:128 * (i + 1)]
+            out.append((nn(R.k_low[l, h, :, at], dsh), nt(R.q_low[l, h, :, at], dsh),
+                        nt(d[i], R.prob_low[l, g, :, 128 * h:128 * (h + 1)])))
+        return out
+
+    items = [(g, p) for g in range(CG) for p in range(H // 2)]
+    slabs = pipeline(items, probs, inner, outer, BAHEAD, between)
+    slabs = [t for pair in slabs for t in pair]
+    out = []
+    for i in range(3):
+        out.append(jnp.concatenate(
+            [join_slabs([t[i] for t in slabs[H * g:H * (g + 1)]]) for g in range(CG)], axis=1))
+    return out[0] * SCALE, out[1], out[2]
 
 
 def embed(R, obs, c):
@@ -389,40 +498,38 @@
         return tile4(R.bc[l, i])
 
     xh, r = normed(x)
-    R.xh1[l, c] = xh
-    R.r1[l, c] = r
-    n1 = low(pad8(xh * vec(G1) + vec(B1)))
-    R.n1[l, c] = n1
+    R.xh1[l] = xh
+    R.r1[l] = r
+    n1 = low(ones8(xh * vec(G1) + vec(B1)))
+    R.n1[l] = n1
     mix = nn(R.qkv_t[l], n1)
-    q = (mix[0:D] + vec(QB)) * SCALE
+    q = mix[0:D] * SCALE
     k = mix[128:128 + D]
-    v = mix[256:256 + D] + vec(VB)
-    R.mix[l, c, 0:D] = q
-    R.mix[l, c, D:2 * D] = k
-    R.mix[l, c, 2 * D:3 * D] = v
-    parts = []
-    for g in range(CG):
-        at = slice(128 * g, 128 * (g + 1))
-        o, p = attend(q[:, at], k[:, at], v[:, at], R.bias[c * CG + g])
-        R.prob[l, c * CG + g] = p
-        parts.append(o)
-    att = low(pad8(jnp.concatenate(parts, axis=1)))
-    R.att[l, c] = att
-    x1 = x + nn(R.out_t[l], att)[0:D] + vec(OB)
+    v = mix[256:256 + D]
+    for h in range(H):
+        a = slab_at(h)
+        R.q_low[l, h] = low(q[a:a + 24])
+        R.k_low[l, h] = low(k[a:a + 24])
+    R.v_low[l] = low(pad8(v))
+    att = low(ones8(attend(R, l, c, q * LOG2E, k, v)))
+    R.att[l] = att
+    x1 = x + nn(R.out_t[l], att)[0:D]
     xh, r = normed(x1)
-    R.xh2[l, c] = xh
-    R.r2[l, c] = r
-    n2 = low(pad8(xh * vec(G2) + vec(B2)))
-    R.n2[l, c] = n2
+    R.xh2[l] = xh
+    R.r2[l] = r
+    n2 = low(ones8(xh * vec(G2) + vec(B2)))
+    R.n2[l] = n2
     pre = nn(R.fc_t[l], n2)
     parts = []
     for j in range(4):
-        pj = pre[128 * j:128 * j + D] + vec(FB0 + j)
-        R.pre[l, c, D * j:D * (j + 1)] = pj
-        parts.append(low(pad8(gelu(pj))))
+        pj = pre[128 * j:128 * j + D]
+        half = gelu_half(pj)
+        R.pre[l, D * j:D * (j + 1)] = pj
+        R.half[l, D * j:D * (j + 1)] = half
+        parts.append(low(ones8(pj * half) if j == 0 else pad8(pj * half)))
     inner = jnp.concatenate(parts, axis=0)
-    R.inner[l, c] = inner
-    return x1 + nn(R.proj_t[l], inner)[0:D] + vec(PB)
+    R.inner[l] = inner
+    return x1 + nn(R.proj_t[l], inner)[0:D]
 
 
 def head_step(R, c, x, live_total, valid_total):
@@ -470,43 +577,48 @@
         R.a_bias[l, i, 0:D] += fold4(v)
 
     outl = low(pad8(dout))
-    R.a_proj[l] += nt(R.inner[l, c], outl)
     add_bias(PB, dout)
-    di = nn(R.proj[l], outl)
     parts = []
     for j in range(4):
-        pj = di[128 * j:128 * j + D] * gelu_back(R.pre[l, c, D * j:D * (j + 1)])
-        plow = low(pad8(pj))
-        add_bias(FB0 + j, plow.astype(F32)[0:D])
-        parts.append(plow)
+        rows = slice(D * j, D * (j + 1))
+        dj = nn(R.proj[l, 128 * j:128 * (j + 1)], outl)
+        parts.append(low(pad8(dj[0:D] * gelu_slope(R.pre[l, rows], R.half[l, rows]))))
     prel = jnp.concatenate(parts, axis=0)
-    R.a_fc[l] += nt(R.n2[l, c], prel)
     dn = nn(R.fc[l], prel)[0:D]
-    xh = R.xh2[l, c]
+    xh = R.xh2[l]
     add_bias(G2, dn * xh)
     add_bias(B2, dn)
-    dmid = normed_back(dn * vec(G2), xh, R.r2[l, c]) + dout
+    dmid = normed_back(dn * vec(G2), xh, R.r2[l]) + dout
     midl = low(pad8(dmid))
-    R.a_out[l] += nt(R.att[l, c], midl)
     add_bias(OB, dmid)
     da = nn(R.out[l], midl)[0:D]
-    dq, dk, dv = [], [], []
-    for g in range(CG):
-        at = slice(128 * g, 128 * (g + 1))
-        res = attend_back(da[:, at], R.prob[l, c * CG + g], R.mix[l, c, 0:D, at],
-                          R.mix[l, c, D:2 * D, at], R.mix[l, c, 2 * D:3 * D, at])
-        for lst, val in zip((dq, dk, dv), res):
-            lst.append(val)
-    dq, dk, dv = (jnp.concatenate(v, axis=1) for v in (dq, dk, dv))
+    later = []
+
+    def a_proj(j):
+        def run():
+            cols = slice(256 * j, 256 * (j + 1))
+            R.a_proj[l, :, cols] += nt(outl, R.inner[l, cols])
+        return run
+
+    def a_fc(j):
+        def run():
+            cols = slice(256 * j, 256 * (j + 1))
+            R.a_fc[l, :, cols] += nt(R.n2[l], prel[cols])
+        return run
+
+    def a_out():
+        R.a_out[l] += nt(R.att[l], midl)
+
+    dq, dk, dv = attend_back(R, l, da, [a_proj(0), a_proj(1), a_fc(0), a_fc(1), a_out])
+    mixl = jnp.concatenate([low(pad8(dq)), low(pad8(dk)), low(pad8(dv))], axis=0)
+    dn = nn(R.qkv[l], mixl)[0:D]
     add_bias(QB, dq)
     add_bias(VB, dv)
-    mixl = jnp.concatenate([low(pad8(dq)), low(pad8(dk)), low(pad8(dv))], axis=0)
-    R.a_qkv[l] += nt(R.n1[l, c], mixl)
-    dn = nn(R.qkv[l], mixl)[0:D]
-    xh = R.xh1[l, c]
+    R.a_qkv[l] += nt(R.n1[l], mixl)
+    xh = R.xh1[l]
     add_bias(G1, dn * xh)
     add_bias(B1, dn)
-    return normed_back(dn * vec(G1), xh, R.r1[l, c]) + dmid
+    return normed_back(dn * vec(G1), xh, R.r1[l]) + dmid
 
 
 def embed_bwd(R, obs, c, dx):
@@ -538,10 +650,13 @@
     rg[pl.ds(b + 364, D), :] = R.a_out[l, 0:D]
     for j in range(4):
         rg[pl.ds(b + 487 + j, D, stride=4), :] = R.a_fc[l, 0:D, 128 * j:128 * (j + 1)]
-        rg[pl.ds(b + 971 + D * j, D), :] = R.a_proj[l, 128 * j:128 * j + D, :]
+        rg[pl.ds(b + 971 + D * j, D), :] = R.a_proj[l, :, 128 * j:128 * (j + 1)].T[0:D]
     rows = nt(jnp.ones((8, 128), F32), R.a_bias[l].reshape(12 * 128, 128), HIGH)
     for i, r in enumerate(VROWS):
-        rg[pl.ds(b + r, 1), :] = rows[0:1, 128 * i:128 * (i + 1)]
+        if FB0 <= i <= FB3:
+            rg[pl.ds(b + r, 1), :] = R.a_fc[l, D:D + 1, 128 * (i - FB0):128 * (i - FB0 + 1)]
+        else:
+            rg[pl.ds(b + r, 1), :] = rows[0:1, 128 * i:128 * (i + 1)]
 
 
 def pack_embed(R, rg):
@@ -735,19 +850,18 @@
         p1.append(send(blk, blk, R.s_p1, (i,), to_z(i)))
         p1[-1].start()
 
-    own = []
-    others = []
-
-    def start_obs(c):
+    def obs_copies(c):
+        cps = []
         for i in range(1, Fn):
             src = obs.at[pl.ds(pl.multiple_of(z_peer(i) * n + CT * c, 16), CT), :]
-            cp = send(src, R.ob.at[c, feat, pl.ds(0, CT), :], R.s_ob, (c, i), to_z(i))
+            cps.append(send(src, R.ob.at[c, feat, pl.ds(0, CT), :], R.s_ob, (c, i), to_z(i)))
+        src = obs.at[pl.ds(pl.multiple_of(feat * n + CT * c, 16), CT), :]
+        cps.append(pltpu.make_async_copy(src, R.ob.at[c, feat, pl.ds(0, CT), :], R.s_ob.at[0, c, 0]))
+        return cps
+
+    def start_obs(c):
+        for cp in obs_copies(c):
             cp.start()
-            others.append(cp)
-        src = obs.at[pl.ds(pl.multiple_of(feat * n + CT * c, 16), CT), :]
-        cp = pltpu.make_async_copy(src, R.ob.at[c, feat, pl.ds(0, CT), :], R.s_ob.at[0, c, 0])
-        cp.start()
-        own.append(cp)
 
     start_obs(0)
     for cp in ins:
@@ -810,8 +924,6 @@
         blk = R.pg.at[core, c_from(i)]
         p3.append(send(blk, blk, R.s_p3, (i,), sibling))
         p3[-1].start()
-    for c in range(1, P.chunks):
-        start_obs(c)
     wait_all(tc)
     ts = hop_s(0, total(R.tc, 0, C))
     for cp in p2:
@@ -836,45 +948,35 @@
     lax.fori_loop(0, Fn * P.toks, place, 0)
     prep_weights(R.rg, R)
 
-    def fwd(c, _):
-        for i in range(1, Fn):
-            send(R.ob.at[c, feat, pl.ds(0, CT), :], R.ob.at[c, feat, pl.ds(0, CT), :],
-                 R.s_ob, (c, i), to_z(i)).wait_recv()
-        pltpu.make_async_copy(obs.at[pl.ds(0, CT), :], R.ob.at[c, feat, pl.ds(0, CT), :],
-                              R.s_ob.at[0, c, 0]).wait()
-        R.x[c] = embed(R, [R.ob[c, f, 0:CT, :] for f in range(Fn)], c)
+    def chunk(c, _):
+        cps = obs_copies(c)
+        for cp in cps[:-1]:
+            cp.wait_recv()
+        cps[-1].wait()
+
+        @pl.when(c + 1 < P.chunks)
+        def _():
+            start_obs(c + 1)
+
+        R.x[...] = embed(R, [R.ob[c, f, 0:CT, :] for f in range(Fn)], c)
 
         def lay(l, _):
-            R.x[c] = layer_fwd(R, l, c, R.x[c])
+            R.x[...] = layer_fwd(R, l, c, R.x[...])
             return 0
 
         lax.fori_loop(0, LAYERS, lay, 0)
+        R.x[...] = head_step(R, c, R.x[...], live_total, valid_total)
+
+        def back(i, _):
+            R.x[...] = layer_bwd(R, LAYERS - 1 - i, c, R.x[...])
+            return 0
+
+        lax.fori_loop(0, LAYERS, back, 0)
+        embed_bwd(R, [R.ob[c, f] for f in range(Fn)], c, R.x[...])
         return 0
 
-    lax.fori_loop(0, P.chunks, fwd, 0)
-
-    def heads(c, _):
-        R.x[c] = head_step(R, c, R.x[c], live_total, valid_total)
-        return 0
-
-    lax.fori_loop(0, P.chunks, heads, 0)
+    lax.fori_loop(0, P.chunks, chunk, 0)
     lz = hop_z(1, two_rows(jnp.sum(R.loss[0], keepdims=True), jnp.sum(R.loss[1], keepdims=True)))
-
-    def back(i, _):
-        def chunk(c, _):
-            R.x[c] = layer_bwd(R, LAYERS - 1 - i, c, R.x[c])
-            return 0
-
-        lax.fori_loop(0, P.chunks, chunk, 0)
-        return 0
-
-    lax.fori_loop(0, LAYERS, back, 0)
-
-    def last(c, _):
-        embed_bwd(R, [R.ob[c, f] for f in range(Fn)], c, R.x[c])
-        return 0
-
-    lax.fori_loop(0, P.chunks, last, 0)
     wait_all(lz)
     lc = hop_c(1, total(R.tz, 1, Fn))
     R.rg[pl.ds(HEAD + 32, P.grid - HEAD - 32), :] = jnp.zeros((P.grid - HEAD - 32, 128), F32)
@@ -936,7 +1038,10 @@
     wait_all(ls)
     lost = total(R.ts, 1, 2)
     sums[...] = jnp.concatenate([lost[0:1], counted[0:1], lost[1:2], counted[1:2], jnp.zeros((4, 128), F32)], axis=0)
-    for cps in (others, r1, r2, r3):
+    for c in range(P.chunks):
+        for cp in obs_copies(c)[:-1]:
+            cp.wait_send()
+    for cps in (r1, r2, r3):
         for cp in cps:
             cp.wait_send()
 

time: 125 us -> 109 us (0.87)
  Pallas kernels: 115 us -> 99.6 us
    pallas_call x1, Pallas kernels: 115 us -> 99.6 us  [shards(): pl.pallas_call(functools.partial(step_kernel, P_, list(scratch)), out_sha...]
where the time goes in v2:
time: 109 us
  Pallas kernels  99.6 us (91%)
  local copies, waits for them, and re-layouts  8.51 us (8%)
    pallas_call x1, Pallas kernels, shards(): pl.pallas_call(functools.partial(step_kernel, P_, list(scratch)), out_sha...  99.6 us
    unnamed x3, local copies, waits for them, and re-layouts  4.3 us
    reshape x2, local copies, waits for them, and re-layouts, shards(): jnp.pad(v, (0, pad)).reshape(P_.local, 128)  2.91 us

profile of v2, /device:TPU:0, one launch (start us, length us, event | category | flops | bytes accessed | tf_op | source)
XLA Modules:
  0.0 108.7 jit_solution(10877838641487422824)
XLA Ops:
  0.6 1.4 %pad_bitcast_fusion.2.master = f32[104,128]{1,0:T(8,128)} fusion(f32[13192]{0:T(1024)} %param.8), kind=kLoop, calls=%fused_computation.2 | loop fusion | bytes 106016 | tf_op jit(solution)/shard_map/reshape | solution.py:1057
  2.1 1.5 %pad_bitcast_fusion = (f32[104,128]{1,0:T(8,128)}, f32[104,128]{1,0:T(8,128)}) fusion(f32[13192]{0:T(1024)} %param.10, f32[13192]{0:T(1024)} %param.9), kind=kLoop, calls=%fused_computation | loop fusion | bytes 212032 | tf_op jit(solution)/shard_map/reshape | solution.py:1057
  3.5 99.6 %shard_map.111 = (f32[104,128]{1,0:T(8,128)}, f32[104,128]{1,0:T(8,128)}, f32[104,128]{1,0:T(8,128)}, f32[8,128]{1,0:T(8,128)}) custom-call(f32[104,128]{1,0:T(8,128)} %pad_bitcast_fusion.2.master, f32[104,128]{1,0:T(8,128)} %get-tuple-element.13.first, f32[104,128]{1,0:T(8,128)} %get-tuple-element.12.second, bf16[7680,128]{1,0:T(8,128)(2,1)} %obs.1, ...), custom_call_target="tpu_custom_call" | custom-call | tf_op jit(solution)/shard_map/pallas_call | solution.py:1061
  103.1 1.3 %slice_reduce_fusion = f32[4]{0:T(128)} fusion(f32[8,128]{1,0:T(8,128)} %get-tuple-element.11), kind=kLoop, calls=%fused_computation.3 | loop fusion | bytes 32 | tf_op jit(solution)/shard_map/slice | solution.py:1071
  104.4 1.4 %copy.15 = f32[13192]{0:T(1024)} copy(f32[13192]{0:T(1024)} %bitcast.17) | data formatting | bytes 105536
  105.9 1.4 %copy.16 = f32[13192]{0:T(1024)} copy(f32[13192]{0:T(1024)} %bitcast.16) | data formatting | bytes 105536
  107.3 1.4 %copy.17 = f32[13192]{0:T(1024)} copy(f32[13192]{0:T(1024)} %bitcast.15) | data formatting | bytes 105536

commit v3 on v2

--- a/solution.py
+++ b/solution.py
@@ -175,6 +175,8 @@
         val=pltpu.VMEM((chunks, 40, L), F32),
         code=pltpu.VMEM((chunks, 2, L), F32),
         x=pltpu.VMEM((D, L), F32),
+        dmid=pltpu.VMEM((D, L), F32),
+        da=pltpu.VMEM((D, L), F32),
         xh1=pltpu.VMEM((LAYERS, D, L), F32),
         r1=pltpu.VMEM((LAYERS, 1, L), F32),
         xh2=pltpu.VMEM((LAYERS, D, L), F32),
@@ -363,7 +365,7 @@
     return hi, v - hi
 
 
-def attend(R, l, c, q, k, v):
+def attend(R, s, c, q, k, v):
     qh, ql = split(q)
     kh, kl = split(k)
     vh, vl = split(v)
@@ -387,18 +389,18 @@
             return nn(jnp.concatenate(ks, axis=1), both)[0:GT]
         return jnp.concatenate([nn(ks[0], qs[0])[0:GT], nn(ks[1], qs[1])[0:GT]], axis=1)
 
-    def soft(g, p, s):
+    def soft(g, p, sc):
         at = slice(128 * g, 128 * (g + 1))
-        e = jnp.exp2(s - jnp.max(s, axis=0, keepdims=True))
+        e = jnp.exp2(sc - jnp.max(sc, axis=0, keepdims=True))
         r = 1.0 / jnp.sum(e, axis=0, keepdims=True)
         e8 = pad8(e)
         eh = low(e8)
         el = low(e8 - eh.astype(F32))
         cols = slice(256 * p, 256 * (p + 1))
-        R.prob[l, g, :, cols] = e
-        R.prob_low[l, g, :, cols] = eh
-        R.rsum[l, 2 * p, :, at] = r[:, 0:128]
-        R.rsum[l, 2 * p + 1, :, at] = r[:, 128:256]
+        R.prob[s, g, :, cols] = e
+        R.prob_low[s, g, :, cols] = eh
+        R.rsum[s, 2 * p, :, at] = r[:, 0:128]
+        R.rsum[s, 2 * p + 1, :, at] = r[:, 128:256]
         return r, eh, el
 
     def values(g, p, r, eh, el):
@@ -443,15 +445,15 @@
     return out
 
 
-def attend_back(R, l, do, between=()):
-    vrows = [R.v_low[l, :, 128 * g:128 * (g + 1)].T for g in range(CG)]
+def attend_back(R, s, do, between=()):
+    vrows = [R.v_low[s, :, 128 * g:128 * (g + 1)].T for g in range(CG)]
 
     def probs(g, p):
         at = slice(128 * g, 128 * (g + 1))
         ds, stack = [], []
         for h in (2 * p, 2 * p + 1):
             a = slab_at(h)
-            d = own_rows(do[a:a + 24, at], h) * R.rsum[l, h, :, at]
+            d = own_rows(do[a:a + 24, at], h) * R.rsum[s, h, :, at]
             parts = ([jnp.zeros((a, 128), F32)] if a else []) + [d] + ([jnp.zeros((104 - a, 128), F32)])
             ds.append(low(d))
             stack.append(low(jnp.concatenate(parts, axis=0)))
@@ -459,8 +461,8 @@
 
     def inner(g, p, d, dp):
         at = slice(128 * g, 128 * (g + 1))
-        e = R.prob[l, g, :, 256 * p:256 * (p + 1)]
-        r = jnp.concatenate([R.rsum[l, 2 * p, :, at], R.rsum[l, 2 * p + 1, :, at]], axis=1)
+        e = R.prob[s, g, :, 256 * p:256 * (p + 1)]
+        r = jnp.concatenate([R.rsum[s, 2 * p, :, at], R.rsum[s, 2 * p + 1, :, at]], axis=1)
         total = jnp.sum(e * dp, axis=0, keepdims=True) * r
         return d, low(pad8(e * (dp - total)))
 
@@ -470,8 +472,8 @@
         for i in range(2):
             h = 2 * p + i
             dsh = ds[:, 128 * i:128 * (i + 1)]
-            out.append((nn(R.k_low[l, h, :, at], dsh), nt(R.q_low[l, h, :, at], dsh),
-                        nt(d[i], R.prob_low[l, g, :, 128 * h:128 * (h + 1)])))
+            out.append((nn(R.k_low[s, h, :, at], dsh), nt(R.q_low[s, h, :, at], dsh),
+                        nt(d[i], R.prob_low[s, g, :, 128 * h:128 * (h + 1)])))
         return out
 
     items = [(g, p) for g in range(CG) for p in range(H // 2)]
@@ -493,25 +495,25 @@
     return jnp.concatenate(parts, axis=1)
 
 
-def layer_fwd(R, l, c, x):
+def layer_fwd(R, l, c, s, x):
     def vec(i):
         return tile4(R.bc[l, i])
 
     xh, r = normed(x)
-    R.xh1[l] = xh
-    R.r1[l] = r
+    R.xh1[s] = xh
+    R.r1[s] = r
     n1 = low(ones8(xh * vec(G1) + vec(B1)))
-    R.n1[l] = n1
+    R.n1[s] = n1
     mix = nn(R.qkv_t[l], n1)
     q = mix[0:D] * SCALE
     k = mix[128:128 + D]
     v = mix[256:256 + D]
     for h in range(H):
         a = slab_at(h)
-        R.q_low[l, h] = low(q[a:a + 24])
-        R.k_low[l, h] = low(k[a:a + 24])
-    R.v_low[l] = low(pad8(v))
-    att = low(ones8(attend(R, l, c, q * LOG2E, k, v)))
+        R.q_low[s, h] = low(q[a:a + 24])
+        R.k_low[s, h] = low(k[a:a + 24])
+    R.v_low[s] = low(pad8(v))
+    att = low(ones8(attend(R, s, c, q * LOG2E, k, v)))
     R.att[l] = att
     x1 = x + nn(R.out_t[l], att)[0:D]
     xh, r = normed(x1)
@@ -569,15 +571,13 @@
     return normed_back(df * tile4(R.bcf[0]), xh, r)
 
 
-def layer_bwd(R, l, c, dout):
-    def vec(i):
-        return tile4(R.bc[l, i])
-
-    def add_bias(i, v):
-        R.a_bias[l, i, 0:D] += fold4(v)
-
+def add_bias(R, l, i, v):
+    R.a_bias[l, i, 0:D] += fold4(v)
+
+
+def mlp_bwd(R, l, dout):
     outl = low(pad8(dout))
-    add_bias(PB, dout)
+    add_bias(R, l, PB, dout)
     parts = []
     for j in range(4):
         rows = slice(D * j, D * (j + 1))
@@ -586,13 +586,12 @@
     prel = jnp.concatenate(parts, axis=0)
     dn = nn(R.fc[l], prel)[0:D]
     xh = R.xh2[l]
-    add_bias(G2, dn * xh)
-    add_bias(B2, dn)
-    dmid = normed_back(dn * vec(G2), xh, R.r2[l]) + dout
+    add_bias(R, l, G2, dn * xh)
+    add_bias(R, l, B2, dn)
+    dmid = normed_back(dn * tile4(R.bc[l, G2]), xh, R.r2[l]) + dout
     midl = low(pad8(dmid))
-    add_bias(OB, dmid)
+    add_bias(R, l, OB, dmid)
     da = nn(R.out[l], midl)[0:D]
-    later = []
 
     def a_proj(j):
         def run():
@@ -609,16 +608,20 @@
     def a_out():
         R.a_out[l] += nt(R.att[l], midl)
 
-    dq, dk, dv = attend_back(R, l, da, [a_proj(0), a_proj(1), a_fc(0), a_fc(1), a_out])
+    return dmid, da, [a_proj(0), a_proj(1), a_fc(0), a_fc(1), a_out]
+
+
+def att_bwd(R, l, s, dmid, da, between):
+    dq, dk, dv = attend_back(R, s, da, between)
     mixl = jnp.concatenate([low(pad8(dq)), low(pad8(dk)), low(pad8(dv))], axis=0)
     dn = nn(R.qkv[l], mixl)[0:D]
-    add_bias(QB, dq)
-    add_bias(VB, dv)
-    R.a_qkv[l] += nt(R.n1[l], mixl)
-    xh = R.xh1[l]
-    add_bias(G1, dn * xh)
-    add_bias(B1, dn)
-    return normed_back(dn * vec(G1), xh, R.r1[l]) + dmid
+    add_bias(R, l, QB, dq)
+    add_bias(R, l, VB, dv)
+    R.a_qkv[l] += nt(R.n1[s], mixl)
+    xh = R.xh1[s]
+    add_bias(R, l, G1, dn * xh)
+    add_bias(R, l, B1, dn)
+    return normed_back(dn * tile4(R.bc[l, G1]), xh, R.r1[s]) + dmid
 
 
 def embed_bwd(R, obs, c, dx):
@@ -643,20 +646,34 @@
 HIGH = lax.Precision.HIGHEST
 
 
-def pack_layer(R, rg, l):
+LATE = 364
+EARLY_ROWS = (OB, G2, B2, FB0, FB1, FB2, FB3, PB)
+
+
+def pack_vectors(R, rg, l, which):
     b = BASE + LROW * l
-    for j in range(3):
-        rg[pl.ds(b + 2 + j, D, stride=3), :] = R.a_qkv[l, 0:D, 128 * j:128 * (j + 1)]
+    for i in which:
+        if FB0 <= i <= FB3:
+            row = R.a_fc[l, D:D + 1, 128 * (i - FB0):128 * (i - FB0 + 1)]
+        else:
+            row = nt(jnp.ones((8, 128), F32), R.a_bias[l, i], HIGH)[0:1]
+        rg[pl.ds(b + VROWS[i], 1), :] = row
+
+
+def pack_early(R, rg, l):
+    b = BASE + LROW * l
     rg[pl.ds(b + 364, D), :] = R.a_out[l, 0:D]
     for j in range(4):
         rg[pl.ds(b + 487 + j, D, stride=4), :] = R.a_fc[l, 0:D, 128 * j:128 * (j + 1)]
         rg[pl.ds(b + 971 + D * j, D), :] = R.a_proj[l, :, 128 * j:128 * (j + 1)].T[0:D]
-    rows = nt(jnp.ones((8, 128), F32), R.a_bias[l].reshape(12 * 128, 128), HIGH)
-    for i, r in enumerate(VROWS):
-        if FB0 <= i <= FB3:
-            rg[pl.ds(b + r, 1), :] = R.a_fc[l, D:D + 1, 128 * (i - FB0):128 * (i - FB0 + 1)]
-        else:
-            rg[pl.ds(b + r, 1), :] = rows[0:1, 128 * i:128 * (i + 1)]
+    pack_vectors(R, rg, l, EARLY_ROWS)
+
+
+def pack_late(R, rg, l):
+    b = BASE + LROW * l
+    for j in range(3):
+        rg[pl.ds(b + 2 + j, D, stride=3), :] = R.a_qkv[l, 0:D, 128 * j:128 * (j + 1)]
+    pack_vectors(R, rg, l, (G1, B1, QB, VB))
 
 
 def pack_embed(R, rg):
@@ -722,10 +739,11 @@
         self.shard = shard
         self.block = round_up(-(-(shard + 112) // D), 16)
         self.flat_rows = self.block // 16 * 15
-        self.local = round_up(-(-shard // 128), 8)
+        self.local = round_up(-(-shard // 1024), 1) * 8
         self.work = round_up(max(self.flat_rows, self.local + 1), 8)
         self.own_rows = tok_rows // feats
         self.chunks = self.own_rows // CT
+        self.early = [f for f in range(feats) if shard * toks * f // D >= BASE + LATE]
         self.grid = round_up(-(-(shard * feats * toks) // D) + self.block, 8)
 
 
@@ -746,15 +764,17 @@
         ts=pltpu.VMEM((2, 2, 8, 128), F32),
         sb1=pltpu.VMEM((C, Fn, B, 128), F32),
         rb1=pltpu.VMEM((C, Fn, B, 128), F32),
-        sb2=pltpu.VMEM((C, Fn, B, 128), F32),
-        rb2=pltpu.VMEM((C, Fn, B, 128), F32),
+        sb2=pltpu.VMEM((C, Fn, B, 128), BF),
+        rb2=pltpu.VMEM((C, Fn, B, 128), BF),
+        col=pltpu.VMEM((Fn, B, 128), F32),
         sb3=pltpu.VMEM((Fn, B, 128), F32),
         rb3=pltpu.VMEM((Fn, B, 128), F32),
         s_p1=dma((2, Fn)), s_p2=dma((2, C)), s_p3=dma((2, C)),
         s_tz=dma((2, 2, Fn)), s_tc=dma((2, 2, C)), s_ts=dma((2, 2)),
-        s_ob=dma((2, P.chunks, Fn)),
+        s_ob=dma((2, 2 * P.chunks, Fn)),
+        s_own=dma((P.chunks,)),
         s_in=dma((3,)),
-        s_r1=dma((2, C)), s_r2=dma((2, C)), s_r3=dma((2, Fn)),
+        s_r1=dma((2, 2, C)), s_r2=dma((2, Fn, C)), s_r3=dma((2, Fn)),
     )
 
 
@@ -789,8 +809,7 @@
     return v[0:P.local]
 
 
-def step_kernel(P, names, master, first, second, obs, counts, codes, actions, valid,
-                new_master, new_first, new_second, sums, *scratch):
+def step_kernel(P, names, master, obs, counts, codes, actions, valid, grad, sums, *scratch):
     R = Refs()
     for name, ref in zip(names, scratch):
         setattr(R, name, ref)
@@ -839,7 +858,11 @@
         pl.semaphore_signal(barrier, inc=1, device_id=dev, device_id_type=MESH)
 
     R.loc[...] = jnp.zeros(R.loc.shape, F32)
-    R.loc[0:P.local, :] = master[...]
+    whole = P.shard // 1024
+    R.loc[0:8 * whole, :] = master[pl.ds(0, 1024 * whole)].reshape(8 * whole, 128)
+    rest = P.shard - 1024 * whole
+    last = jnp.concatenate([master[pl.ds(1024 * whole, rest)], jnp.zeros((1024 - rest,), F32)])
+    R.loc[8 * whole:8 * whole + 8, :] = last.reshape(8, 128)
     to_rows(R.loc, R.rblk, delta, P)
     R.pg[core, chip, feat] = low(R.rblk[...])
     pl.semaphore_wait(barrier, len(peers))
@@ -850,20 +873,27 @@
         p1.append(send(blk, blk, R.s_p1, (i,), to_z(i)))
         p1[-1].start()
 
-    def obs_copies(c):
+    half = CT // 2
+
+    def obs_copies(p):
         cps = []
         for i in range(1, Fn):
-            src = obs.at[pl.ds(pl.multiple_of(z_peer(i) * n + CT * c, 16), CT), :]
-            cps.append(send(src, R.ob.at[c, feat, pl.ds(0, CT), :], R.s_ob, (c, i), to_z(i)))
+            src = obs.at[pl.ds(pl.multiple_of(z_peer(i) * n + half * p, 16), half), :]
+            dst = R.ob.at[p // 2, feat, pl.ds(pl.multiple_of(half * (p % 2), 16), half), :]
+            cps.append(send(src, dst, R.s_ob, (p, i), to_z(i)))
+        return cps
+
+    def start_obs(p):
+        for cp in obs_copies(p):
+            cp.start()
+
+    own = []
+    for c in range(P.chunks):
         src = obs.at[pl.ds(pl.multiple_of(feat * n + CT * c, 16), CT), :]
-        cps.append(pltpu.make_async_copy(src, R.ob.at[c, feat, pl.ds(0, CT), :], R.s_ob.at[0, c, 0]))
-        return cps
-
-    def start_obs(c):
-        for cp in obs_copies(c):
-            cp.start()
-
+        own.append(pltpu.make_async_copy(src, R.ob.at[c, feat, pl.ds(0, CT), :], R.s_own.at[c]))
+        own[-1].start()
     start_obs(0)
+    start_obs(1)
     for cp in ins:
         cp.wait()
     zero_grads(R)
@@ -876,27 +906,18 @@
         return jnp.concatenate([jnp.broadcast_to(a, (1, 128)), jnp.broadcast_to(b, (1, 128)),
                                 jnp.zeros((6, 128), F32)], axis=0)
 
-    def hop_z(w, value):
-        R.tz[w, feat] = value
-        cps = []
-        for i in range(1, Fn):
-            cps.append(send(R.tz.at[w, feat], R.tz.at[w, feat], R.s_tz.at[w], (i,), to_z(i)))
-            cps[-1].start()
-        return cps
-
-    def hop_c(w, value):
-        R.tc[w, chip] = value
-        cps = []
-        for i in range(1, C):
-            cps.append(send(R.tc.at[w, chip], R.tc.at[w, chip], R.s_tc.at[w], (i,), to_c(i)))
-            cps[-1].start()
-        return cps
-
-    def hop_s(w, value):
-        R.ts[w, core] = value
-        cp = send(R.ts.at[w, core], R.ts.at[w, core], R.s_ts.at[w], (), sibling)
-        cp.start()
-        return [cp]
+    def z_copies(w):
+        return [send(R.tz.at[w, feat], R.tz.at[w, feat], R.s_tz.at[w], (i,), to_z(i)) for i in range(1, Fn)]
+
+    def c_copies(w):
+        return [send(R.tc.at[w, chip], R.tc.at[w, chip], R.s_tc.at[w], (i,), to_c(i)) for i in range(1, C)]
+
+    def s_copies(w):
+        return [send(R.ts.at[w, core], R.ts.at[w, core], R.s_ts.at[w], (), sibling)]
+
+    def start_all(cps):
+        for cp in cps:
+            cp.start()
 
     def total(ref, w, count):
         v = ref[w, 0]
@@ -908,8 +929,10 @@
         for cp in cps:
             cp.wait()
 
-    tz = hop_z(0, two_rows(live_n, valid_n))
+    R.tz[0, feat] = two_rows(live_n, valid_n)
+    start_all(z_copies(0))
     wait_all(p1)
+    start_obs(2)
     p2 = []
     for i in range(1, C):
         blk = R.pg.at[core, chip]
@@ -917,23 +940,21 @@
         p2[-1].start()
     p3 = [send(R.pg.at[core, chip], R.pg.at[core, chip], R.s_p3, (0,), sibling)]
     p3[0].start()
-    wait_all(tz)
-    tc = hop_c(0, total(R.tz, 0, Fn))
+    wait_all(z_copies(0))
+    R.tc[0, chip] = total(R.tz, 0, Fn)
+    start_all(c_copies(0))
     for i in range(1, C):
         p2[i - 1].wait_recv()
         blk = R.pg.at[core, c_from(i)]
         p3.append(send(blk, blk, R.s_p3, (i,), sibling))
         p3[-1].start()
-    wait_all(tc)
-    ts = hop_s(0, total(R.tc, 0, C))
+    start_obs(3)
+    wait_all(c_copies(0))
+    R.ts[0, core] = total(R.tc, 0, C)
+    start_all(s_copies(0))
     for cp in p2:
         cp.wait_send()
     wait_all(p3)
-    wait_all(ts)
-    counted = total(R.ts, 0, 2)
-    live_total = counted[0:1, 0:1]
-    valid_total = counted[1:2, 0:1]
-
     R.rg[0:8, :] = jnp.zeros((8, 128), F32)
 
     def place(d, _):
@@ -947,103 +968,146 @@
 
     lax.fori_loop(0, Fn * P.toks, place, 0)
     prep_weights(R.rg, R)
-
-    def chunk(c, _):
-        cps = obs_copies(c)
-        for cp in cps[:-1]:
-            cp.wait_recv()
-        cps[-1].wait()
-
-        @pl.when(c + 1 < P.chunks)
-        def _():
-            start_obs(c + 1)
-
-        R.x[...] = embed(R, [R.ob[c, f, 0:CT, :] for f in range(Fn)], c)
-
-        def lay(l, _):
-            R.x[...] = layer_fwd(R, l, c, R.x[...])
-            return 0
-
-        lax.fori_loop(0, LAYERS, lay, 0)
-        R.x[...] = head_step(R, c, R.x[...], live_total, valid_total)
-
-        def back(i, _):
-            R.x[...] = layer_bwd(R, LAYERS - 1 - i, c, R.x[...])
-            return 0
-
-        lax.fori_loop(0, LAYERS, back, 0)
-        embed_bwd(R, [R.ob[c, f] for f in range(Fn)], c, R.x[...])
-        return 0
-
-    lax.fori_loop(0, P.chunks, chunk, 0)
-    lz = hop_z(1, two_rows(jnp.sum(R.loss[0], keepdims=True), jnp.sum(R.loss[1], keepdims=True)))
-    wait_all(lz)
-    lc = hop_c(1, total(R.tz, 1, Fn))
-    R.rg[pl.ds(HEAD + 32, P.grid - HEAD - 32), :] = jnp.zeros((P.grid - HEAD - 32, 128), F32)
-    for l in range(LAYERS):
-        pack_layer(R, R.rg, l)
-    pack_embed(R, R.rg)
-    pack_head(R, R.rg)
+    wait_all(s_copies(0))
+    counted = total(R.ts, 0, 2)
+    live_total = counted[0:1, 0:1]
+    valid_total = counted[1:2, 0:1]
+
+    for cp in own:
+        cp.wait()
+
 
     def rows_of(f, ch, co):
         return (P.shard * (f * P.toks + 2 * ch + co)) // D
 
-    r1 = []
-    for i in range(1, C + 1):
-        ch = c_peer(i)
-        for f in range(Fn):
-            R.sb1[i - 1, f] = R.rg[pl.ds(rows_of(f, ch, 1 - core), B), :]
-        r1.append(send(R.sb1.at[i - 1], R.rb1.at[i - 1], R.s_r1, (i - 1,), sibling))
-        r1[-1].start()
-    wait_all(lc)
-    ls = hop_s(1, total(R.tc, 1, C))
-    r2 = []
-    for i in range(1, C):
-        ch = c_peer(i)
-        r1[i - 1].wait_recv()
-        for f in range(Fn):
-            R.sb2[i, f] = R.rg[pl.ds(rows_of(f, ch, core), B), :] + R.rb1[i - 1, f]
-        r2.append(send(R.sb2.at[i], R.rb2.at[i], R.s_r2, (i,), to_c(i)))
-        r2[-1].start()
-    r1[C - 1].wait_recv()
-    for f in range(Fn):
-        R.sb2[0, f] = R.rg[pl.ds(rows_of(f, chip, core), B), :] + R.rb1[C - 1, f]
-    for cp in r2:
-        cp.wait_recv()
-    r3 = []
+    early = P.early[0] if P.early else Fn
+    planes = [slice(early, Fn), slice(0, early)]
+
+    def r1_copy(w, i):
+        at = pl.ds(planes[w].start, planes[w].stop - planes[w].start)
+        return send(R.sb1.at[i, at], R.rb1.at[i, at], R.s_r1.at[w], (i,), sibling)
+
+    def r2_copy(f, i):
+        return send(R.sb2.at[i, f], R.rb2.at[i, f], R.s_r2.at[:, f], (i,), to_c(i))
+
+    def r3_copy(i):
+        return send(R.sb3.at[i], R.rb3.at[i], R.s_r3, (i,), to_z(i))
+
+    order = list(range(1, C)) + [0]
+
+    def sum_cores(w):
+        for i in order:
+            for f in range(planes[w].start, planes[w].stop):
+                R.sb1[i, f] = R.rg[pl.ds(rows_of(f, c_peer(i), 1 - core), B), :]
+            r1_copy(w, i).start()
+
+    def sum_chips(w):
+        for i in order:
+            r1_copy(w, i).wait_recv()
+            for f in reversed(range(planes[w].start, planes[w].stop)):
+                v = R.rg[pl.ds(rows_of(f, c_peer(i), core), B), :] + R.rb1[i, f]
+                if i:
+                    R.sb2[i, f] = low(v)
+                    r2_copy(f, i).start()
+                else:
+                    R.col[f] = v
+
+    def sum_column(f):
+        v = R.col[f]
+        for i in range(1, C):
+            r2_copy(f, i).wait_recv()
+            v = v + R.rb2[i, f].astype(F32)
+        R.col[f] = v
+        for i in range(1, Fn):
+            @pl.when(z_peer(i) == f)
+            def _():
+                R.sb3[i] = v
+                r3_copy(i).start()
+
+    def chunk(c, _):
+        for p in (2 * c, 2 * c + 1):
+            for cp in obs_copies(p):
+                cp.wait_recv()
+
+        @pl.when(2 * c + 4 < 2 * P.chunks)
+        def _():
+            start_obs(2 * c + 4)
+
+        R.x[...] = embed(R, [R.ob[c, f, 0:CT, :] for f in range(Fn)], c)
+
+        def lay(l, _):
+            R.x[...] = layer_fwd(R, l, c, l, R.x[...])
+            return 0
+
+        lax.fori_loop(0, LAYERS, lay, 0)
+
+        @pl.when(2 * c + 5 < 2 * P.chunks)
+        def _():
+            start_obs(2 * c + 5)
+
+        dx = head_step(R, c, R.x[...], live_total, valid_total)
+        dmid, da, rest = mlp_bwd(R, 1, dx)
+        R.x[...] = att_bwd(R, 1, 1, dmid, da, rest)
+        dmid, da, rest = mlp_bwd(R, 0, R.x[...])
+        R.dmid[...] = dmid
+        R.da[...] = da
+        for run in rest:
+            run()
+
+        @pl.when(c == P.chunks - 1)
+        def _():
+            R.rg[pl.ds(HEAD + 32, P.grid - HEAD - 32), :] = jnp.zeros((P.grid - HEAD - 32, 128), F32)
+            pack_head(R, R.rg)
+            pack_late(R, R.rg, 1)
+            for l in range(LAYERS):
+                pack_early(R, R.rg, l)
+            R.ts[1, core] = two_rows(jnp.sum(R.loss[0], keepdims=True), jnp.sum(R.loss[1], keepdims=True))
+            start_all(s_copies(1))
+            sum_cores(0)
+
+        dx = att_bwd(R, 0, 0, R.dmid[...], R.da[...], [])
+
+        @pl.when(c == P.chunks - 1)
+        def _():
+            sum_chips(0)
+            wait_all(s_copies(1))
+            R.tc[1, chip] = total(R.ts, 1, 2)
+            start_all(c_copies(1))
+
+        embed_bwd(R, [R.ob[c, f] for f in range(Fn)], c, dx)
+        return 0
+
+    lax.fori_loop(0, P.chunks, chunk, 0)
+    pack_embed(R, R.rg)
+    pack_late(R, R.rg, 0)
+    sum_cores(1)
+    sum_chips(1)
+    wait_all(c_copies(1))
+    R.tz[1, feat] = total(R.tc, 1, C)
+    start_all(z_copies(1))
+    for f in reversed(range(Fn)):
+        sum_column(f)
     for i in range(1, Fn):
-        f = z_peer(i)
-        v = R.sb2[0, f]
-        for j in range(1, C):
-            v = v + R.rb2[j, f]
-        R.sb3[i] = v
-        r3.append(send(R.sb3.at[i], R.rb3.at[i], R.s_r3, (i,), to_z(i)))
-        r3[-1].start()
-    v = R.sb2[0, feat]
-    for j in range(1, C):
-        v = v + R.rb2[j, feat]
+        r3_copy(i).wait_recv()
+    v = R.col[feat]
     for i in range(1, Fn):
-        r3[i - 1].wait_recv()
         v = v + R.rb3[i]
     R.rblk[...] = v
-    grad = from_rows(R.rblk, R.loc, delta, P)
-    f_new = BETA_ONE * first[...] + (1.0 - BETA_ONE) * grad
-    s_new = BETA_TWO * second[...] + (1.0 - BETA_TWO) * grad * grad
-    f_hat = f_new / (1.0 - BETA_ONE ** STEP_NO)
-    s_hat = s_new / (1.0 - BETA_TWO ** STEP_NO)
-    old = master[...]
-    new_first[...] = f_new
-    new_second[...] = s_new
-    new_master[...] = old - LEARN_RATE * (f_hat / (jnp.sqrt(s_hat) + ADAM_EPS) + DECAY_RATE * old)
-    wait_all(ls)
-    lost = total(R.ts, 1, 2)
+    grad[...] = from_rows(R.rblk, R.loc, delta, P)
+    wait_all(z_copies(1))
+    lost = total(R.tz, 1, Fn)
     sums[...] = jnp.concatenate([lost[0:1], counted[0:1], lost[1:2], counted[1:2], jnp.zeros((4, 128), F32)], axis=0)
-    for c in range(P.chunks):
-        for cp in obs_copies(c)[:-1]:
+    for p in range(2 * P.chunks):
+        for cp in obs_copies(p):
             cp.wait_send()
-    for cps in (r1, r2, r3):
-        for cp in cps:
-            cp.wait_send()
+    for w in range(2):
+        for i in range(C):
+            r1_copy(w, i).wait_send()
+    for i in range(1, C):
+        for f in range(Fn):
+            r2_copy(f, i).wait_send()
+    for i in range(1, Fn):
+        r3_copy(i).wait_send()
 
 
 def solution(mesh):
@@ -1053,22 +1117,24 @@
         P_ = Plan(feats, toks, master.shape[0], obs.shape[0])
         scratch = dict(scratch_list(P_.chunks))
         scratch.update(comm_scratch(P_))
-        pad = P_.local * 128 - P_.shard
-        flat = [jnp.pad(v, (0, pad)).reshape(P_.local, 128) for v in (master, first, second)]
         vmem = pl.BlockSpec(memory_space=pltpu.VMEM)
         hbm = pl.BlockSpec(memory_space=pl.ANY)
-        out = jax.ShapeDtypeStruct((P_.local, 128), F32)
-        outs = pl.pallas_call(
+        grad, sums = pl.pallas_call(
             functools.partial(step_kernel, P_, list(scratch)),
-            out_shape=(out, out, out, jax.ShapeDtypeStruct((8, 128), F32)),
-            in_specs=[vmem, vmem, vmem, hbm, vmem, hbm, hbm, hbm],
-            out_specs=(vmem,) * 4,
+            out_shape=(jax.ShapeDtypeStruct((P_.local, 128), F32), jax.ShapeDtypeStruct((8, 128), F32)),
+            in_specs=[vmem, hbm, vmem, hbm, hbm, hbm],
+            out_specs=(vmem, vmem),
             scratch_shapes=list(scratch.values()),
             compiler_params=pltpu.CompilerParams(
                 collective_id=0, has_side_effects=True, vmem_limit_bytes=60 * 2 ** 20),
-        )(*flat, obs, counts.T, codes.T, actions, valid)
-        cut = [v.reshape(-1)[:P_.shard] for v in outs[:3]]
-        return (*cut, outs[3][0:4, 0])
+        )(master, obs, counts.T, codes.T, actions, valid)
+        grad = grad.reshape(-1)[:P_.shard]
+        f_new = BETA_ONE * first + (1.0 - BETA_ONE) * grad
+        s_new = BETA_TWO * second + (1.0 - BETA_TWO) * grad * grad
+        f_hat = f_new / (1.0 - BETA_ONE ** STEP_NO)
+        s_hat = s_new / (1.0 - BETA_TWO ** STEP_NO)
+        new = master - LEARN_RATE * (f_hat / (jnp.sqrt(s_hat) + ADAM_EPS) + DECAY_RATE * master)
+        return new, f_new, s_new, sums[0:4, 0]
 
     weights = PSpec(("feat", "tok"))
     return jax.shard_map(

time: 109 us -> 92.4 us (0.85)
  Pallas kernels: 99.6 us -> 88.6 us
  local copies, waits for them, and re-layouts: 8.51 us -> 1.32 us
  other arithmetic: 0 us -> 1.49 us
    pallas_call x1, Pallas kernels: 99.6 us -> 88.6 us  [shards(): pl.pallas_call(functools.partial(step_kernel, P_, list(scratch)), out_sha...]
    unnamed x3 -> x6, local copies, waits for them, and re-layouts: 4.3 us -> 0.01 us
    reshape x2 -> x0, local copies, waits for them, and re-layouts: 2.91 us -> none  [shards(): jnp.pad(v, (0, pad)).reshape(P_.local, 128)]
    sub x0 -> x1, other arithmetic: none -> 1.49 us  [shards(): master - LEARN_RATE * (f_hat / (jnp.sqrt(s_hat) + ADAM_EPS) + DECAY_RATE...]
where the time goes in v3:
time: 92.4 us; the launch traced here: 92.1 us
  Pallas kernels  88.6 us (96%)
  other arithmetic  1.49 us (2%)
  local copies, waits for them, and re-layouts  1.32 us (1%)
    pallas_call x1, Pallas kernels, shards(): pl.pallas_call(functools.partial(step_kernel, P_, list(scratch)), out_sha...  88.6 us

profile of v3, /device:TPU:0, one launch (start us, length us, event | category | flops | bytes accessed | tf_op | source)
XLA Modules:
  0.0 92.1 jit_solution(11418805732772007902)
XLA Ops:
  0.6 0.0 copy-start
  0.6 0.0 copy-start.1
  0.7 0.0 copy-start.2
  0.7 88.6 %shard_map.111 = (f32[104,128]{1,0:T(8,128)}, f32[8,128]{1,0:T(8,128)}) custom-call(f32[13192]{0:T(1024)} %master.1, bf16[7680,128]{1,0:T(8,128)(2,1)} %obs.1, s32[10,256]{1,0:T(8,128)} %bitcast.5, s32[2,7680]{1,0:T(2,128)} %bitcast.3, f32[35,7680]{1,0:T(8,128)} %actions.1, s32[35,7680]{1,0:T(8,128)} %valid.1), custom_call_target="tpu_custom_call" | custom-call | tf_op jit(solution)/shard_map/pallas_call | solution.py:1122
  89.3 1.3 %slice_reduce_fusion = f32[4]{0:T(128)} fusion(f32[8,128]{1,0:T(8,128)} %get-tuple-element.7), kind=kLoop, calls=%fused_computation.4 | loop fusion | bytes 32 | tf_op jit(solution)/shard_map/slice | solution.py:1137
  90.6 0.0 copy-done
  90.6 0.0 copy-done.1
  90.6 0.0 copy-done.2
  90.6 1.5 %multiply_subtract_fusion = (f32[13192]{0:T(1024)}, f32[13192]{0:T(1024)}, f32[13192]{0:T(1024)}) fusion(f32[13192]{0:T(1024)S(1)} %copy-done, f32[13312]{0:T(1024)} %bitcast.4, f32[13192]{0:T(1024)S(1)} %copy-done.1, f32[13192]{0:T(1024)S(1)} %copy-done.2), kind=kLoop, calls=%fused_computation.2 | loop fusion | flops 197880 | bytes 369376 | tf_op jit(solution)/shard_map/sub | solution.py:1136
Async XLA Ops:
  0.6 90.0 %copy-start = (f32[13192]{0:T(1024)S(1)}, f32[13192]{0:T(1024)}, u32[]{:S(2)}) copy-start(f32[13192]{0:T(1024)} %master.1) | copy-start | bytes 158308
  0.6 90.0 %copy-start.1 = (f32[13192]{0:T(1024)S(1)}, f32[13192]{0:T(1024)}, u32[]{:S(2)}) copy-start(f32[13192]{0:T(1024)} %param.9) | copy-start | bytes 158308
  0.7 90.0 %copy-start.2 = (f32[13192]{0:T(1024)S(1)}, f32[13192]{0:T(1024)}, u32[]{:S(2)}) copy-start(f32[13192]{0:T(1024)} %param.10) | copy-start | bytes 158308

commit v4 on v3

--- a/solution.py
+++ b/solution.py
@@ -196,10 +196,12 @@
         pre=pltpu.VMEM((LAYERS, FF, L), F32),
         half=pltpu.VMEM((LAYERS, FF, L), F32),
         inner=pltpu.VMEM((LAYERS, 512, L), BF),
-        a_qkv=pltpu.VMEM((LAYERS, 128, 384), F32),
+        a_qkv=pltpu.VMEM((LAYERS, 384, 128), F32),
+        ds_t=pltpu.VMEM((CG * H // 2, 128, 256), BF),
+        turned=pltpu.VMEM((5, L, 128), BF),
         a_out=pltpu.VMEM((LAYERS, 128, 128), F32),
-        a_fc=pltpu.VMEM((LAYERS, 128, 512), F32),
-        a_proj=pltpu.VMEM((LAYERS, 128, 512), F32),
+        a_fc=pltpu.VMEM((LAYERS, 512, 128), F32),
+        a_proj=pltpu.VMEM((LAYERS, 512, 128), F32),
         a_bias=pltpu.VMEM((LAYERS, 12, 128, 128), F32),
         a_obs=pltpu.VMEM((128, 512), F32),
         a_x=pltpu.VMEM((128, 128), F32),
@@ -398,7 +400,9 @@
         el = low(e8 - eh.astype(F32))
         cols = slice(256 * p, 256 * (p + 1))
         R.prob[s, g, :, cols] = e
-        R.prob_low[s, g, :, cols] = eh
+        for i in range(2):
+            at_h = slice(256 * p + 128 * i, 256 * p + 128 * (i + 1))
+            R.prob_low[s, g, :, at_h] = eh[:, 128 * i:128 * (i + 1)].T
         R.rsum[s, 2 * p, :, at] = r[:, 0:128]
         R.rsum[s, 2 * p + 1, :, at] = r[:, 128:256]
         return r, eh, el
@@ -464,7 +468,11 @@
         e = R.prob[s, g, :, 256 * p:256 * (p + 1)]
         r = jnp.concatenate([R.rsum[s, 2 * p, :, at], R.rsum[s, 2 * p + 1, :, at]], axis=1)
         total = jnp.sum(e * dp, axis=0, keepdims=True) * r
-        return d, low(pad8(e * (dp - total)))
+        ds = low(pad8(e * (dp - total)))
+        for i in range(2):
+            cols = slice(128 * i, 128 * (i + 1))
+            R.ds_t[3 * g + p, :, cols] = ds[:, cols].T
+        return d, ds
 
     def outer(g, p, d, ds):
         at = slice(128 * g, 128 * (g + 1))
@@ -472,8 +480,8 @@
         for i in range(2):
             h = 2 * p + i
             dsh = ds[:, 128 * i:128 * (i + 1)]
-            out.append((nn(R.k_low[s, h, :, at], dsh), nt(R.q_low[s, h, :, at], dsh),
-                        nt(d[i], R.prob_low[s, g, :, 128 * h:128 * (h + 1)])))
+            out.append((nn(R.k_low[s, h, :, at], dsh), nn(R.q_low[s, h, :, at], R.ds_t[3 * g + p, :, 128 * i:128 * (i + 1)]),
+                        nn(d[i], R.prob_low[s, g, :, 128 * h:128 * (h + 1)])))
         return out
 
     items = [(g, p) for g in range(CG) for p in range(H // 2)]
@@ -484,6 +492,11 @@
         out.append(jnp.concatenate(
             [join_slabs([t[i] for t in slabs[H * g:H * (g + 1)]]) for g in range(CG)], axis=1))
     return out[0] * SCALE, out[1], out[2]
+
+
+def turn(R, i, v):
+    for g in range(CG):
+        R.turned[i, 128 * g:128 * (g + 1), :] = v[:, 128 * g:128 * (g + 1)].T
 
 
 def embed(R, obs, c):
@@ -564,7 +577,8 @@
     dh = jnp.concatenate(grads, axis=0)
     R.a_hb[0:72] += fold4(dh)
     dhl = low(jnp.concatenate([dh, jnp.zeros((56, L), F32)], axis=0))
-    R.a_head[...] += nt(fin, dhl)
+    turn(R, 4, dhl)
+    R.a_head[...] += nn(fin, R.turned[4])
     df = nn(R.head[...], dhl)[0:D]
     R.a_fin[0, 0:D] += fold4(df * xh)
     R.a_fin[1, 0:D] += fold4(df)
@@ -593,31 +607,36 @@
     add_bias(R, l, OB, dmid)
     da = nn(R.out[l], midl)[0:D]
 
+    turn(R, 0, outl)
+    turn(R, 1, R.n2[l])
+    turn(R, 2, midl)
+
     def a_proj(j):
         def run():
-            cols = slice(256 * j, 256 * (j + 1))
-            R.a_proj[l, :, cols] += nt(outl, R.inner[l, cols])
+            rows = slice(256 * j, 256 * (j + 1))
+            R.a_proj[l, rows] += nn(R.inner[l, rows], R.turned[0])
         return run
 
     def a_fc(j):
         def run():
-            cols = slice(256 * j, 256 * (j + 1))
-            R.a_fc[l, :, cols] += nt(R.n2[l], prel[cols])
+            rows = slice(256 * j, 256 * (j + 1))
+            R.a_fc[l, rows] += nn(prel[rows], R.turned[1])
         return run
 
     def a_out():
-        R.a_out[l] += nt(R.att[l], midl)
+        R.a_out[l] += nn(R.att[l], R.turned[2])
 
     return dmid, da, [a_proj(0), a_proj(1), a_fc(0), a_fc(1), a_out]
 
 
 def att_bwd(R, l, s, dmid, da, between):
+    turn(R, 3, R.n1[s])
     dq, dk, dv = attend_back(R, s, da, between)
     mixl = jnp.concatenate([low(pad8(dq)), low(pad8(dk)), low(pad8(dv))], axis=0)
     dn = nn(R.qkv[l], mixl)[0:D]
     add_bias(R, l, QB, dq)
     add_bias(R, l, VB, dv)
-    R.a_qkv[l] += nt(R.n1[s], mixl)
+    R.a_qkv[l] += nn(mixl, R.turned[3])
     xh = R.xh1[s]
     add_bias(R, l, G1, dn * xh)
     add_bias(R, l, B1, dn)
@@ -647,32 +666,34 @@
 
 
 LATE = 364
-EARLY_ROWS = (OB, G2, B2, FB0, FB1, FB2, FB3, PB)
+EARLY_ROWS = (OB, G2, B2, PB)
+
+
+def lane_sums(v):
+    return jnp.sum(v.T, axis=0, keepdims=True)
 
 
 def pack_vectors(R, rg, l, which):
     b = BASE + LROW * l
     for i in which:
-        if FB0 <= i <= FB3:
-            row = R.a_fc[l, D:D + 1, 128 * (i - FB0):128 * (i - FB0 + 1)]
-        else:
-            row = nt(jnp.ones((8, 128), F32), R.a_bias[l, i], HIGH)[0:1]
-        rg[pl.ds(b + VROWS[i], 1), :] = row
+        rg[pl.ds(b + VROWS[i], 1), :] = lane_sums(R.a_bias[l, i])
 
 
 def pack_early(R, rg, l):
     b = BASE + LROW * l
     rg[pl.ds(b + 364, D), :] = R.a_out[l, 0:D]
     for j in range(4):
-        rg[pl.ds(b + 487 + j, D, stride=4), :] = R.a_fc[l, 0:D, 128 * j:128 * (j + 1)]
-        rg[pl.ds(b + 971 + D * j, D), :] = R.a_proj[l, :, 128 * j:128 * (j + 1)].T[0:D]
+        fc = R.a_fc[l, 128 * j:128 * (j + 1), :].T
+        rg[pl.ds(b + 487 + j, D, stride=4), :] = fc[0:D]
+        rg[pl.ds(b + 967 + j, 1), :] = fc[D:D + 1]
+        rg[pl.ds(b + 971 + D * j, D), :] = R.a_proj[l, 128 * j:128 * j + D, :]
     pack_vectors(R, rg, l, EARLY_ROWS)
 
 
 def pack_late(R, rg, l):
     b = BASE + LROW * l
     for j in range(3):
-        rg[pl.ds(b + 2 + j, D, stride=3), :] = R.a_qkv[l, 0:D, 128 * j:128 * (j + 1)]
+        rg[pl.ds(b + 2 + j, D, stride=3), :] = R.a_qkv[l, 128 * j:128 * (j + 1), :].T[0:D]
     pack_vectors(R, rg, l, (G1, B1, QB, VB))
 
 
@@ -687,9 +708,8 @@
 
 
 def pack_head(R, rg):
-    rows = nt(jnp.ones((8, 128), F32), R.a_fin[...].reshape(256, 128), HIGH)
     for i in range(2):
-        rg[pl.ds(HEAD + i, 1), :] = rows[0:1, 128 * i:128 * (i + 1)]
+        rg[pl.ds(HEAD + i, 1), :] = lane_sums(R.a_fin[i])
     lanes8 = iota((8, 128), 1)
     grad = R.a_head[...]
     R.hc[...] = jnp.where(iota((128, 128), 1) < 32, grad, 0.0)
@@ -713,7 +733,7 @@
     acc = put(code_phases(), R.hc, 8, 15, 32, 4)
     for a in range(4):
         rg[pl.ds(c0 + a, 8, stride=4), :] = acc[a]
-    hb = nt(jnp.ones((8, 128), F32), R.a_hb[...], HIGH)[0:1]
+    hb = lane_sums(R.a_hb[...])
     lane1 = iota((1, 128), 1)
     rg[pl.ds(o0, 48), :] = jnp.zeros((48, 128), F32)
     acc = put(off_phases(), R.ho, 5, 24, OFFS, 7)
@@ -892,8 +912,6 @@
         src = obs.at[pl.ds(pl.multiple_of(feat * n + CT * c, 16), CT), :]
         own.append(pltpu.make_async_copy(src, R.ob.at[c, feat, pl.ds(0, CT), :], R.s_own.at[c]))
         own[-1].start()
-    start_obs(0)
-    start_obs(1)
     for cp in ins:
         cp.wait()
     zero_grads(R)
@@ -932,7 +950,8 @@
     R.tz[0, feat] = two_rows(live_n, valid_n)
     start_all(z_copies(0))
     wait_all(p1)
-    start_obs(2)
+    start_obs(0)
+    start_obs(1)
     p2 = []
     for i in range(1, C):
         blk = R.pg.at[core, chip]
@@ -948,7 +967,6 @@
         blk = R.pg.at[core, c_from(i)]
         p3.append(send(blk, blk, R.s_p3, (i,), sibling))
         p3[-1].start()
-    start_obs(3)
     wait_all(c_copies(0))
     R.ts[0, core] = total(R.tc, 0, C)
     start_all(s_copies(0))
@@ -1029,9 +1047,10 @@
             for cp in obs_copies(p):
                 cp.wait_recv()
 
-        @pl.when(2 * c + 4 < 2 * P.chunks)
+        @pl.when(c + 1 < P.chunks)
         def _():
-            start_obs(2 * c + 4)
+            start_obs(2 * c + 2)
+            start_obs(2 * c + 3)
 
         R.x[...] = embed(R, [R.ob[c, f, 0:CT, :] for f in range(Fn)], c)
 
@@ -1040,10 +1059,6 @@
             return 0
 
         lax.fori_loop(0, LAYERS, lay, 0)
-
-        @pl.when(2 * c + 5 < 2 * P.chunks)
-        def _():
-            start_obs(2 * c + 5)
 
         dx = head_step(R, c, R.x[...], live_total, valid_total)
         dmid, da, rest = mlp_bwd(R, 1, dx)

time: 92.4 us -> 84.6 us (0.916)
  Pallas kernels: 88.6 us -> 80.9 us
    pallas_call x1, Pallas kernels: 88.6 us -> 80.9 us  [shards(): pl.pallas_call(functools.partial(step_kernel, P_, list(scratch)), out_sha...]
where the time goes in v4:
time: 84.6 us; the launch traced here: 84.4 us
  Pallas kernels  80.9 us (96%)
  other arithmetic  1.49 us (2%)
  local copies, waits for them, and re-layouts  1.32 us (2%)
    pallas_call x1, Pallas kernels, shards(): pl.pallas_call(functools.partial(step_kernel, P_, list(scratch)), out_sha...  80.9 us

profile of v4, /device:TPU:0, one launch (start us, length us, event | category | flops | bytes accessed | tf_op | source)
XLA Modules:
  0.0 84.4 jit_solution(14652273873831046921)
XLA Ops:
  0.6 0.0 copy-start
  0.6 0.0 copy-start.1
  0.7 0.0 copy-start.2
  0.7 80.9 %shard_map.111 = (f32[104,128]{1,0:T(8,128)}, f32[8,128]{1,0:T(8,128)}) custom-call(f32[13192]{0:T(1024)} %master.1, bf16[7680,128]{1,0:T(8,128)(2,1)} %obs.1, s32[10,256]{1,0:T(8,128)} %bitcast.5, s32[2,7680]{1,0:T(2,128)} %bitcast.3, f32[35,7680]{1,0:T(8,128)} %actions.1, s32[35,7680]{1,0:T(8,128)} %valid.1), custom_call_target="tpu_custom_call" | custom-call | tf_op jit(solution)/shard_map/pallas_call | solution.py:1137
  81.6 1.3 %slice_reduce_fusion = f32[4]{0:T(128)} fusion(f32[8,128]{1,0:T(8,128)} %get-tuple-element.7), kind=kLoop, calls=%fused_computation.4 | loop fusion | bytes 32 | tf_op jit(solution)/shard_map/slice | solution.py:1152
  82.9 0.0 copy-done
  82.9 0.0 copy-done.1
  82.9 0.0 copy-done.2
  82.9 1.5 %multiply_subtract_fusion = (f32[13192]{0:T(1024)}, f32[13192]{0:T(1024)}, f32[13192]{0:T(1024)}) fusion(f32[13192]{0:T(1024)S(1)} %copy-done, f32[13312]{0:T(1024)} %bitcast.4, f32[13192]{0:T(1024)S(1)} %copy-done.1, f32[13192]{0:T(1024)S(1)} %copy-done.2), kind=kLoop, calls=%fused_computation.2 | loop fusion | flops 197880 | bytes 369376 | tf_op jit(solution)/shard_map/sub | solution.py:1151
Async XLA Ops:
  0.6 82.3 %copy-start = (f32[13192]{0:T(1024)S(1)}, f32[13192]{0:T(1024)}, u32[]{:S(2)}) copy-start(f32[13192]{0:T(1024)} %master.1) | copy-start | bytes 158308
  0.6 82.2 %copy-start.1 = (f32[13192]{0:T(1024)S(1)}, f32[13192]{0:T(1024)}, u32[]{:S(2)}) copy-start(f32[13192]{0:T(1024)} %param.9) | copy-start | bytes 158308
  0.7 82.2 %copy-start.2 = (f32[13192]{0:T(1024)S(1)}, f32[13192]{0:T(1024)}, u32[]{:S(2)}) copy-start(f32[13192]{0:T(1024)} %param.10) | copy-start | bytes 158308

commit v5 on v4

--- a/solution.py
+++ b/solution.py
@@ -397,7 +397,6 @@
         r = 1.0 / jnp.sum(e, axis=0, keepdims=True)
         e8 = pad8(e)
         eh = low(e8)
-        el = low(e8 - eh.astype(F32))
         cols = slice(256 * p, 256 * (p + 1))
         R.prob[s, g, :, cols] = e
         for i in range(2):
@@ -405,16 +404,16 @@
             R.prob_low[s, g, :, at_h] = eh[:, 128 * i:128 * (i + 1)].T
         R.rsum[s, 2 * p, :, at] = r[:, 0:128]
         R.rsum[s, 2 * p + 1, :, at] = r[:, 128:256]
-        return r, eh, el
-
-    def values(g, p, r, eh, el):
+        return r, eh
+
+    def values(g, p, r, eh):
         at = slice(128 * g, 128 * (g + 1))
         out = []
         for i in range(2):
             sl = slice(slab_at(2 * p + i), slab_at(2 * p + i) + 24)
             cols = slice(128 * i, 128 * (i + 1))
             vs = low(jnp.concatenate([vh[sl, at], vl[sl, at]], axis=0))
-            o = nn(jnp.concatenate([vs, vs], axis=1), jnp.concatenate([eh[:, cols], el[:, cols]], axis=0))
+            o = nn(vs, eh[:, cols])
             out.append((o[0:24] + o[24:48]) * r[:, cols])
         return out
 
@@ -794,7 +793,7 @@
         s_ob=dma((2, 2 * P.chunks, Fn)),
         s_own=dma((P.chunks,)),
         s_in=dma((3,)),
-        s_r1=dma((2, 2, C)), s_r2=dma((2, Fn, C)), s_r3=dma((2, Fn)),
+        s_r1=dma((3, 2, C)), s_r2=dma((2, Fn, C)), s_r3=dma((2, Fn)),
     )
 
 
@@ -999,7 +998,7 @@
         return (P.shard * (f * P.toks + 2 * ch + co)) // D
 
     early = P.early[0] if P.early else Fn
-    planes = [slice(early, Fn), slice(0, early)]
+    planes = [slice(Fn - 1, Fn), slice(early, Fn - 1), slice(0, early)]
 
     def r1_copy(w, i):
         at = pl.ds(planes[w].start, planes[w].stop - planes[w].start)
@@ -1022,7 +1021,7 @@
     def sum_chips(w):
         for i in order:
             r1_copy(w, i).wait_recv()
-            for f in reversed(range(planes[w].start, planes[w].stop)):
+            for f in range(planes[w].start, planes[w].stop):
                 v = R.rg[pl.ds(rows_of(f, c_peer(i), core), B), :] + R.rb1[i, f]
                 if i:
                     R.sb2[i, f] = low(v)
@@ -1063,6 +1062,16 @@
         dx = head_step(R, c, R.x[...], live_total, valid_total)
         dmid, da, rest = mlp_bwd(R, 1, dx)
         R.x[...] = att_bwd(R, 1, 1, dmid, da, rest)
+        @pl.when(c == P.chunks - 1)
+        def _():
+            R.rg[pl.ds(HEAD + 32, P.grid - HEAD - 32), :] = jnp.zeros((P.grid - HEAD - 32, 128), F32)
+            pack_head(R, R.rg)
+            pack_late(R, R.rg, 1)
+            pack_early(R, R.rg, 1)
+            R.ts[1, core] = two_rows(jnp.sum(R.loss[0], keepdims=True), jnp.sum(R.loss[1], keepdims=True))
+            sum_cores(0)
+            start_all(s_copies(1))
+
         dmid, da, rest = mlp_bwd(R, 0, R.x[...])
         R.dmid[...] = dmid
         R.da[...] = da
@@ -1071,36 +1080,32 @@
 
         @pl.when(c == P.chunks - 1)
         def _():
-            R.rg[pl.ds(HEAD + 32, P.grid - HEAD - 32), :] = jnp.zeros((P.grid - HEAD - 32, 128), F32)
-            pack_head(R, R.rg)
-            pack_late(R, R.rg, 1)
-            for l in range(LAYERS):
-                pack_early(R, R.rg, l)
-            R.ts[1, core] = two_rows(jnp.sum(R.loss[0], keepdims=True), jnp.sum(R.loss[1], keepdims=True))
-            start_all(s_copies(1))
-            sum_cores(0)
-
-        dx = att_bwd(R, 0, 0, R.dmid[...], R.da[...], [])
-
-        @pl.when(c == P.chunks - 1)
-        def _():
+            pack_early(R, R.rg, 0)
+            sum_cores(1)
             sum_chips(0)
             wait_all(s_copies(1))
             R.tc[1, chip] = total(R.ts, 1, 2)
             start_all(c_copies(1))
 
+        dx = att_bwd(R, 0, 0, R.dmid[...], R.da[...], [])
+
+        @pl.when(c == P.chunks - 1)
+        def _():
+            sum_chips(1)
+
         embed_bwd(R, [R.ob[c, f] for f in range(Fn)], c, dx)
         return 0
 
     lax.fori_loop(0, P.chunks, chunk, 0)
     pack_embed(R, R.rg)
     pack_late(R, R.rg, 0)
-    sum_cores(1)
-    sum_chips(1)
+    sum_cores(2)
     wait_all(c_copies(1))
     R.tz[1, feat] = total(R.tc, 1, C)
     start_all(z_copies(1))
-    for f in reversed(range(Fn)):
+    sum_column(Fn - 1)
+    sum_chips(2)
+    for f in (*range(early, Fn - 1), *range(early)):
         sum_column(f)
     for i in range(1, Fn):
         r3_copy(i).wait_recv()
@@ -1115,7 +1120,7 @@
     for p in range(2 * P.chunks):
         for cp in obs_copies(p):
             cp.wait_send()
-    for w in range(2):
+    for w in range(3):
         for i in range(C):
             r1_copy(w, i).wait_send()
     for i in range(1, C):

time: 84.6 us -> 84.5 us (level)
  no operation moved by 1% of the time
where the time goes in v5:
time: 84.5 us; the launch traced here: 84.3 us
  Pallas kernels  80.8 us (96%)
  other arithmetic  1.49 us (2%)
  local copies, waits for them, and re-layouts  1.32 us (2%)
    pallas_call x1, Pallas kernels, shards(): pl.pallas_call(functools.partial(step_kernel, P_, list(scratch)), out_sha...  80.8 us

profile of v5, /device:TPU:0, one launch (start us, length us, event | category | flops | bytes accessed | tf_op | source)
XLA Modules:
  0.0 84.3 jit_solution(12923889424610058286)
XLA Ops:
  0.6 0.0 copy-start
  0.6 0.0 copy-start.1
  0.7 0.0 copy-start.2
  0.7 80.8 %shard_map.111 = (f32[104,128]{1,0:T(8,128)}, f32[8,128]{1,0:T(8,128)}) custom-call(f32[13192]{0:T(1024)} %master.1, bf16[7680,128]{1,0:T(8,128)(2,1)} %obs.1, s32[10,256]{1,0:T(8,128)} %bitcast.5, s32[2,7680]{1,0:T(2,128)} %bitcast.3, f32[35,7680]{1,0:T(8,128)} %actions.1, s32[35,7680]{1,0:T(8,128)} %valid.1), custom_call_target="tpu_custom_call" | custom-call | tf_op jit(solution)/shard_map/pallas_call | solution.py:1142
  81.5 1.3 %slice_reduce_fusion = f32[4]{0:T(128)} fusion(f32[8,128]{1,0:T(8,128)} %get-tuple-element.7), kind=kLoop, calls=%fused_computation.4 | loop fusion | bytes 32 | tf_op jit(solution)/shard_map/slice | solution.py:1157
  82.8 0.0 copy-done
  82.8 0.0 copy-done.1
  82.8 0.0 copy-done.2
  82.8 1.5 %multiply_subtract_fusion = (f32[13192]{0:T(1024)}, f32[13192]{0:T(1024)}, f32[13192]{0:T(1024)}) fusion(f32[13192]{0:T(1024)S(1)} %copy-done, f32[13312]{0:T(1024)} %bitcast.4, f32[13192]{0:T(1024)S(1)} %copy-done.1, f32[13192]{0:T(1024)S(1)} %copy-done.2), kind=kLoop, calls=%fused_computation.2 | loop fusion | flops 197880 | bytes 369376 | tf_op jit(solution)/shard_map/sub | solution.py:1156
Async XLA Ops:
  0.6 82.2 %copy-start = (f32[13192]{0:T(1024)S(1)}, f32[13192]{0:T(1024)}, u32[]{:S(2)}) copy-start(f32[13192]{0:T(1024)} %master.1) | copy-start | bytes 158308
  0.6 82.2 %copy-start.1 = (f32[13192]{0:T(1024)S(1)}, f32[13192]{0:T(1024)}, u32[]{:S(2)}) copy-start(f32[13192]{0:T(1024)} %param.9) | copy-start | bytes 158308
  0.7 82.2 %copy-start.2 = (f32[13192]{0:T(1024)S(1)}, f32[13192]{0:T(1024)}, u32[]{:S(2)}) copy-start(f32[13192]{0:T(1024)} %param.10) | copy-start | bytes 158308

commit v6 on v5

--- a/solution.py
+++ b/solution.py
@@ -397,6 +397,7 @@
         r = 1.0 / jnp.sum(e, axis=0, keepdims=True)
         e8 = pad8(e)
         eh = low(e8)
+        el = low(e8 - eh.astype(F32))
         cols = slice(256 * p, 256 * (p + 1))
         R.prob[s, g, :, cols] = e
         for i in range(2):
@@ -404,16 +405,16 @@
             R.prob_low[s, g, :, at_h] = eh[:, 128 * i:128 * (i + 1)].T
         R.rsum[s, 2 * p, :, at] = r[:, 0:128]
         R.rsum[s, 2 * p + 1, :, at] = r[:, 128:256]
-        return r, eh
-
-    def values(g, p, r, eh):
+        return r, eh, el
+
+    def values(g, p, r, eh, el):
         at = slice(128 * g, 128 * (g + 1))
         out = []
         for i in range(2):
             sl = slice(slab_at(2 * p + i), slab_at(2 * p + i) + 24)
             cols = slice(128 * i, 128 * (i + 1))
             vs = low(jnp.concatenate([vh[sl, at], vl[sl, at]], axis=0))
-            o = nn(vs, eh[:, cols])
+            o = nn(jnp.concatenate([vs, vs], axis=1), jnp.concatenate([eh[:, cols], el[:, cols]], axis=0))
             out.append((o[0:24] + o[24:48]) * r[:, cols])
         return out
 
@@ -1130,6 +1131,24 @@
         r3_copy(i).wait_send()
 
 
+def adam_kernel(shard, grad, sums, master, first, second, new_master, new_first, new_second, parts):
+    whole = shard // 1024
+    for lo, hi in ((0, whole), (whole, whole + 1)):
+        n = min(1024 * hi, shard) - 1024 * lo
+        at = pl.ds(1024 * lo, n)
+        g = grad[8 * lo:8 * hi].reshape(1024 * (hi - lo))[0:n]
+        old = master[at]
+        f_new = BETA_ONE * first[at] + (1.0 - BETA_ONE) * g
+        s_new = BETA_TWO * second[at] + (1.0 - BETA_TWO) * g * g
+        f_hat = f_new / (1.0 - BETA_ONE ** STEP_NO)
+        s_hat = s_new / (1.0 - BETA_TWO ** STEP_NO)
+        new_first[at] = f_new
+        new_second[at] = s_new
+        new_master[at] = old - LEARN_RATE * (f_hat / (jnp.sqrt(s_hat) + ADAM_EPS) + DECAY_RATE * old)
+    for i in range(4):
+        parts[i] = sums[i, 0]
+
+
 def solution(mesh):
     feats, toks = mesh.shape["feat"], mesh.shape["tok"]
 
@@ -1148,13 +1167,13 @@
             compiler_params=pltpu.CompilerParams(
                 collective_id=0, has_side_effects=True, vmem_limit_bytes=60 * 2 ** 20),
         )(master, obs, counts.T, codes.T, actions, valid)
-        grad = grad.reshape(-1)[:P_.shard]
-        f_new = BETA_ONE * first + (1.0 - BETA_ONE) * grad
-        s_new = BETA_TWO * second + (1.0 - BETA_TWO) * grad * grad
-        f_hat = f_new / (1.0 - BETA_ONE ** STEP_NO)
-        s_hat = s_new / (1.0 - BETA_TWO ** STEP_NO)
-        new = master - LEARN_RATE * (f_hat / (jnp.sqrt(s_hat) + ADAM_EPS) + DECAY_RATE * master)
-        return new, f_new, s_new, sums[0:4, 0]
+        flat = jax.ShapeDtypeStruct((P_.shard,), F32)
+        return pl.pallas_call(
+            functools.partial(adam_kernel, P_.shard),
+            out_shape=(flat, flat, flat, jax.ShapeDtypeStruct((4,), F32)),
+            in_specs=[vmem] * 5,
+            out_specs=(vmem, vmem, vmem, pl.BlockSpec(memory_space=pltpu.SMEM)),
+        )(grad, sums, master, first, second)
 
     weights = PSpec(("feat", "tok"))
     return jax.shard_map(

time: 84.5 us -> 81.9 us (0.969)
  other arithmetic: 1.49 us -> 0 us
  local copies, waits for them, and re-layouts: 1.32 us -> 0 us
    pallas_call x0 -> x1, Pallas kernels: none -> 1.61 us  [shards(): pl.pallas_call(functools.partial(adam_kernel, P_.shard), out_shape=(flat,...]
    sub x1 -> x0, other arithmetic: 1.49 us -> none  [shards(): master - LEARN_RATE * (f_hat / (jnp.sqrt(s_hat) + ADAM_EPS) + DECAY_RATE...]
    pallas_call x1, Pallas kernels: 80.8 us -> 79.4 us  [shards(): pl.pallas_call(functools.partial(step_kernel, P_, list(scratch)), out_sha...]
    slice x1 -> x0, local copies, waits for them, and re-layouts: 1.31 us -> none  [shards(): return (new, f_new, s_new, sums[0:4, 0])]
where the time goes in v6:
time: 81.9 us; the launch traced here: 81.7 us
  Pallas kernels  81 us (99%)
    pallas_call x1, Pallas kernels, shards(): pl.pallas_call(functools.partial(step_kernel, P_, list(scratch)), out_sha...  79.4 us

profile of v6, /device:TPU:0, one launch (start us, length us, event | category | flops | bytes accessed | tf_op | source)
XLA Modules:
  0.0 81.7 jit_solution(276680688283165387)
XLA Ops:
  0.6 79.4 %shard_map.111 = (f32[104,128]{1,0:T(8,128)}, f32[8,128]{1,0:T(8,128)}) custom-call(f32[13192]{0:T(1024)} %master.3, bf16[7680,128]{1,0:T(8,128)(2,1)} %obs.1, s32[10,256]{1,0:T(8,128)} %bitcast.3, s32[2,7680]{1,0:T(2,128)} %bitcast.2, f32[35,7680]{1,0:T(8,128)} %actions.1, s32[35,7680]{1,0:T(8,128)} %valid.1), custom_call_target="tpu_custom_call" | custom-call | tf_op jit(solution)/shard_map/pallas_call | solution.py:1161
  80.1 1.6 %shard_map.112 = (f32[13192]{0:T(1024)}, f32[13192]{0:T(1024)}, f32[13192]{0:T(1024)}, f32[4]{0:T(128)}) custom-call(f32[104,128]{1,0:T(8,128)} %get-tuple-element.6.grad, f32[8,128]{1,0:T(8,128)} %get-tuple-element.7.sums, f32[13192]{0:T(1024)} %master.3, f32[13192]{0:T(1024)} %first.1, f32[13192]{0:T(1024)} %second.1), custom_call_target="tpu_custom_call" | custom-call | tf_op jit(solution)/shard_map/pallas_call | solution.py:1171

commit v7 on v6

--- a/solution.py
+++ b/solution.py
@@ -866,16 +866,16 @@
             src_ref=src, dst_ref=dst, send_sem=sems.at[(0,) + at], recv_sem=sems.at[(1,) + at],
             device_id=dev, device_id_type=MESH)
 
+    barrier = pltpu.get_barrier_semaphore()
+    peers = [to_z(i) for i in range(1, Fn)] + [to_c(i) for i in range(1, C)] + [sibling]
+    for dev in peers:
+        pl.semaphore_signal(barrier, inc=1, device_id=dev, device_id_type=MESH)
+
     n = P.own_rows
     ins = []
     for i, (src, dst) in enumerate(((codes, R.codes_in), (actions, R.act_in), (valid, R.val_in))):
         ins.append(pltpu.make_async_copy(src.at[:, pl.ds(pl.multiple_of(feat * n, 128), n)], dst, R.s_in.at[i]))
         ins[-1].start()
-
-    barrier = pltpu.get_barrier_semaphore()
-    peers = [to_z(i) for i in range(1, Fn)] + [to_c(i) for i in range(1, C)] + [sibling]
-    for dev in peers:
-        pl.semaphore_signal(barrier, inc=1, device_id=dev, device_id_type=MESH)
 
     R.loc[...] = jnp.zeros(R.loc.shape, F32)
     whole = P.shard // 1024
@@ -1047,10 +1047,9 @@
             for cp in obs_copies(p):
                 cp.wait_recv()
 
-        @pl.when(c + 1 < P.chunks)
-        def _():
-            start_obs(2 * c + 2)
-            start_obs(2 * c + 3)
+            @pl.when(c + 1 < P.chunks)
+            def _():
+                start_obs(p + 2)
 
         R.x[...] = embed(R, [R.ob[c, f, 0:CT, :] for f in range(Fn)], c)
 
@@ -1092,6 +1091,7 @@
 
         @pl.when(c == P.chunks - 1)
         def _():
+            pack_late(R, R.rg, 0)
             sum_chips(1)
 
         embed_bwd(R, [R.ob[c, f] for f in range(Fn)], c, dx)
@@ -1099,7 +1099,6 @@
 
     lax.fori_loop(0, P.chunks, chunk, 0)
     pack_embed(R, R.rg)
-    pack_late(R, R.rg, 0)
     sum_cores(2)
     wait_all(c_copies(1))
     R.tz[1, feat] = total(R.tc, 1, C)

time: 81.9 us -> 82 us (level)
  no operation moved by 1% of the time
where the time goes in v7:
time: 82 us; the launch traced here: 81.8 us
  Pallas kernels  81.1 us (99%)
    pallas_call x1, Pallas kernels, shards(): pl.pallas_call(functools.partial(step_kernel, P_, list(scratch)), out_sha...  79.5 us

profile of v7, /device:TPU:0, one launch (start us, length us, event | category | flops | bytes accessed | tf_op | source)
XLA Modules:
  0.0 81.8 jit_solution(8671139028685829495)
XLA Ops:
  0.6 79.5 %shard_map.111 = (f32[104,128]{1,0:T(8,128)}, f32[8,128]{1,0:T(8,128)}) custom-call(f32[13192]{0:T(1024)} %master.3, bf16[7680,128]{1,0:T(8,128)(2,1)} %obs.1, s32[10,256]{1,0:T(8,128)} %bitcast.3, s32[2,7680]{1,0:T(2,128)} %bitcast.2, f32[35,7680]{1,0:T(8,128)} %actions.1, s32[35,7680]{1,0:T(8,128)} %valid.1), custom_call_target="tpu_custom_call" | custom-call | tf_op jit(solution)/shard_map/pallas_call | solution.py:1160
  80.2 1.6 %shard_map.112 = (f32[13192]{0:T(1024)}, f32[13192]{0:T(1024)}, f32[13192]{0:T(1024)}, f32[4]{0:T(128)}) custom-call(f32[104,128]{1,0:T(8,128)} %get-tuple-element.6.grad, f32[8,128]{1,0:T(8,128)} %get-tuple-element.7.sums, f32[13192]{0:T(1024)} %master.3, f32[13192]{0:T(1024)} %first.1, f32[13192]{0:T(1024)} %second.1), custom_call_target="tpu_custom_call" | custom-call | tf_op jit(solution)/shard_map/pallas_call | solution.py:1170

commit v8 on v7

--- a/solution.py
+++ b/solution.py
@@ -426,7 +426,7 @@
 
 PAIR = True
 FAHEAD = 2
-BAHEAD = 2
+BAHEAD = 6
 
 
 def pipeline(items, first, second, third, ahead, between=()):

time: 82 us -> 81.2 us (level)
  no operation moved by 1% of the time
where the time goes in v8:
time: 81.2 us; the launch traced here: 81 us
  Pallas kernels  80.4 us (99%)
    pallas_call x1, Pallas kernels, shards(): pl.pallas_call(functools.partial(step_kernel, P_, list(scratch)), out_sha...  78.8 us

profile of v8, /device:TPU:0, one launch (start us, length us, event | category | flops | bytes accessed | tf_op | source)
XLA Modules:
  0.0 81.0 jit_solution(9097229831557432411)
XLA Ops:
  0.6 78.8 %shard_map.111 = (f32[104,128]{1,0:T(8,128)}, f32[8,128]{1,0:T(8,128)}) custom-call(f32[13192]{0:T(1024)} %master.3, bf16[7680,128]{1,0:T(8,128)(2,1)} %obs.1, s32[10,256]{1,0:T(8,128)} %bitcast.3, s32[2,7680]{1,0:T(2,128)} %bitcast.2, f32[35,7680]{1,0:T(8,128)} %actions.1, s32[35,7680]{1,0:T(8,128)} %valid.1), custom_call_target="tpu_custom_call" | custom-call | tf_op jit(solution)/shard_map/pallas_call | solution.py:1160
  79.4 1.6 %shard_map.112 = (f32[13192]{0:T(1024)}, f32[13192]{0:T(1024)}, f32[13192]{0:T(1024)}, f32[4]{0:T(128)}) custom-call(f32[104,128]{1,0:T(8,128)} %get-tuple-element.6.grad, f32[8,128]{1,0:T(8,128)} %get-tuple-element.7.sums, f32[13192]{0:T(1024)} %master.3, f32[13192]{0:T(1024)} %first.1, f32[13192]{0:T(1024)} %second.1), custom_call_target="tpu_custom_call" | custom-call | tf_op jit(solution)/shard_map/pallas_call | solution.py:1170

commit v9 on v8

--- a/solution.py
+++ b/solution.py
@@ -397,7 +397,6 @@
         r = 1.0 / jnp.sum(e, axis=0, keepdims=True)
         e8 = pad8(e)
         eh = low(e8)
-        el = low(e8 - eh.astype(F32))
         cols = slice(256 * p, 256 * (p + 1))
         R.prob[s, g, :, cols] = e
         for i in range(2):
@@ -405,16 +404,16 @@
             R.prob_low[s, g, :, at_h] = eh[:, 128 * i:128 * (i + 1)].T
         R.rsum[s, 2 * p, :, at] = r[:, 0:128]
         R.rsum[s, 2 * p + 1, :, at] = r[:, 128:256]
-        return r, eh, el
-
-    def values(g, p, r, eh, el):
+        return r, eh
+
+    def values(g, p, r, eh):
         at = slice(128 * g, 128 * (g + 1))
         out = []
         for i in range(2):
             sl = slice(slab_at(2 * p + i), slab_at(2 * p + i) + 24)
             cols = slice(128 * i, 128 * (i + 1))
             vs = low(jnp.concatenate([vh[sl, at], vl[sl, at]], axis=0))
-            o = nn(jnp.concatenate([vs, vs], axis=1), jnp.concatenate([eh[:, cols], el[:, cols]], axis=0))
+            o = nn(vs, eh[:, cols])
             out.append((o[0:24] + o[24:48]) * r[:, cols])
         return out
 

time: 81.2 us -> 80.8 us (level)
  no operation moved by 1% of the time
where the time goes in v9:
time: 80.8 us; the launch traced here: 80.6 us
  Pallas kernels  79.9 us (99%)
    pallas_call x1, Pallas kernels, shards(): pl.pallas_call(functools.partial(step_kernel, P_, list(scratch)), out_sha...  78.3 us

profile of v9, /device:TPU:0, one launch (start us, length us, event | category | flops | bytes accessed | tf_op | source)
XLA Modules:
  0.0 80.6 jit_solution(3497041390215600767)
XLA Ops:
  0.6 78.3 %shard_map.111 = (f32[104,128]{1,0:T(8,128)}, f32[8,128]{1,0:T(8,128)}) custom-call(f32[13192]{0:T(1024)} %master.3, bf16[7680,128]{1,0:T(8,128)(2,1)} %obs.1, s32[10,256]{1,0:T(8,128)} %bitcast.3, s32[2,7680]{1,0:T(2,128)} %bitcast.2, f32[35,7680]{1,0:T(8,128)} %actions.1, s32[35,7680]{1,0:T(8,128)} %valid.1), custom_call_target="tpu_custom_call" | custom-call | tf_op jit(solution)/shard_map/pallas_call | solution.py:1159
  79.0 1.6 %shard_map.112 = (f32[13192]{0:T(1024)}, f32[13192]{0:T(1024)}, f32[13192]{0:T(1024)}, f32[4]{0:T(128)}) custom-call(f32[104,128]{1,0:T(8,128)} %get-tuple-element.6.grad, f32[8,128]{1,0:T(8,128)} %get-tuple-element.7.sums, f32[13192]{0:T(1024)} %master.3, f32[13192]{0:T(1024)} %first.1, f32[13192]{0:T(1024)} %second.1), custom_call_target="tpu_custom_call" | custom-call | tf_op jit(solution)/shard_map/pallas_call | solution.py:1169

commit v10 on v9

--- a/solution.py
+++ b/solution.py
@@ -425,7 +425,7 @@
 
 PAIR = True
 FAHEAD = 2
-BAHEAD = 6
+BAHEAD = 4
 
 
 def pipeline(items, first, second, third, ahead, between=()):

time: 80.8 us -> 81 us (level)
  no operation moved by 1% of the time
where the time goes in v10:
time: 81 us; the launch traced here: 80.8 us
  Pallas kernels  80.2 us (99%)
    pallas_call x1, Pallas kernels, shards(): pl.pallas_call(functools.partial(step_kernel, P_, list(scratch)), out_sha...  78.6 us

profile of v10, /device:TPU:0, one launch (start us, length us, event | category | flops | bytes accessed | tf_op | source)
XLA Modules:
  0.0 80.8 jit_solution(13366120575424747601)
XLA Ops:
  0.6 78.6 %shard_map.111 = (f32[104,128]{1,0:T(8,128)}, f32[8,128]{1,0:T(8,128)}) custom-call(f32[13192]{0:T(1024)} %master.3, bf16[7680,128]{1,0:T(8,128)(2,1)} %obs.1, s32[10,256]{1,0:T(8,128)} %bitcast.3, s32[2,7680]{1,0:T(2,128)} %bitcast.2, f32[35,7680]{1,0:T(8,128)} %actions.1, s32[35,7680]{1,0:T(8,128)} %valid.1), custom_call_target="tpu_custom_call" | custom-call | tf_op jit(solution)/shard_map/pallas_call | solution.py:1159
  79.2 1.6 %shard_map.112 = (f32[13192]{0:T(1024)}, f32[13192]{0:T(1024)}, f32[13192]{0:T(1024)}, f32[4]{0:T(128)}) custom-call(f32[104,128]{1,0:T(8,128)} %get-tuple-element.6.grad, f32[8,128]{1,0:T(8,128)} %get-tuple-element.7.sums, f32[13192]{0:T(1024)} %master.3, f32[13192]{0:T(1024)} %first.1, f32[13192]{0:T(1024)} %second.1), custom_call_target="tpu_custom_call" | custom-call | tf_op jit(solution)/shard_map/pallas_call | solution.py:1169
